TPU v7x, 32 devices: a whole 2x2x4 slice. The times are simulated.
32 devices in a mesh: dp: 8 (over y, x, core), ctx: 4 (over z).
Axes of the slice: x: 2, y: 2, z: 4, core: 2. Of those that a mesh axis runs over, the one named last changes fastest.
Arguments:
- layer_input: bfloat16 [8192, 1024], P(('dp', 'ctx')), may hold values from -6 to 6
- out_cotangent: bfloat16 [8192, 1024], P(('dp', 'ctx')), may hold values from -6 to 6
- params: float32 [2, 4, 24576, 128], P(None, 'ctx', 'dp')
- vectors: float32 [2, 12288], P(None, ('dp', 'ctx')), may hold values from -1.2 to 1.6, as said below
- param_moment: float32 [2, 4, 24576, 128], P(None, 'ctx', 'dp'), may hold values from -6 to 6
- vector_moment: float32 [2, 12288], P(None, ('dp', 'ctx')), may hold values from -6 to 6
- param_square: float32 [2, 4, 24576, 128], P(None, 'ctx', 'dp'), may hold values from 1 to 100
- vector_square: float32 [2, 12288], P(None, ('dp', 'ctx')), may hold values from 1 to 100
Outputs:
- layer_output: bfloat16 [8192, 1024], P(('dp', 'ctx'))
- input_grad: float32 [8192, 1024], P(('dp', 'ctx'))
- param_grad: float32 [2, 4, 24576, 128], P(None, 'ctx', 'dp')
- vector_grad: float32 [2, 12288], P(None, ('dp', 'ctx'))
- param_moment_next: float32 [2, 4, 24576, 128], P(None, 'ctx', 'dp')
- vector_moment_next: float32 [2, 12288], P(None, ('dp', 'ctx'))
- param_square_next: float32 [2, 4, 24576, 128], P(None, 'ctx', 'dp')
- vector_square_next: float32 [2, 12288], P(None, ('dp', 'ctx'))
- param_update: float32 [2, 4, 24576, 128], P(None, 'ctx', 'dp')
- vector_update: float32 [2, 12288], P(None, ('dp', 'ctx'))
Inputs may be any that keep to these rules, and one draw needn't show every extreme that they name: Rows 0 and 5 of each block's vectors are norm gains between 0.4 and 1.6; the others are biases.
All inputs are finite; a program needn't handle non-finite values.
Results may differ from a plain program's by a relative error of at most 0.015.
Values may be sent and summed in bfloat16 or wider, within the bound.
A program may use at most 256 MiB of HBM per device.

v0:
```python
import jax
import jax.numpy as jnp
from jax import lax
from jax.sharding import PartitionSpec as P

D = 1024
HEADS = 16
HEAD = 64
FF = 4096
LAYERS = 2
STEP = 10


norm_eps = 1e-05
beta_one = 0.9
beta_two = 0.999
rate = 0.01
decay = 0.1
adam_eps = 1e-08


def weight_views(slabs):
    count = slabs.shape[0]
    flat = slabs.reshape(count, -1)
    first = 3 * D * D // count
    second = first + D * D // count
    third = second + D * FF // count
    return (
        flat[:, :first].reshape(count, D, 3 * D // count),
        flat[:, first:second].reshape(count, D, D // count),
        flat[:, second:third].reshape(count, D, FF // count),
        flat[:, third:].reshape(count, FF, D // count),
    )


def layer_norm(values, gain, shift):
    center = values - jnp.mean(values, axis=-1, keepdims=True)
    spread = jnp.mean(center * center, axis=-1, keepdims=True)
    return center * lax.rsqrt(spread + norm_eps) * gain + shift


def gelu_tanh(values):
    return (
        0.5
        * values
        * (1.0 + jnp.tanh(0.7978845608028654 * (values + 0.044715 * values * values * values)))
    )


def fetch(params, vectors, layer_id):
    piece = params[layer_id].astype(jnp.bfloat16)
    vec_piece = vectors[layer_id].astype(jnp.bfloat16)
    wide = (
        lax.all_gather(piece, "ctx", axis=0, tiled=True),
        lax.all_gather(vec_piece, "ctx", axis=0, tiled=True),
    )
    whole = (
        lax.all_gather(wide[0], "dp", axis=1, tiled=True),
        lax.all_gather(wide[1], "dp", axis=0, tiled=True),
    )
    vec_line = whole[1]
    attend_w, output_w, expand_w, reduce_w = weight_views(whole[0])
    return (attend_w, output_w, expand_w, reduce_w, vec_line.reshape(12, D))


def project(inputs, weight):
    count = weight.shape[0]
    product = jnp.einsum("td,ndc->tnc", inputs, weight, preferred_element_type=jnp.float32)
    return product.reshape(inputs.shape[0], count * weight.shape[2])


def project_back(grads, weight):
    count = weight.shape[0]
    split = grads.reshape(grads.shape[0], count, weight.shape[2])
    return jnp.einsum("tnc,ndc->td", split, weight, preferred_element_type=jnp.float32)


def masked_scores(queries, keys_all):
    raw = jnp.einsum("thd,shd->hts", queries, keys_all, preferred_element_type=jnp.float32)
    rows = queries.shape[0]
    qpos = lax.axis_index("ctx") * rows + lax.broadcasted_iota(
        jnp.int32, (rows, keys_all.shape[0]), 0
    )
    kpos = lax.broadcasted_iota(jnp.int32, (rows, keys_all.shape[0]), 1)
    return jnp.where((kpos <= qpos)[None], raw * 0.125, -1000000000.0)


def forward_layer(resid, weights):
    attend_w, output_w, expand_w, reduce_w, vector_low = weights
    vec = vector_low.astype(jnp.float32)
    rows = resid.shape[0]
    normed1 = layer_norm(resid, vec[0], vec[1]).astype(jnp.bfloat16)
    mixed = project(normed1, attend_w)
    queries = (mixed[:, :D] + vec[2]).astype(jnp.bfloat16)
    keys = mixed[:, D : 2 * D].astype(jnp.bfloat16)
    values = (mixed[:, 2 * D :] + vec[3]).astype(jnp.bfloat16)
    keys_all, values_all = (
        lax.all_gather(keys, "ctx", axis=0, tiled=True),
        lax.all_gather(values, "ctx", axis=0, tiled=True),
    )
    span = keys_all.shape[0]
    query_heads = queries.reshape(rows, HEADS, HEAD)
    key_heads = keys_all.reshape(span, HEADS, HEAD)
    value_heads = values_all.reshape(span, HEADS, HEAD)
    scores = masked_scores(query_heads, key_heads)
    top = jnp.max(scores, axis=-1, keepdims=True)
    expo = jnp.exp(scores - top)
    total = jnp.sum(expo, axis=-1, keepdims=True)
    log_total = top + jnp.log(total)
    probs = (expo / total).astype(jnp.bfloat16)
    attended = jnp.einsum("hts,shd->thd", probs, value_heads, preferred_element_type=jnp.float32)
    attended = attended.reshape(rows, D).astype(jnp.bfloat16)
    hidden = resid + project(attended, output_w) + vec[4]
    normed2 = layer_norm(hidden, vec[5], vec[6]).astype(jnp.bfloat16)
    upper = project(normed2, expand_w) + vec[7:11].reshape(FF)
    active = gelu_tanh(upper).astype(jnp.bfloat16)
    result = hidden + project(active, reduce_w) + vec[11]
    kept = (
        resid,
        normed1,
        query_heads,
        key_heads,
        value_heads,
        log_total,
        attended,
        hidden,
        normed2,
        upper,
        active,
    )
    return (result, kept)


def backward_layer(grad_out, weights, kept):
    attend_w, output_w, expand_w, reduce_w, vector_low = weights
    vec = vector_low.astype(jnp.float32)
    (
        resid,
        normed1,
        query_heads,
        key_heads,
        value_heads,
        log_total,
        attended,
        hidden,
        normed2,
        upper,
        active,
    ) = kept
    rows = resid.shape[0]
    span = key_heads.shape[0]
    bias_reduce = jnp.sum(grad_out, axis=0)
    out_low = grad_out.astype(jnp.bfloat16)
    grad_active = project_back(out_low, reduce_w)
    unused, gelu_pull = jax.vjp(gelu_tanh, upper)
    grad_upper = gelu_pull(grad_active)[0]
    bias_expand = jnp.sum(grad_upper, axis=0)
    upper_low = grad_upper.astype(jnp.bfloat16)
    grad_normed2 = project_back(upper_low, expand_w)
    unused, norm_pull2 = jax.vjp(layer_norm, hidden, vec[5], vec[6])
    grad_from_norm2, gain_two, shift_two = norm_pull2(grad_normed2)
    grad_hidden = grad_out + grad_from_norm2
    bias_output = jnp.sum(grad_hidden, axis=0)
    hidden_low = grad_hidden.astype(jnp.bfloat16)
    grad_attended = project_back(hidden_low, output_w)
    grad_heads = grad_attended.astype(jnp.bfloat16).reshape(rows, HEADS, HEAD)
    probs = jnp.exp(masked_scores(query_heads, key_heads) - log_total)
    probs_low = probs.astype(jnp.bfloat16)
    grad_values_all = jnp.einsum(
        "hts,thd->shd", probs_low, grad_heads, preferred_element_type=jnp.float32
    )
    grad_probs = jnp.einsum(
        "thd,shd->hts", grad_heads, value_heads, preferred_element_type=jnp.float32
    )
    inner = jnp.sum(probs * grad_probs, axis=-1, keepdims=True)
    grad_scores = (probs * (grad_probs - inner) * 0.125).astype(jnp.bfloat16)
    grad_queries = jnp.einsum(
        "hts,shd->thd", grad_scores, key_heads, preferred_element_type=jnp.float32
    )
    grad_keys_all = jnp.einsum(
        "hts,thd->shd", grad_scores, query_heads, preferred_element_type=jnp.float32
    )
    grad_keys, grad_values = (
        lax.psum_scatter(
            grad_keys_all.reshape(span, D).astype(jnp.bfloat16),
            "ctx",
            scatter_dimension=0,
            tiled=True,
        ).astype(jnp.float32),
        lax.psum_scatter(
            grad_values_all.reshape(span, D).astype(jnp.bfloat16),
            "ctx",
            scatter_dimension=0,
            tiled=True,
        ).astype(jnp.float32),
    )
    grad_queries = grad_queries.reshape(rows, D)
    bias_query = jnp.sum(grad_queries, axis=0)
    bias_value = jnp.sum(grad_values, axis=0)
    grad_mixed = jnp.concatenate([grad_queries, grad_keys, grad_values], axis=1).astype(
        jnp.bfloat16
    )
    grad_normed1 = project_back(grad_mixed, attend_w)
    unused, norm_pull1 = jax.vjp(layer_norm, resid, vec[0], vec[1])
    grad_from_norm1, gain_one, shift_one = norm_pull1(grad_normed1)
    grad_input = grad_hidden + grad_from_norm1
    vector_grads = jnp.concatenate(
        [
            gain_one[None],
            shift_one[None],
            bias_query[None],
            bias_value[None],
            bias_output[None],
            gain_two[None],
            shift_two[None],
            bias_expand.reshape(4, D),
            bias_reduce[None],
        ],
        axis=0,
    )
    seq_inputs = (
        lax.all_gather(active, "ctx", axis=0, tiled=True),
        lax.all_gather(normed2, "ctx", axis=0, tiled=True),
        lax.all_gather(attended, "ctx", axis=0, tiled=True),
        lax.all_gather(normed1, "ctx", axis=0, tiled=True),
    )
    seq_grads = (
        lax.all_to_all(out_low, "ctx", split_axis=1, concat_axis=0, tiled=True),
        lax.all_to_all(upper_low, "ctx", split_axis=1, concat_axis=0, tiled=True),
        lax.all_to_all(hidden_low, "ctx", split_axis=1, concat_axis=0, tiled=True),
        lax.all_to_all(grad_mixed, "ctx", split_axis=1, concat_axis=0, tiled=True),
    )
    grad_reduce = jnp.einsum(
        "tf,tc->fc", seq_inputs[0], seq_grads[0], preferred_element_type=jnp.float32
    )
    grad_expand = jnp.einsum(
        "td,tc->dc", seq_inputs[1], seq_grads[1], preferred_element_type=jnp.float32
    )
    grad_output = jnp.einsum(
        "td,tc->dc", seq_inputs[2], seq_grads[2], preferred_element_type=jnp.float32
    )
    grad_attend = jnp.einsum(
        "td,tc->dc", seq_inputs[3], seq_grads[3], preferred_element_type=jnp.float32
    )
    slab = jnp.concatenate(
        [
            grad_attend.reshape(-1),
            grad_output.reshape(-1),
            grad_expand.reshape(-1),
            grad_reduce.reshape(-1),
        ]
    ).reshape(-1, 128)
    owned = lax.psum_scatter(
        slab.astype(jnp.bfloat16), "dp", scatter_dimension=0, tiled=True
    ).astype(jnp.float32)
    vec_owned = lax.psum_scatter(
        vector_grads.reshape(-1), ("dp", "ctx"), scatter_dimension=0, tiled=True
    )
    return (grad_input, owned, vec_owned)


def adam_step(grad, moment, square, master, weight_decay):
    moment_next = beta_one * moment + (1.0 - beta_one) * grad
    square_next = beta_two * square + (1.0 - beta_two) * grad * grad
    corrected = moment_next / (1.0 - beta_one**STEP)
    scaled = square_next / (1.0 - beta_two**STEP)
    update = -rate * (corrected / (jnp.sqrt(scaled) + adam_eps) + weight_decay * master)
    return (moment_next, square_next, update)


def per_device(
    layer_input,
    out_cotangent,
    params,
    vectors,
    param_moment,
    vector_moment,
    param_square,
    vector_square,
):
    resid = layer_input.astype(jnp.float32)
    saved = []
    for layer_id in range(LAYERS):
        resid, kept = forward_layer(resid, fetch(params, vectors, layer_id))
        saved.append(kept)
    layer_output = resid.astype(jnp.bfloat16)
    grad_flow = out_cotangent.astype(jnp.float32)
    slab_grads = [None] * LAYERS
    vec_grads = [None] * LAYERS
    for layer_id in reversed(range(LAYERS)):
        grad_flow, owned, vec_owned = backward_layer(
            grad_flow, fetch(params, vectors, layer_id), saved[layer_id]
        )
        slab_grads[layer_id] = owned[None]
        vec_grads[layer_id] = vec_owned
    param_grad = jnp.stack(slab_grads)
    vector_grad = jnp.stack(vec_grads)
    param_step = adam_step(param_grad, param_moment, param_square, params, decay)
    vector_step = adam_step(vector_grad, vector_moment, vector_square, vectors, 0.0)
    return (
        layer_output,
        grad_flow,
        param_grad,
        vector_grad,
        param_step[0],
        vector_step[0],
        param_step[1],
        vector_step[1],
        param_step[2],
        vector_step[2],
    )


def solution(mesh):
    placed = (
        P(("dp", "ctx"), None),
        P(("dp", "ctx"), None),
        P(None, "ctx", "dp", None),
        P(None, ("dp", "ctx")),
        P(None, "ctx", "dp", None),
        P(None, ("dp", "ctx")),
        P(None, "ctx", "dp", None),
        P(None, ("dp", "ctx")),
    )
    return jax.shard_map(
        per_device,
        mesh=mesh,
        in_specs=placed,
        out_specs=(
            P(("dp", "ctx"), None),
            P(("dp", "ctx"), None),
            P(None, "ctx", "dp", None),
            P(None, ("dp", "ctx")),
            P(None, "ctx", "dp", None),
            P(None, ("dp", "ctx")),
            P(None, "ctx", "dp", None),
            P(None, ("dp", "ctx")),
            P(None, "ctx", "dp", None),
            P(None, ("dp", "ctx")),
        ),
        check_vma=False,
    )
```

profile of v0, /device:TPU:0, one launch (start us, length us, event | category | flops | bytes accessed | tf_op | source)
XLA Modules:
  0.0 1923.4 jit_solution(8467037937947035056)
XLA Ops:
  11.4 65.6 %all-gather.49.cloned.1.call-done = bf16[4,1,3072,128]{3,2,1,0:T(8,128)(2,1)} async-done(((bf16[1,1,3072,128]{3,2,1,0:T(8,128)(2,1)}), bf16[4,1,3072,128]{3,2,1,0:T(8,128)(2,1)}) %all-gather.49.cloned.1.call-update) | async-done | bytes 3145744 | tf_op jit(solution)/shard_map/all_gather | solution.py:54
  77.0 64.3 %all-gather.53.cloned.1.call-done = bf16[4,1,3072,128]{3,2,1,0:T(8,128)(2,1)} async-done(((bf16[1,1,3072,128]{3,2,1,0:T(8,128)(2,1)}), bf16[4,1,3072,128]{3,2,1,0:T(8,128)(2,1)}) %all-gather.53.cloned.1.call-update) | async-done | bytes 3145744 | tf_op jit(solution)/shard_map/all_gather | solution.py:54
  163.8 103.5 %all-gather.51.cloned.1.call-done = bf16[4,1,24576,128]{3,2,1,0:T(8,128)(2,1)} async-done(((bf16[4,1,3072,128]{3,2,1,0:T(8,128)(2,1)}), bf16[4,1,24576,128]{3,2,1,0:T(8,128)(2,1)}) %all-gather.51.cloned.1.call-update) | async-done | bytes 25165840 | tf_op jit(solution)/shard_map/all_gather | solution.py:58
  267.3 32.1 %copy.253 = bf16[1,4,24576,128]{3,1,2,0:T(4,128)(2,1)} copy(bf16[1,4,24576,128]{3,2,1,0:T(8,128)(2,1)} %bitcast.367) | data formatting | bytes 50331648
  416.3 32.1 %copy.252 = bf16[1,4,24576,128]{3,1,2,0:T(4,128)(2,1)} copy(bf16[1,4,24576,128]{3,2,1,0:T(8,128)(2,1)} %bitcast.366) | data formatting | bytes 50331648
  593.1 27.4 %all-gather.29.cloned.1.call-done = bf16[1024,1024]{1,0:T(8,128)(2,1)} async-done(((bf16[256,1024]{1,0:T(8,128)(2,1)}), bf16[1024,1024]{1,0:T(8,128)(2,1)}) %all-gather.29.cloned.1.call-update) | async-done | bytes 2097168 | tf_op jit(solution)/shard_map/all_gather | solution.py:99
  684.4 38.7 %fusion.80 = bf16[16,64,1024]{2,1,0:T(8,128)(2,1)} fusion(bf16[256,16,64]{0,2,1:T(8,128)(2,1)S(1)} %bitcast.417, f32[16,256,1024]{2,1,0:T(8,128)} %fusion.192, f32[16,256,1024]{2,1,0:T(8,128)} %copy-done.1, f32[16,256]{1,0:T(8,128)S(1)} %log_add_fusion.1), kind=kOutput, calls=%fused_computation.101 | convolution fusion | flops 567284736 | bytes 36192256 | tf_op jit(solution)/shard_map/hts,thd->shd/dot_general | solution.py:180
  723.2 30.4 %fusion.177 = (f32[16,64]{1,0:T(8,128)S(1)}, bf16[256,16,64]{0,2,1:T(8,128)(2,1)S(1)}) fusion(bf16[1024,16,64]{0,2,1:T(8,128)(2,1)} %bitcast.399, f32[16,256,1024]{2,1,0:T(8,128)} %fusion.192, f32[16,256,1024]{2,1,0:T(8,128)} %copy-done.1, f32[16,256]{1,0:T(8,128)S(1)} %log_add_fusion.1), kind=kOutput, calls=%fused_computation.239 | convolution fusion | flops 566759424 | bytes 36196352 | tf_op jit(solution)/shard_map/hts,shd->thd/dot_general | solution.py:177
  814.0 39.4 %fusion.77 = bf16[16,64,1024]{2,1,0:T(8,128)(2,1)} fusion(bf16[256,16,64]{0,2,1:T(8,128)(2,1)S(1)} %bitcast.410, f32[16,256,1024]{2,1,0:T(8,128)} %fusion.193, f32[16,256,1024]{2,1,0:T(8,128)} %copy-done, f32[16,256]{1,0:T(8,128)S(1)} %log_add_fusion), kind=kOutput, calls=%fused_computation.100 | convolution fusion | flops 567284736 | bytes 36192256 | tf_op jit(solution)/shard_map/hts,thd->shd/dot_general | solution.py:180
  862.8 28.2 %all-to-all-done.7 = bf16[256,4,256]{0,2,1:T(8,128)(2,1)S(1)} async-done(((bf16[256,4,256]{0,2,1:T(8,128)(2,1)}), bf16[256,4,256]{0,2,1:T(8,128)(2,1)S(1)}, u32[]{:S(2)}, u32[]{:S(2)}) %all-to-all-start.7) | async-done | bytes 524320 | tf_op jit(solution)/shard_map/all_to_all | solution.py:228
  925.9 27.1 %all-to-all-done.1 = bf16[256,4,256]{2,0,1:T(8,128)(2,1)S(1)} async-done(((bf16[256,4,256]{2,0,1:T(8,128)(2,1)}), bf16[256,4,256]{2,0,1:T(8,128)(2,1)S(1)}, u32[]{:S(2)}, u32[]{:S(2)}) %all-to-all-start.1) | async-done | bytes 524320 | tf_op jit(solution)/shard_map/all_to_all | solution.py:230
  957.4 37.3 %fusion.176 = (f32[16,64]{1,0:T(8,128)S(1)}, bf16[256,16,64]{0,2,1:T(8,128)(2,1)S(1)}) fusion(bf16[1024,16,64]{0,2,1:T(8,128)(2,1)S(1)} %bitcast.396, f32[16,256,1024]{2,1,0:T(8,128)} %fusion.193, f32[16,256,1024]{2,1,0:T(8,128)} %copy-done, f32[16,256]{1,0:T(8,128)S(1)} %log_add_fusion), kind=kOutput, calls=%fused_computation.238 | convolution fusion | flops 566759424 | bytes 36196352 | tf_op jit(solution)/shard_map/hts,shd->thd/dot_general | solution.py:177
  1027.5 58.5 %all-gather.37.cloned.1.call-done = bf16[1024,1024]{1,0:T(8,128)(2,1)} async-done(((bf16[256,1024]{1,0:T(8,128)(2,1)}), bf16[1024,1024]{1,0:T(8,128)(2,1)}) %all-gather.37.cloned.1.call-update) | async-done | bytes 2097168 | tf_op jit(solution)/shard_map/all_gather | solution.py:223
  1103.5 144.0 %all-gather.39.cloned.1.call-done = bf16[1024,4096]{1,0:T(8,128)(2,1)} async-done(((bf16[256,4096]{1,0:T(8,128)(2,1)}), bf16[1024,4096]{1,0:T(8,128)(2,1)}) %all-gather.39.cloned.1.call-update) | async-done | bytes 8388624 | tf_op jit(solution)/shard_map/all_gather | solution.py:222
  1258.6 34.4 %all-gather.33.cloned.1.call-done = bf16[1024,1024]{1,0:T(8,128)(2,1)} async-done(((bf16[256,1024]{1,0:T(8,128)(2,1)}), bf16[1024,1024]{1,0:T(8,128)(2,1)}) %all-gather.33.cloned.1.call-update) | async-done | bytes 2097168 | tf_op jit(solution)/shard_map/all_gather | solution.py:225
  1306.3 29.7 %maximum_bitcast_fusion = bf16[24576,128]{1,0:T(8,128)(2,1)} fusion(bf16[1048576]{0:T(1024)(128)(2,1)} %bitcast.393, bf16[1048576]{0:T(1024)(128)(2,1)S(1)} %bitcast.391, bf16[262144]{0:T(1024)(128)(2,1)S(1)} %bitcast.415, bf16[786432]{0:T(1024)(128)(2,1)} %reshape.601), kind=kLoop, calls=%fused_computation.56 | loop fusion | flops 25165824 | bytes 12582912 | tf_op jit(solution)/shard_map/convert_element_type | solution.py:254
  1336.1 47.5 %all-to-all-done.6 = bf16[256,4,1024]{2,0,1:T(8,128)(2,1)} async-done(((bf16[256,4,1024]{2,0,1:T(8,128)(2,1)}), bf16[256,4,1024]{2,0,1:T(8,128)(2,1)}, u32[]{:S(2)}, u32[]{:S(2)}) %all-to-all-start.6) | async-done | bytes 2097184 | tf_op jit(solution)/shard_map/all_to_all | solution.py:229
  1394.4 60.0 %all-gather.43.cloned.1.call-done = bf16[1024,1024]{0,1:T(8,128)(2,1)} async-done(((bf16[256,1024]{0,1:T(8,128)(2,1)}), bf16[1024,1024]{0,1:T(8,128)(2,1)}) %all-gather.43.cloned.1.call-update) | async-done | bytes 2097168 | tf_op jit(solution)/shard_map/all_gather | solution.py:224
  1459.9 41.3 %all-gather.41.cloned.1.call-done = bf16[1024,1024]{1,0:T(8,128)(2,1)} async-done(((bf16[256,1024]{1,0:T(8,128)(2,1)}), bf16[1024,1024]{1,0:T(8,128)(2,1)}) %all-gather.41.cloned.1.call-update) | async-done | bytes 2097168 | tf_op jit(solution)/shard_map/all_gather | solution.py:225
  1510.2 141.3 %all-gather.47.cloned.1.call-done = bf16[1024,4096]{1,0:T(8,128)(2,1)} async-done(((bf16[256,4096]{1,0:T(8,128)(2,1)}), bf16[1024,4096]{1,0:T(8,128)(2,1)}) %all-gather.47.cloned.1.call-update) | async-done | bytes 8388624 | tf_op jit(solution)/shard_map/all_gather | solution.py:222
  1659.6 45.3 %maximum_bitcast_fusion.1 = bf16[24576,128]{1,0:T(8,128)(2,1)} fusion(bf16[1048576]{0:T(1024)(128)(2,1)S(1)} %bitcast.394, bf16[1048576]{0:T(1024)(128)(2,1)S(1)} %bitcast.392, bf16[262144]{0:T(1024)(128)(2,1)S(1)} %bitcast.418, bf16[786432]{0:T(1024)(128)(2,1)S(1)} %copy-done.21), kind=kLoop, calls=%fused_computation.57 | loop fusion | flops 25165824 | bytes 12582912 | tf_op jit(solution)/shard_map/convert_element_type | solution.py:254
  1733.6 42.9 %all-reduce.5.cloned.1.call-done = (f32[12288]{0:T(1024)}, f32[12288]{0:T(1024)}) async-done(((f32[12288]{0:T(1024)}, f32[12288]{0:T(1024)}), (f32[12288]{0:T(1024)}, f32[12288]{0:T(1024)})) %all-reduce.5.cloned.1.call-update) | async-done | bytes 98320
  1778.7 63.8 %reduce-scatter.15.cloned.1.call-done = bf16[3072,128]{1,0:T(8,128)(2,1)} async-done(((bf16[24576,128]{1,0:T(8,128)(2,1)}), bf16[3072,128]{1,0:T(8,128)(2,1)}) %reduce-scatter.15.cloned.1.call-update) | async-done | bytes 786448 | tf_op jit(solution)/shard_map/reduce_scatter | solution.py:253
  1842.6 65.6 %reduce-scatter.17.cloned.1.call-done = bf16[3072,128]{1,0:T(8,128)(2,1)} async-done(((bf16[24576,128]{1,0:T(8,128)(2,1)}), bf16[3072,128]{1,0:T(8,128)(2,1)}) %reduce-scatter.17.cloned.1.call-update) | async-done | bytes 786448 | tf_op jit(solution)/shard_map/reduce_scatter | solution.py:253
  (390 shorter events, 606.9 us)
Async XLA Ops:
  10.6 130.7 %all-gather.53.cloned.1.call-start = ((), (), s32[]{:S(2)}) async-start(), calls=%async_computation.34 | async-start | bytes 3932160 | tf_op jit(solution)/shard_map/all_gather | solution.py:54
  11.3 256.0 %all-gather.51.cloned.1.call-start = ((), (), s32[]{:S(2)}) async-start(), calls=%async_computation.33 | async-start | bytes 28311552 | tf_op jit(solution)/shard_map/all_gather | solution.py:58
  77.0 339.3 %all-gather.55.cloned.1.call-start = ((), (), s32[]{:S(2)}) async-start(), calls=%async_computation.35 | async-start | bytes 28311552 | tf_op jit(solution)/shard_map/all_gather | solution.py:58
  141.3 325.9 %all-gather.27.cloned.1.call-start = ((), (), s32[]{:S(2)}) async-start(), calls=%async_computation.15 | async-start | bytes 2621440 | tf_op jit(solution)/shard_map/all_gather | solution.py:98
  325.5 163.8 %all-gather.25.cloned.1.call-start = ((), (), s32[]{:S(2)}) async-start(), calls=%async_computation.14 | async-start | bytes 2621440 | tf_op jit(solution)/shard_map/all_gather | solution.py:99
  350.2 228.4 %all-gather.31.cloned.1.call-start = ((), (), s32[]{:S(2)}) async-start(), calls=%async_computation.17 | async-start | bytes 2621440 | tf_op jit(solution)/shard_map/all_gather | solution.py:98
  528.9 91.6 %all-gather.29.cloned.1.call-start = ((), (), s32[]{:S(2)}) async-start(), calls=%async_computation.16 | async-start | bytes 2621440 | tf_op jit(solution)/shard_map/all_gather | solution.py:99
  532.6 221.0 %reduce-scatter.9.cloned.1.call-start = ((), (), s32[]{:S(2)}) async-start(), calls=%async_computation.19 | async-start | bytes 2621440 | tf_op jit(solution)/shard_map/reduce_scatter | solution.py:190
  674.5 91.2 %reduce-scatter.7.cloned.1.call-start = ((), (), s32[]{:S(2)}) async-start(), calls=%async_computation.18 | async-start | bytes 2621440 | tf_op jit(solution)/shard_map/reduce_scatter | solution.py:184
  723.2 271.7 %reduce-scatter.13.cloned.1.call-start = ((), (), s32[]{:S(2)}) async-start(), calls=%async_computation.21 | async-start | bytes 2621440 | tf_op jit(solution)/shard_map/reduce_scatter | solution.py:190
  805.7 189.2 %reduce-scatter.11.cloned.1.call-start = ((), (), s32[]{:S(2)}) async-start(), calls=%async_computation.20 | async-start | bytes 2621440 | tf_op jit(solution)/shard_map/reduce_scatter | solution.py:184
  853.5 171.1 %all-gather.35.cloned.1.call-start = ((), (), s32[]{:S(2)}) async-start(), calls=%async_computation.23 | async-start | bytes 2621440 | tf_op jit(solution)/shard_map/all_gather | solution.py:224
  854.2 231.8 %all-gather.37.cloned.1.call-start = ((), (), s32[]{:S(2)}) async-start(), calls=%async_computation.24 | async-start | bytes 2621440 | tf_op jit(solution)/shard_map/all_gather | solution.py:223
  854.8 392.7 %all-gather.39.cloned.1.call-start = ((), (), s32[]{:S(2)}) async-start(), calls=%async_computation.25 | async-start | bytes 10485760 | tf_op jit(solution)/shard_map/all_gather | solution.py:222
  855.4 437.6 %all-gather.33.cloned.1.call-start = ((), (), s32[]{:S(2)}) async-start(), calls=%async_computation.22 | async-start | bytes 2621440 | tf_op jit(solution)/shard_map/all_gather | solution.py:225
  856.0 533.2 %all-gather.45.cloned.1.call-start = ((), (), s32[]{:S(2)}) async-start(), calls=%async_computation.29 | async-start | bytes 2621440 | tf_op jit(solution)/shard_map/all_gather | solution.py:223
  856.6 597.9 %all-gather.43.cloned.1.call-start = ((), (), s32[]{:S(2)}) async-start(), calls=%async_computation.28 | async-start | bytes 2621440 | tf_op jit(solution)/shard_map/all_gather | solution.py:224
  857.1 644.0 %all-gather.41.cloned.1.call-start = ((), (), s32[]{:S(2)}) async-start(), calls=%async_computation.27 | async-start | bytes 2621440 | tf_op jit(solution)/shard_map/all_gather | solution.py:225
  857.9 793.6 %all-gather.47.cloned.1.call-start = ((), (), s32[]{:S(2)}) async-start(), calls=%async_computation.30 | async-start | bytes 10485760 | tf_op jit(solution)/shard_map/all_gather | solution.py:222
  1016.2 82.9 %all-to-all-start = ((bf16[256,4,768]{0,2,1:T(8,128)(2,1)}), bf16[256,4,768]{0,2,1:T(8,128)(2,1)}, u32[]{:S(2)}, u32[]{:S(2)}) async-start(bf16[256,4,768]{0,2,1:T(8,128)(2,1)} %bitcast.67), calls=%async_computation.4 | async-start | bytes 3145728 | tf_op jit(solution)/shard_map/all_to_all | solution.py:231
  1020.7 755.9 %all-reduce.5.cloned.1.call-start = ((), (), s32[]{:S(2)}) async-start(), calls=%async_computation.36 | async-start | bytes 196608
  1099.1 202.7 %all-to-all-start.5 = ((bf16[256,4,256]{2,0,1:T(8,128)(2,1)}), bf16[256,4,256]{2,0,1:T(8,128)(2,1)}, u32[]{:S(2)}, u32[]{:S(2)}) async-start(bf16[256,4,256]{2,0,1:T(8,128)(2,1)} %bitcast.427), calls=%async_computation.10 | async-start | bytes 1048576 | tf_op jit(solution)/shard_map/all_to_all | solution.py:230
  1306.3 536.3 %reduce-scatter.15.cloned.1.call-start = ((), (), s32[]{:S(2)}) async-start(), calls=%async_computation.26 | async-start | bytes 7077888 | tf_op jit(solution)/shard_map/reduce_scatter | solution.py:253
  1387.9 520.2 %reduce-scatter.17.cloned.1.call-start = ((), (), s32[]{:S(2)}) async-start(), calls=%async_computation.31 | async-start | bytes 7077888 | tf_op jit(solution)/shard_map/reduce_scatter | solution.py:253
  (89 other events, 2415.3 us)
Sparse Core Ops, SparseCore 0:
  10.7 66.1 all-gather.48
  79.1 62.1 all-gather.52
  143.2 124.0 all-gather.50
  269.1 125.5 all-gather.54
  396.6 45.9 all-gather.26
  444.6 44.6 all-gather.24
  529.0 44.6 all-gather.30
  575.9 44.6 all-gather.28
  674.6 42.5 reduce-scatter.8
  723.3 42.3 reduce-scatter.6
  805.8 43.4 reduce-scatter.12
  853.6 56.8 reduce-scatter.10
  912.6 92.8 all-gather.34
  1007.0 79.0 all-gather.36
  1088.1 159.3 all-gather.38
  1248.9 44.0 all-gather.32
  1294.4 81.4 all-gather.44
  1377.3 77.0 all-gather.42
  1456.0 45.0 all-gather.40
  1503.1 148.3 all-gather.46
  1657.2 119.3 all-reduce.4
  1779.9 62.5 reduce-scatter.14
  1846.3 61.7 reduce-scatter.16
where the time goes:
time: 1930 us; the launch traced here: 1920 us
  waiting for transfers between devices  1080 us (56%)
  matrix products  333 us (17%)
  local copies, waits for them, and re-layouts  306 us (16%)
  other arithmetic  112 us (6%)
  blocking collectives  42 us (2%)
  starting transfers between devices  33.8 us (2%)
    all_gather x2, waiting for transfers between devices, backward_layer(): lax.all_gather(active, 'ctx', axis=0, tiled=True)  285 us
    unnamed x183, local copies, waits for them, and re-layouts  145 us
    all_gather x2, waiting for transfers between devices, fetch(): lax.all_gather(piece, 'ctx', axis=0, tiled=True)  130 us
    reduce_scatter x2, waiting for transfers between devices, backward_layer(): lax.psum_scatter(slab.astype(jnp.bfloat16), 'dp', scatter_dimension=0, ti...  129 us
    all_gather x2, waiting for transfers between devices, fetch(): lax.all_gather(wide[0], 'dp', axis=1, tiled=True)  104 us
    dot_general x2, matrix products, backward_layer(): jnp.einsum('hts,thd->shd', grad_scores, query_heads, preferred_element_ty...  78.1 us
    all_gather x2, waiting for transfers between devices, backward_layer(): lax.all_gather(normed1, 'ctx', axis=0, tiled=True)  75.7 us
    convert_element_type x2, other arithmetic, backward_layer(): slab.astype(jnp.bfloat16)  75 us
  transfers between devices with their start and end apart: 31, of which 20 were waited for; matrix products, arithmetic and copies ran while one was open for 31% of the time, Pallas kernels for 0%

commit v1 on v0

v1 whole, which is shorter than its diff:
```python
import functools

import jax
import jax.numpy as jnp
from jax import lax
from jax.experimental import pallas as pl
from jax.experimental.pallas import tpu as pltpu
from jax.sharding import PartitionSpec as P

D = 1024
HEADS = 16
HEAD = 64
FF = 4096
LAYERS = 2
STEP = 10
BF = jnp.bfloat16
F32 = jnp.float32
LANES = 128
GROUP = 4
WIDE = D // GROUP
CHUNKS = FF // WIDE

norm_eps = 1e-05
beta_one = 0.9
beta_two = 0.999
rate = 0.01
decay = 0.1
adam_eps = 1e-08
gelu_c = 0.7978845608028654
gelu_a = 0.044715

VMEM_LIMIT = 58 * 1024 * 1024

ROWS = (D, D, D, FF)
PANELS = (3 * D // 4 // LANES, D // 4 // LANES, FF // 4 // LANES, D // 4 // LANES)


def pieces_of(count):
    size = sum(r * p for r, p in zip(ROWS, PANELS)) // count
    result = []
    for d in range(count):
        low, high = d * size, (d + 1) * size
        held, start = [], 0
        for mat in range(4):
            end = start + ROWS[mat] * PANELS[mat]
            a, b = max(low, start), min(high, end)
            if a < b:
                held.append((mat, (a - start) // PANELS[mat], (b - start) // PANELS[mat], a - low))
            start = end
        result.append(held)
    return size, result


def params_of(**extra):
    return pltpu.CompilerParams(vmem_limit_bytes=VMEM_LIMIT, **extra)


ANY = pl.BlockSpec(memory_space=pl.ANY)
VM = pl.BlockSpec(memory_space=pltpu.VMEM)
SM = pl.BlockSpec(memory_space=pltpu.SMEM)


def shape(dims, dtype):
    return jax.ShapeDtypeStruct(dims, dtype)


def nt(a, b):
    return lax.dot_general(a, b, (((1,), (1,)), ((), ())), preferred_element_type=F32)


def tn(a, b):
    return lax.dot_general(a, b, (((0,), (0,)), ((), ())), preferred_element_type=F32)


def nn(a, b):
    return jnp.dot(a, b, preferred_element_type=F32)


def norm_parts(values):
    center = values - jnp.mean(values, axis=-1, keepdims=True)
    spread = jnp.mean(center * center, axis=-1, keepdims=True)
    scale = lax.rsqrt(spread + norm_eps)
    return center * scale, scale


def norm_back(values, gain, grad):
    hat, scale = norm_parts(values)
    dhat = grad * gain
    back = scale * (
        dhat
        - jnp.mean(dhat, axis=-1, keepdims=True)
        - hat * jnp.mean(dhat * hat, axis=-1, keepdims=True)
    )
    return back, jnp.sum(grad * hat, axis=0, keepdims=True), jnp.sum(grad, axis=0, keepdims=True)


def load_matrix(whole, target, mat, pieces, sem):
    for c in range(4):
        for d, held in enumerate(pieces):
            for m, k0, k1, base in held:
                if m != mat:
                    continue
                for j in range(PANELS[mat]):
                    pltpu.make_async_copy(
                        whole.at[c, d, pl.ds(base + j * (k1 - k0), k1 - k0)],
                        target.at[c * PANELS[mat] + j, pl.ds(k0, k1 - k0)],
                        sem,
                    ).start()


def wait_all(ref, sem):
    pltpu.make_async_copy(ref, ref, sem).wait()


def store_matrix(stage, whole, mat, pieces, sem):
    for c in range(4):
        for d, held in enumerate(pieces):
            for m, k0, k1, base in held:
                if m != mat:
                    continue
                for j in range(PANELS[mat]):
                    pltpu.make_async_copy(
                        stage.at[c * PANELS[mat] + j, pl.ds(k0, k1 - k0)],
                        whole.at[c, d, pl.ds(base + j * (k1 - k0), k1 - k0)],
                        sem,
                    ).start()


def prep_kernel(plan, me, slab, out):
    for d, held in enumerate(plan.pieces):

        @pl.when(me[0] == d)
        def _(held=held):
            for mat, k0, k1, base in held:
                count, step = k1 - k0, PANELS[mat]
                for j in range(step):
                    out[pl.ds(base + j * count, count), :] = slab[pl.ds(base + j, count, stride=step), :].astype(BF)


def prepare(plan, me, slab):
    return pl.pallas_call(
        functools.partial(prep_kernel, plan),
        out_shape=shape((plan.size, LANES), BF),
        in_specs=[SM, VM],
        out_specs=VM,
        compiler_params=params_of(),
        name="prep",
    )(me, slab)


def qkv_kernel(pieces, me, x, vec, whole, normed, out0, out1, out2, out3, weight, qkv, sem):
    load_matrix(whole, weight, 0, pieces, sem)
    hat, _ = norm_parts(x[...])
    normed[...] = (hat * vec[0:1, :] + vec[1:2, :]).astype(BF)
    wait_all(weight, sem)
    for b in range(3 * GROUP):
        kind, at = b // GROUP, b % GROUP
        acc = nn(normed[...], jnp.concatenate([weight[2 * b], weight[2 * b + 1]], axis=1))
        if kind != 1:
            row = 2 if kind == 0 else 3
            acc = acc + vec[row : row + 1, at * WIDE : (at + 1) * WIDE]
        qkv[b] = acc.astype(BF)
    mine = me[0] % GROUP
    for r, out in enumerate((out0, out1, out2, out3)):
        for kind in range(3):
            out[:, kind * WIDE : (kind + 1) * WIDE] = qkv[kind * GROUP + (mine ^ r)]


def qkv_call(plan, me, x, vec, whole):
    rows = x.shape[0]
    return pl.pallas_call(
        functools.partial(qkv_kernel, plan.pieces),
        out_shape=[shape((rows, D), BF)] + [shape((rows, 3 * WIDE), BF)] * GROUP,
        in_specs=[SM, VM, VM, ANY],
        out_specs=[VM] * 5,
        scratch_shapes=[
            pltpu.VMEM((3 * D // LANES, D, LANES), BF),
            pltpu.VMEM((3 * GROUP, rows, WIDE), BF),
            pltpu.SemaphoreType.DMA,
        ],
        compiler_params=params_of(),
        name="qkv",
    )(me, x, vec, whole)


def diagonal(rows):
    return lax.broadcasted_iota(jnp.int32, (rows, rows), 1) <= lax.broadcasted_iota(jnp.int32, (rows, rows), 0)


def attend_kernel(me, in0, in1, in2, in3, out0, out1, out2, out3, lse, q, k, v, o):
    mine = me[0] % GROUP
    rows = in0.shape[0]
    for r, ref in enumerate((in0, in1, in2, in3)):
        at = pl.ds(pl.multiple_of((mine ^ r) * rows, rows), rows)
        q[at, :] = ref[:, 0:WIDE]
        k[at, :] = ref[:, WIDE : 2 * WIDE]
        v[at, :] = ref[:, 2 * WIDE : 3 * WIDE]
    seen = diagonal(rows)
    for h in range(WIDE // HEAD):
        cols = slice(h * HEAD, (h + 1) * HEAD)
        for i in range(GROUP):
            here = slice(i * rows, (i + 1) * rows)
            qi = q[here, cols]
            near = jnp.where(seen, nt(qi, k[here, cols]) * 0.125, -1000000000.0)
            top = jnp.max(near, axis=1, keepdims=True)
            if i:
                far = nt(qi, k[0 : i * rows, cols]) * 0.125
                top = jnp.maximum(top, jnp.max(far, axis=1, keepdims=True))
                far = jnp.exp(far - top)
            near = jnp.exp(near - top)
            total = jnp.sum(near, axis=1, keepdims=True)
            if i:
                total = total + jnp.sum(far, axis=1, keepdims=True)
            inv = 1.0 / total
            res = nn((near * inv).astype(BF), v[here, cols])
            if i:
                res = res + nn((far * inv).astype(BF), v[0 : i * rows, cols])
            o[i, :, cols] = res.astype(BF)
            lse[here, h : h + 1] = top + jnp.log(total)
    for r, out in enumerate((out0, out1, out2, out3)):
        out[...] = o[mine ^ r]


def attend_call(me, heads):
    rows = heads[0].shape[0]
    span = GROUP * rows
    return pl.pallas_call(
        attend_kernel,
        out_shape=[shape((rows, WIDE), BF)] * GROUP + [shape((span, LANES), F32)],
        in_specs=[SM] + [VM] * GROUP,
        out_specs=[VM] * 5,
        scratch_shapes=[pltpu.VMEM((span, WIDE), BF)] * 3 + [pltpu.VMEM((GROUP, rows, WIDE), BF)],
        compiler_params=params_of(),
        name="attend",
    )(me, *heads)


def side(ref, at, count=2):
    return jnp.concatenate([ref[at + i] for i in range(count)], axis=1)


def rows_of(ref, at):
    return jnp.concatenate([ref[p, at, :] for p in range(D // LANES)], axis=1)


def ff_kernel(
    pieces, me, in0, in1, in2, in3, x, vec, bias, whole,
    attended, hidden, normed, upper, active, out,
    wo, we, wr, parts, sems,
):
    load_matrix(whole, wo, 1, pieces, sems.at[0])
    load_matrix(whole, we, 2, pieces, sems.at[1])
    load_matrix(whole, wr, 3, pieces, sems.at[2])
    mine = me[0] % GROUP
    for r, ref in enumerate((in0, in1, in2, in3)):
        parts[mine ^ r] = ref[...]
    for g in range(GROUP):
        attended[:, g * WIDE : (g + 1) * WIDE] = parts[g]
    wait_all(wo, sems.at[0])
    for g in range(GROUP):
        cols = slice(g * WIDE, (g + 1) * WIDE)
        hidden[:, cols] = x[:, cols] + nn(attended[...], side(wo, 2 * g)) + vec[4:5, cols]
    hat, _ = norm_parts(hidden[...])
    normed[...] = (hat * vec[5:6, :] + vec[6:7, :]).astype(BF)
    out[...] = hidden[...] + vec[11:12, :]
    wait_all(we, sems.at[1])
    wait_all(wr, sems.at[2])

    def body(n, _):
        u = nn(normed[...], side(we, 2 * n)) + bias[n]
        upper[n] = u
        act = (0.5 * u * (1.0 + jnp.tanh(gelu_c * (u + gelu_a * u * u * u)))).astype(BF)
        active[n] = act
        out[...] += nn(act, rows_of(wr, pl.ds(pl.multiple_of(n * WIDE, WIDE), WIDE)))
        return 0

    lax.fori_loop(0, CHUNKS, body, 0)


def ff_call(plan, me, heads, x, vec, bias, whole):
    rows = x.shape[0]
    return pl.pallas_call(
        functools.partial(ff_kernel, plan.pieces),
        out_shape=[
            shape((rows, D), BF),
            shape((rows, D), F32),
            shape((rows, D), BF),
            shape((CHUNKS, rows, WIDE), F32),
            shape((CHUNKS, rows, WIDE), BF),
            shape((rows, D), F32),
        ],
        in_specs=[SM] + [VM] * 7 + [ANY],
        out_specs=[VM] * 6,
        scratch_shapes=[
            pltpu.VMEM((D // LANES, D, LANES), BF),
            pltpu.VMEM((FF // LANES, D, LANES), BF),
            pltpu.VMEM((D // LANES, FF, LANES), BF),
            pltpu.VMEM((GROUP, rows, WIDE), BF),
            pltpu.SemaphoreType.DMA((3,)),
        ],
        compiler_params=params_of(),
        name="ff",
    )(me, *heads, x, vec, bias, whole)


def ff_back_kernel(
    pieces, me, dy, upper, hidden, vec, whole,
    dyb, dub, dh, dhb, out0, out1, out2, out3, bias_grad, vec_grad,
    wo, we, wr, acc, parts, sems,
):
    load_matrix(whole, wr, 3, pieces, sems.at[2])
    load_matrix(whole, we, 2, pieces, sems.at[1])
    load_matrix(whole, wo, 1, pieces, sems.at[0])
    dyb[...] = dy[...].astype(BF)
    vec_grad[0:1, :] = jnp.sum(dy[...], axis=0, keepdims=True)
    acc[...] = jnp.zeros_like(acc)
    wait_all(wr, sems.at[2])
    wait_all(we, sems.at[1])

    def body(n, _):
        dg = nt(dyb[...], rows_of(wr, pl.ds(pl.multiple_of(n * WIDE, WIDE), WIDE)))
        u = upper[n]
        t = jnp.tanh(gelu_c * (u + gelu_a * u * u * u))
        slope = 0.5 * (1.0 + t) + 0.5 * u * (1.0 - t * t) * (gelu_c * (1.0 + 3.0 * gelu_a * u * u))
        du = dg * slope
        bias_grad[n] = jnp.sum(du, axis=0, keepdims=True)
        low = du.astype(BF)
        dub[n] = low
        acc[...] += nt(low, side(we, 2 * n))
        return 0

    lax.fori_loop(0, CHUNKS, body, 0)
    back, gain, shift = norm_back(hidden[...], vec[5:6, :], acc[...])
    total = dy[...] + back
    vec_grad[1:2, :] = gain
    vec_grad[2:3, :] = shift
    vec_grad[3:4, :] = jnp.sum(total, axis=0, keepdims=True)
    vec_grad[4:8, :] = jnp.zeros((4, D), F32)
    dh[...] = total
    dhb[...] = total.astype(BF)
    wait_all(wo, sems.at[0])
    for g in range(GROUP):
        parts[g] = nt(dhb[...], rows_of(wo, slice(g * WIDE, (g + 1) * WIDE))).astype(BF)
    mine = me[0] % GROUP
    for r, out in enumerate((out0, out1, out2, out3)):
        out[...] = parts[mine ^ r]


def ff_back_call(plan, me, dy, upper, hidden, vec, whole):
    rows = dy.shape[0]
    return pl.pallas_call(
        functools.partial(ff_back_kernel, plan.pieces),
        out_shape=[
            shape((rows, D), BF),
            shape((CHUNKS, rows, WIDE), BF),
            shape((rows, D), F32),
            shape((rows, D), BF),
        ]
        + [shape((rows, WIDE), BF)] * GROUP
        + [shape((CHUNKS, 1, WIDE), F32), shape((8, D), F32)],
        in_specs=[SM] + [VM] * 4 + [ANY],
        out_specs=[VM] * 10,
        scratch_shapes=[
            pltpu.VMEM((D // LANES, D, LANES), BF),
            pltpu.VMEM((FF // LANES, D, LANES), BF),
            pltpu.VMEM((D // LANES, FF, LANES), BF),
            pltpu.VMEM((rows, D), F32),
            pltpu.VMEM((GROUP, rows, WIDE), BF),
            pltpu.SemaphoreType.DMA((3,)),
        ],
        compiler_params=params_of(),
        name="ff_back",
    )(me, dy, upper, hidden, vec, whole)


def attend_back_kernel(
    me, in0, in1, in2, in3, do0, do1, do2, do3, lse,
    out0, out1, out2, out3, sums,
    q, k, v, do, dq, dk, dv,
):
    mine = me[0] % GROUP
    rows = in0.shape[0]
    for r, (ref, grad) in enumerate(((in0, do0), (in1, do1), (in2, do2), (in3, do3))):
        at = pl.ds(pl.multiple_of((mine ^ r) * rows, rows), rows)
        q[at, :] = ref[:, 0:WIDE]
        k[at, :] = ref[:, WIDE : 2 * WIDE]
        v[at, :] = ref[:, 2 * WIDE : 3 * WIDE]
        do[at, :] = grad[...]
    seen = diagonal(rows)
    for h in range(WIDE // HEAD):
        cols = slice(h * HEAD, (h + 1) * HEAD)
        total = jnp.zeros((1, HEAD), F32)
        for i in reversed(range(GROUP)):
            here = slice(i * rows, (i + 1) * rows)
            past = slice(0, i * rows)
            qi, doi, ls = q[here, cols], do[here, cols], lse[here, h : h + 1]
            near = jnp.exp(jnp.where(seen, nt(qi, k[here, cols]) * 0.125, -1000000000.0) - ls)
            dnear = nt(doi, v[here, cols])
            inner = jnp.sum(near * dnear, axis=1, keepdims=True)
            if i:
                far = jnp.exp(nt(qi, k[past, cols]) * 0.125 - ls)
                dfar = nt(doi, v[past, cols])
                inner = inner + jnp.sum(far * dfar, axis=1, keepdims=True)
            snear = (near * (dnear - inner) * 0.125).astype(BF)
            res = nn(snear, k[here, cols])
            dkn = tn(snear, qi)
            dvn = tn(near.astype(BF), doi)
            last = i == GROUP - 1
            dk[here, cols] = dkn if last else dk[here, cols] + dkn
            dv[here, cols] = dvn if last else dv[here, cols] + dvn
            if i:
                sfar = (far * (dfar - inner) * 0.125).astype(BF)
                res = res + nn(sfar, k[past, cols])
                dkf = tn(sfar, qi)
                dvf = tn(far.astype(BF), doi)
                dk[past, cols] = dkf if last else dk[past, cols] + dkf
                dv[past, cols] = dvf if last else dv[past, cols] + dvf
            total = total + jnp.sum(res, axis=0, keepdims=True)
            dq[i, :, cols] = res.astype(BF)
        sums[0:1, cols] = total
    sums[1:2, :] = jnp.sum(dv[...], axis=0, keepdims=True)
    sums[2:8, :] = jnp.zeros((6, WIDE), F32)
    for r, out in enumerate((out0, out1, out2, out3)):
        at = pl.ds(pl.multiple_of((mine ^ r) * rows, rows), rows)
        out[:, 0:WIDE] = dq[mine ^ r]
        out[:, WIDE : 2 * WIDE] = dk[at, :].astype(BF)
        out[:, 2 * WIDE : 3 * WIDE] = dv[at, :].astype(BF)


def attend_back_call(me, heads, grads, lse):
    rows = heads[0].shape[0]
    span = GROUP * rows
    return pl.pallas_call(
        attend_back_kernel,
        out_shape=[shape((rows, 3 * WIDE), BF)] * GROUP + [shape((8, WIDE), F32)],
        in_specs=[SM] + [VM] * 9,
        out_specs=[VM] * 5,
        scratch_shapes=[pltpu.VMEM((span, WIDE), BF)] * 4
        + [pltpu.VMEM((GROUP, rows, WIDE), BF)]
        + [pltpu.VMEM((span, WIDE), F32)] * 2,
        compiler_params=params_of(),
        name="attend_back",
    )(me, *heads, *grads, lse)


def qkv_back_kernel(pieces, me, in0, in1, in2, in3, dh, x, vec, whole, mixed, dx, vec_grad, weight, acc, sem):
    load_matrix(whole, weight, 0, pieces, sem)
    mine = me[0] % GROUP
    for r, ref in enumerate((in0, in1, in2, in3)):
        for kind in range(3):
            mixed[kind * GROUP + (mine ^ r)] = ref[:, kind * WIDE : (kind + 1) * WIDE]
    acc[...] = jnp.zeros_like(acc)
    wait_all(weight, sem)

    def body(b, _):
        acc[...] += nt(mixed[b], side(weight, 2 * b))
        return 0

    lax.fori_loop(0, 3 * GROUP, body, 0)
    back, gain, shift = norm_back(x[...], vec[0:1, :], acc[...])
    dx[...] = dh[...] + back
    vec_grad[0:1, :] = gain
    vec_grad[1:2, :] = shift
    vec_grad[2:8, :] = jnp.zeros((6, D), F32)


def qkv_back_call(plan, me, grads, dh, x, vec, whole):
    rows = x.shape[0]
    return pl.pallas_call(
        functools.partial(qkv_back_kernel, plan.pieces),
        out_shape=[shape((3 * GROUP, rows, WIDE), BF), shape((rows, D), F32), shape((8, D), F32)],
        in_specs=[SM] + [VM] * 7 + [ANY],
        out_specs=[VM] * 3,
        scratch_shapes=[
            pltpu.VMEM((3 * D // LANES, D, LANES), BF),
            pltpu.VMEM((rows, D), F32),
            pltpu.SemaphoreType.DMA,
        ],
        compiler_params=params_of(),
        name="qkv_back",
    )(me, *grads, dh, x, vec, whole)


def ff_weight_kernel(pieces, attended, normed, active, dhb, dub, dyb, out, so, se, sr, sems):
    def reduce_body(n, _):
        res = tn(active[n], dyb[...]).astype(BF)
        at = pl.ds(pl.multiple_of(n * WIDE, WIDE), WIDE)
        for p in range(D // LANES):
            sr[p, at, :] = res[:, p * LANES : (p + 1) * LANES]
        return 0

    lax.fori_loop(0, CHUNKS, reduce_body, 0)
    store_matrix(sr, out, 3, pieces, sems.at[2])

    def expand_body(n, _):
        res = tn(normed[...], dub[n]).astype(BF)
        se[2 * n] = res[:, :LANES]
        se[2 * n + 1] = res[:, LANES:]
        return 0

    lax.fori_loop(0, CHUNKS, expand_body, 0)
    store_matrix(se, out, 2, pieces, sems.at[1])
    for g in range(GROUP):
        res = tn(attended[...], dhb[:, g * WIDE : (g + 1) * WIDE]).astype(BF)
        so[2 * g] = res[:, :LANES]
        so[2 * g + 1] = res[:, LANES:]
    store_matrix(so, out, 1, pieces, sems.at[0])
    wait_all(sr, sems.at[2])
    wait_all(se, sems.at[1])
    wait_all(so, sems.at[0])


def ff_weight_call(plan, attended, normed, active, dhb, dub, dyb):
    return pl.pallas_call(
        functools.partial(ff_weight_kernel, plan.pieces),
        out_shape=shape((4, plan.n_dp, plan.size, LANES), BF),
        in_specs=[VM] * 6,
        out_specs=ANY,
        scratch_shapes=[
            pltpu.VMEM((D // LANES, D, LANES), BF),
            pltpu.VMEM((FF // LANES, D, LANES), BF),
            pltpu.VMEM((D // LANES, FF, LANES), BF),
            pltpu.SemaphoreType.DMA((3,)),
        ],
        compiler_params=params_of(),
        name="ff_weight",
    )(attended, normed, active, dhb, dub, dyb)


def qkv_weight_kernel(pieces, normed, mixed, before, out, stage, sem):
    def body(b, _):
        res = tn(normed[...], mixed[b]).astype(BF)
        stage[2 * b] = res[:, :LANES]
        stage[2 * b + 1] = res[:, LANES:]
        return 0

    lax.fori_loop(0, 3 * GROUP, body, 0)
    store_matrix(stage, out, 0, pieces, sem)
    wait_all(stage, sem)


def qkv_weight_call(plan, normed, mixed, buffer):
    return pl.pallas_call(
        functools.partial(qkv_weight_kernel, plan.pieces),
        out_shape=shape(buffer.shape, BF),
        in_specs=[VM, VM, ANY],
        out_specs=ANY,
        input_output_aliases={2: 0},
        scratch_shapes=[pltpu.VMEM((3 * D // LANES, D, LANES), BF), pltpu.SemaphoreType.DMA],
        compiler_params=params_of(),
        name="qkv_weight",
    )(normed, mixed, buffer)


def adam_parts(grad, moment, square, master, weight_decay):
    moment_next = beta_one * moment + (1.0 - beta_one) * grad
    square_next = beta_two * square + (1.0 - beta_two) * grad * grad
    corrected = moment_next / (1.0 - beta_one**STEP)
    scaled = square_next / (1.0 - beta_two**STEP)
    update = -rate * (corrected / (jnp.sqrt(scaled) + adam_eps) + weight_decay * master)
    return moment_next, square_next, update


def adam_kernel(plan, me, owned, master, moment, square, *refs):
    grad, moment_next, square_next, update = refs[-4:]
    for d, held in enumerate(plan.pieces):

        @pl.when(me[0] == d)
        def _(held=held):
            for mat, k0, k1, base in held:
                size, step = k1 - k0, PANELS[mat]
                for j in range(step):
                    grad[0, 0, pl.ds(base + j, size, stride=step), :] = owned[pl.ds(base + j * size, size), :]

    new = adam_parts(grad[0, 0], moment[0, 0], square[0, 0], master[0, 0], decay)
    moment_next[0, 0], square_next[0, 0], update[0, 0] = new


def adam_call(plan, me, layer, grads, master, moment, square, before):
    block = pl.BlockSpec((1, 1) + master.shape[2:], lambda i: (layer, 0, 0, 0))
    whole = [pl.BlockSpec(g.shape, lambda i: (0, 0)) for g in grads]
    first = 1 + len(grads) + 3
    return pl.pallas_call(
        functools.partial(adam_kernel, plan),
        grid=(1,),
        out_shape=[shape(master.shape, F32)] * 4,
        in_specs=[SM] + whole + [block] * 3 + [ANY] * len(before),
        out_specs=[block] * 4,
        input_output_aliases={first + i: i for i in range(len(before))},
        compiler_params=params_of(),
        name="adam",
    )(me, *grads, master, moment, square, *before)


class Mover:
    def __init__(self, n_dp):
        self.n_dp = n_dp
        self.size, self.pieces = pieces_of(n_dp)

    def gather_all(self, helds):
        wholes = [lax.all_gather(held, ("ctx", "dp"), axis=0, tiled=True) for held in helds]
        return [whole.reshape(4, self.n_dp, self.size, LANES) for whole in wholes]

    def scatter(self, buffer):
        flat = buffer.reshape(-1, LANES)
        return [lax.psum_scatter(flat, ("ctx", "dp"), scatter_dimension=0, tiled=True).astype(F32)]

    def scatter_vectors(self, grads):
        return lax.psum_scatter(grads.reshape(-1), ("dp", "ctx"), scatter_dimension=0, tiled=True)


MESH = pl.DeviceIdType.MESH
CORE = 1
FLIPS = ((1, 0), (2, 0), (4, 0), (0, 1), (0, 2), (0, 3))


def exchange(values, flip_dp, flip_ctx):
    pairs = [(d * 4 + z, (d ^ flip_dp) * 4 + (z ^ flip_ctx)) for d in range(8) for z in range(4)]
    return lax.ppermute(values, ("dp", "ctx"), pairs)


def greet(d, z):
    barrier = pltpu.get_barrier_semaphore()
    for fd, fz in FLIPS:
        pl.semaphore_signal(barrier, inc=1, device_id=(d ^ fd, z ^ fz), device_id_type=MESH)
    pl.semaphore_wait(barrier, len(FLIPS))


def run_jobs(jobs, lag):
    live = list(zip(jobs, lag))
    step = 0
    while live:
        rest = []
        for job, late in live:
            if step >= late:
                try:
                    next(job)
                except StopIteration:
                    continue
            rest.append((job, late))
        live = rest
        step += 1


class BitMover(Mover):
    def __init__(self, n_dp):
        super().__init__(n_dp)
        unit = self.size // 6
        self.rows = [(0, 2 * unit), (2 * unit, 2 * unit), (4 * unit, unit), (5 * unit, unit)]
        self.orders = [(True, 2, 4), (True, 4, 2), (False, 2, 4), (False, 4, 2)]

    def gather_all(self, helds):
        layers = len(helds)
        per_job = 16

        def kernel(*refs):
            helds, wholes = refs[:layers], refs[layers : 2 * layers]
            local, send, recv = refs[2 * layers :]
            d, z = lax.axis_index("dp"), lax.axis_index("ctx")
            greet(d, z)

            def job(layer, part):
                low, size = self.rows[part]
                z_first, a, b = self.orders[part]
                rows = pl.ds(low, size)
                held, whole = helds[layer].at[rows], wholes[layer]
                slots = iter(range((layer * 4 + part) * per_job, (layer * 4 + part + 1) * per_job))
                started = []

                def push(src, dst, fd, fz):
                    slot = next(slots)
                    copy = pltpu.make_async_remote_copy(
                        src_ref=src, dst_ref=dst, send_sem=send.at[slot], recv_sem=recv.at[slot],
                        device_id=(d ^ fd, z ^ fz), device_id_type=MESH,
                    )
                    copy.start()
                    started.append(copy)
                    return copy

                def line(dd, fd):
                    ref = whole.at[:, dd, rows]
                    return push(ref, ref, fd, 0)

                own = pltpu.make_async_copy(held, whole.at[z, d, rows], local.at[layer * 4 + part])
                own.start()
                mine = [push(held, whole.at[z, d, rows], 0, k) for k in (3, 2, 1)]
                if z_first:
                    yield
                    own.wait()
                    for copy in mine:
                        copy.wait_recv()
                    first = line(d, a)
                    second = line(d, b)
                    cores = [line(d, CORE)]
                    yield
                    first.wait_recv()
                    third = line(d ^ a, b)
                    cores.append(line(d ^ a, CORE))
                    yield
                    second.wait_recv()
                    cores.append(line(d ^ b, CORE))
                    third.wait_recv()
                    cores.append(line(d ^ a ^ b, CORE))
                else:
                    first = push(held, whole.at[z, d, rows], a, 0)
                    yield
                    first.wait_recv()
                    other = whole.at[z, d ^ a, rows]
                    theirs = [push(other, other, 0, k) for k in (3, 2, 1)]
                    yield
                    own.wait()
                    for copy in mine:
                        copy.wait_recv()
                    second = line(d, b)
                    cores = [line(d, CORE)]
                    yield
                    for copy in theirs:
                        copy.wait_recv()
                    third = line(d ^ a, b)
                    cores.append(line(d ^ a, CORE))
                    yield
                    second.wait_recv()
                    cores.append(line(d ^ b, CORE))
                    third.wait_recv()
                    cores.append(line(d ^ a ^ b, CORE))
                yield
                for copy in cores:
                    copy.wait_recv()
                for copy in started:
                    copy.wait_send()

            jobs = [job(layer, part) for layer in range(layers) for part in range(4)]
            run_jobs(jobs, [2 * (i // 4) for i in range(len(jobs))])

        count = layers * 4 * per_job
        return pl.pallas_call(
            kernel,
            out_shape=[shape((4, self.n_dp, self.size, LANES), BF)] * layers,
            in_specs=[VM] * layers,
            out_specs=[ANY] * layers,
            scratch_shapes=[
                pltpu.SemaphoreType.DMA((4 * layers,)),
                pltpu.SemaphoreType.DMA((count,)),
                pltpu.SemaphoreType.DMA((count,)),
            ],
            compiler_params=params_of(collective_id=1, has_side_effects=True),
            name="gather",
        )(*helds)

    def scatter(self, buffer):
        per_job = 16

        def kernel(grads, out, *scratch):
            sums, cores, bees, ays, zees = (scratch[i : i + 4] for i in range(0, 20, 4))
            local, send, recv = scratch[20:]
            d, z = lax.axis_index("dp"), lax.axis_index("ctx")
            greet(d, z)

            def job(part):
                low, size = self.rows[part]
                z_first, a, b = self.orders[part]
                rows = pl.ds(low, size)
                acc, from_c, from_b, from_a, from_z = sums[part], cores[part], bees[part], ays[part], zees[part]
                slots = iter(range(part * per_job, (part + 1) * per_job))
                started = []

                def push(src, dst, fd, fz):
                    slot = next(slots)
                    copy = pltpu.make_async_remote_copy(
                        src_ref=src, dst_ref=dst, send_sem=send.at[slot], recv_sem=recv.at[slot],
                        device_id=(d ^ fd, z ^ fz), device_id_type=MESH,
                    )
                    copy.start()
                    started.append(copy)
                    return copy

                def add(into, more):
                    block = 256

                    def body(i, _):
                        at = pl.ds(pl.multiple_of(i * block, block), block)
                        for x, y in zip(into, more):
                            x[at, :] = x[at, :] + y[at, :]
                        return 0

                    lax.fori_loop(0, size // block, body, 0)

                places = [(1, 1), (0, 1), (1, 0), (0, 0)]
                loads, gives = [], []
                for i, (ja, jb) in enumerate(places):
                    here = d ^ (ja * a) ^ (jb * b)
                    load = pltpu.make_async_copy(grads.at[:, here, rows], acc.at[i], local.at[part * 4 + i])
                    load.start()
                    loads.append(load)
                    gives.append(push(grads.at[:, here ^ CORE, rows], from_c.at[i], CORE, 0))
                yield
                for i in (0, 1):
                    loads[i].wait()
                    gives[i].wait_recv()
                    add([acc.at[i, k] for k in range(4)], [from_c.at[i, k] for k in range(4)])
                to_b = [push(acc.at[i], from_b.at[i], b, 0) for i in (0, 1)]
                for i in (2, 3):
                    loads[i].wait()
                    gives[i].wait_recv()
                    add([acc.at[i, k] for k in range(4)], [from_c.at[i, k] for k in range(4)])
                yield
                if z_first:
                    to_b[0].wait_recv()
                    add([acc.at[2, k] for k in range(4)], [from_b.at[0, k] for k in range(4)])
                    to_a = push(acc.at[2], from_a, a, 0)
                    to_b[1].wait_recv()
                    add([acc.at[3, k] for k in range(4)], [from_b.at[1, k] for k in range(4)])
                    yield
                    to_a.wait_recv()
                    add([acc.at[3, k] for k in range(4)], [from_a.at[k] for k in range(4)])
                    to_z = [push(acc.at[3, z ^ k], from_z.at[k - 1, 0], 0, k) for k in (3, 2, 1)]
                    yield
                    for copy in to_z:
                        copy.wait_recv()

                    def total(at):
                        value = acc[3, z, at, :].astype(F32)
                        for k in range(3):
                            value = value + from_z[k, 0, at, :].astype(F32)
                        return value
                else:
                    for i in (0, 1):
                        to_b[i].wait_recv()
                        add([acc.at[2 + i, k] for k in range(4)], [from_b.at[i, k] for k in range(4)])
                    to_z = [push(acc.at[2 + i, z ^ k], from_z.at[k - 1, i], 0, k) for i in (0, 1) for k in (3, 2, 1)]
                    yield
                    for copy in to_z[:3]:
                        copy.wait_recv()
                    for k in range(3):
                        add([acc.at[2, z]], [from_z.at[k, 0]])
                    to_a = push(acc.at[2, z], from_a.at[0], a, 0)
                    for copy in to_z[3:]:
                        copy.wait_recv()
                    yield
                    to_a.wait_recv()

                    def total(at):
                        value = acc[3, z, at, :].astype(F32)
                        for k in range(3):
                            value = value + from_z[k, 1, at, :].astype(F32)
                        return value + from_a[0, at, :].astype(F32)

                def body(i, _):
                    at = pl.multiple_of(i * 256, 256)
                    out[pl.ds(low + at, 256), :] = total(pl.ds(at, 256))
                    return 0

                lax.fori_loop(0, size // 256, body, 0)
                for copy in started:
                    copy.wait_send()

            run_jobs([job(part) for part in range(4)], [0, 0, 0, 0])

        sizes = [size for _, size in self.rows]
        firsts = [order[0] for order in self.orders]
        count = 4 * per_job
        return [
            pl.pallas_call(
                kernel,
                out_shape=shape((self.size, LANES), F32),
                in_specs=[ANY],
                out_specs=VM,
                scratch_shapes=[pltpu.VMEM((4, 4, n, LANES), BF) for n in sizes]
                + [pltpu.VMEM((4, 4, n, LANES), BF) for n in sizes]
                + [pltpu.VMEM((2, 4, n, LANES), BF) for n in sizes]
                + [pltpu.VMEM((4 if first else 1, n, LANES), BF) for n, first in zip(sizes, firsts)]
                + [pltpu.VMEM((3, 1 if first else 2, n, LANES), BF) for n, first in zip(sizes, firsts)]
                + [
                    pltpu.SemaphoreType.DMA((16,)),
                    pltpu.SemaphoreType.DMA((count,)),
                    pltpu.SemaphoreType.DMA((count,)),
                ],
                compiler_params=params_of(collective_id=2, has_side_effects=True),
                name="scatter",
            )(buffer)
        ]

    def scatter_vectors(self, grads):
        d, z = lax.axis_index("dp"), lax.axis_index("ctx")
        value = grads.reshape(2, -1)
        for flip_dp, flip_ctx in ((4, 0), (2, 0), (1, 0), (0, 2), (0, 1)):
            bit = jnp.where((d & flip_dp) + (z & flip_ctx) > 0, 1, 0)
            halves = value.reshape(2, -1)
            keep = lax.dynamic_index_in_dim(halves, bit, 0, keepdims=False)
            give = lax.dynamic_index_in_dim(halves, 1 - bit, 0, keepdims=False)
            value = keep + exchange(give, flip_dp, flip_ctx)
        return value


def swap(values, n_dp):
    pairs = [
        (d * GROUP + z, ((d // GROUP) * GROUP + z) * GROUP + d % GROUP) for d in range(n_dp) for z in range(GROUP)
    ]
    return lax.ppermute(values, ("dp", "ctx"), pairs)


def trade(arrays, n_dp):
    result = [arrays[0]]
    for r in range(1, GROUP):
        pairs = [(d * GROUP + z, (d ^ r) * GROUP + z) for d in range(n_dp) for z in range(GROUP)]
        result.append(lax.ppermute(arrays[r], ("dp", "ctx"), pairs))
    return result


def per_device(
    n_dp,
    layer_input,
    out_cotangent,
    params,
    vectors,
    param_moment,
    vector_moment,
    param_square,
    vector_square,
):
    plan = BitMover(n_dp) if n_dp == 8 else Mover(n_dp)
    me = jnp.stack([lax.axis_index("dp"), lax.axis_index("ctx")]).astype(jnp.int32)
    place = me[0] % GROUP

    wholes = plan.gather_all([prepare(plan, me, params[layer, 0]) for layer in range(LAYERS)])
    lines = lax.all_gather(vectors.astype(BF), ("dp", "ctx"), axis=1, tiled=True).astype(F32)
    vecs = [lines[layer].reshape(12, D) for layer in range(LAYERS)]

    value = swap(layer_input, n_dp).astype(F32)
    grad = swap(out_cotangent, n_dp).astype(F32)

    saved = []
    for layer in range(LAYERS):
        vec, whole = vecs[layer], wholes[layer]
        bias = vec[7:11].reshape(CHUNKS, 1, WIDE)
        normed1, *sent = qkv_call(plan, me, value, vec, whole)
        heads = trade(sent, n_dp)
        *sent, lse = attend_call(me, heads)
        attended, hidden, normed2, upper, active, result = ff_call(
            plan, me, trade(sent, n_dp), value, vec, bias, whole
        )
        saved.append((value, normed1, heads, lse, attended, hidden, normed2, upper, active))
        value = result
    layer_output = swap(value.astype(BF), n_dp)

    owned, vec_owned = [None] * LAYERS, [None] * LAYERS
    for layer in reversed(range(LAYERS)):
        vec, whole = vecs[layer], wholes[layer]
        x, normed1, heads, lse, attended, hidden, normed2, upper, active = saved[layer]
        dyb, dub, dh, dhb, *rest = ff_back_call(plan, me, grad, upper, hidden, vec, whole)
        sent, bias_grad, vec_grad2 = rest[:GROUP], rest[GROUP], rest[GROUP + 1]
        buffer = ff_weight_call(plan, attended, normed2, active, dhb, dub, dyb)
        *sent, sums = attend_back_call(me, heads, trade(sent, n_dp), lse)
        mixed, grad, vec_grad1 = qkv_back_call(plan, me, trade(sent, n_dp), dh, x, vec, whole)
        buffer = qkv_weight_call(plan, normed1, mixed, buffer)
        spread = lax.dynamic_update_slice(jnp.zeros((2, D), F32), sums[0:2], (0, place * WIDE))
        vector_grads = jnp.concatenate(
            [
                vec_grad1[0:2],
                spread,
                vec_grad2[3:4],
                vec_grad2[1:3],
                bias_grad.reshape(4, D),
                vec_grad2[0:1],
            ]
        )
        owned[layer] = plan.scatter(buffer)
        vec_owned[layer] = plan.scatter_vectors(vector_grads)
    input_grad = swap(grad.astype(BF), n_dp).astype(F32)

    done = []
    for layer in reversed(range(LAYERS)):
        done = adam_call(plan, me, layer, owned[layer], params, param_moment, param_square, done)
    vector_grad = jnp.stack(vec_owned)
    vector_step = adam_parts(vector_grad, vector_moment, vector_square, vectors, 0.0)
    return (
        layer_output,
        input_grad,
        done[0],
        vector_grad,
        done[1],
        vector_step[0],
        done[2],
        vector_step[1],
        done[3],
        vector_step[2],
    )


def solution(mesh):
    tokens = P(("dp", "ctx"), None)
    slabs = P(None, "ctx", "dp", None)
    lines = P(None, ("dp", "ctx"))
    return jax.shard_map(
        functools.partial(per_device, mesh.shape["dp"]),
        mesh=mesh,
        in_specs=(tokens, tokens, slabs, lines, slabs, lines, slabs, lines),
        out_specs=(tokens, tokens, slabs, lines, slabs, lines, slabs, lines, slabs, lines),
        check_vma=False,
    )
```

time: 1930 us -> 1100 us (0.57)
  waiting for transfers between devices: 1080 us -> 109 us
  Pallas kernels: 0 us -> 831 us
  matrix products: 333 us -> 0 us
  local copies, waits for them, and re-layouts: 306 us -> 19.4 us
  other arithmetic: 112 us -> 8.14 us
  blocking collectives: 42 us -> 86 us
    pallas_call x0 -> x23, Pallas kernels: none -> 831 us  [the longest x2 342 us: scatter(): pl.pallas_call(kernel, out_shape=shape((self.size, LANES), F32), in_specs...]
    all_gather x16 -> x0, waiting for transfers between devices: 747 us -> none  [the longest x2 285 us: backward_layer(): lax.all_gather(active, 'ctx', axis=0, tiled=True)]
    dot_general x36 -> x0, matrix products: 333 us -> none  [the longest x2 78.1 us: backward_layer(): jnp.einsum('hts,thd->shd', grad_scores, query_heads, preferred_element_ty...]
    all_to_all x8 -> x0, waiting for transfers between devices: 144 us -> none  [the longest x2 66.2 us: backward_layer(): lax.all_to_all(upper_low, 'ctx', split_axis=1, concat_axis=0, tiled=True)]
    reduce_scatter x6 -> x0, waiting for transfers between devices: 141 us -> none  [the longest x2 129 us: backward_layer(): lax.psum_scatter(slab.astype(jnp.bfloat16), 'dp', scatter_dimension=0, ti...]
    unnamed x183 -> x59, local copies, waits for them, and re-layouts: 145 us -> 6.45 us
    ppermute x0 -> x38, waiting for transfers between devices: none -> 109 us  [the longest x24 92.4 us: trade(): result.append(lax.ppermute(arrays[r], ('dp', 'ctx'), pairs))]
    convert_element_type x11 -> x7, other arithmetic: 82.5 us -> 5.39 us  [the longest x2 2.38 us: per_device(): input_grad = swap(grad.astype(BF), n_dp).astype(F32)]
  transfers between devices with their start and end apart: 31 -> 38, of which waited for: 20 -> 18; matrix products, arithmetic and copies ran while one was open for 31% -> 2% of each run, Pallas kernels for 0% -> 67%
where the time goes in v1:
time: 1100 us; the launch traced here: 1090 us
  Pallas kernels  831 us (76%)
  waiting for transfers between devices  109 us (10%)
  blocking collectives  86 us (8%)
  starting transfers between devices  37.8 us (3%)
  local copies, waits for them, and re-layouts  19.4 us (2%)
    pallas_call x2, Pallas kernels, scatter(): pl.pallas_call(kernel, out_shape=shape((self.size, LANES), F32), in_specs...  342 us
    pallas_call x1, Pallas kernels, gather_all(): pl.pallas_call(kernel, out_shape=[shape((4, self.n_dp, self.size, LANES),...  235 us
    ppermute x24, waiting for transfers between devices, trade(): result.append(lax.ppermute(arrays[r], ('dp', 'ctx'), pairs))  92.4 us
    all_gather x1, blocking collectives, per_device(): lax.all_gather(vectors.astype(BF), ('dp', 'ctx'), axis=1, tiled=True)  86 us
    pallas_call x2, Pallas kernels, ff_back_call(): pl.pallas_call(functools.partial(ff_back_kernel, plan.pieces), out_shape=...  49.2 us
    pallas_call x2, Pallas kernels, ff_call(): pl.pallas_call(functools.partial(ff_kernel, plan.pieces), out_shape=[shap...  46.7 us
    pallas_call x2, Pallas kernels, ff_weight_call(): pl.pallas_call(functools.partial(ff_weight_kernel, plan.pieces), out_shap...  35.8 us
    pallas_call x2, Pallas kernels, attend_back_call(): pl.pallas_call(attend_back_kernel, out_shape=[shape((rows, 3 * WIDE), BF)...  32.6 us
  transfers between devices with their start and end apart: 38, of which 18 were waited for; matrix products, arithmetic and copies ran while one was open for 2% of the time, Pallas kernels for 67%

profile of v1, /device:TPU:0, one launch (start us, length us, event | category | flops | bytes accessed | tf_op | source)
XLA Modules:
  0.0 1093.2 jit_solution(11420857995954839559)
XLA Ops:
  3.0 86.0 %all_gather.3 = bf16[2,12288]{1,0:T(2,128)(2,1)S(1)} all-gather(bf16[2,384]{1,0:T(2,128)(2,1)S(1)} %convert_element_type.22), channel_id=1, replica_groups=mesh['dp'=8,'ctx'=4] {'dp','ctx'}, dimensions={1}, use_global_device_ids=true | all-gather | bytes 50688 | tf_op jit(solution)/shard_map/all_gather | solution.py:926
  99.5 234.9 %gather.1 = (bf16[4,8,3072,128]{3,2,1,0:T(8,128)(2,1)}, bf16[4,8,3072,128]{3,2,1,0:T(8,128)(2,1)}) custom-call(bf16[3072,128]{1,0:T(8,128)(2,1)} %prep.2.refs_0_, bf16[3072,128]{1,0:T(8,128)(2,1)} %prep.3.refs_1_), custom_call_target="tpu_custom_call" | custom-call | tf_op jit(solution)/shard_map/gather/pallas_call | solution.py:736
  344.6 10.6 collective-permute-done.2.in2
  362.7 10.6 attend.2
  382.1 23.3 %ff.2 = (bf16[256,1024]{1,0:T(8,128)(2,1)}, f32[256,1024]{1,0:T(8,128)}, bf16[256,1024]{1,0:T(8,128)(2,1)}, f32[16,256,256]{2,1,0:T(8,128)}, bf16[16,256,256]{2,1,0:T(8,128)(2,1)}, /*index=5*/f32[256,1024]{1,0:T(8,128)}) custom-call(s32[2]{0:T(128)} %pad_add_fusion.me, bf16[256,256]{1,0:T(8,128)(2,1)} %get-tuple-element.93.in0, bf16[256,256]{1,0:T(8,128)(2,1)} %copy-done.13, ...), custom_call_target="tpu_custom_call" | custom-call | tf_op jit(solution)/shard_map/ff/pallas_call | solution.py:282
  415.5 10.4 collective-permute-done.8.in2
  425.9 17.1 %collective-permute-done.9.in3 = bf16[256,768]{1,0:T(8,128)(2,1)S(1)} collective-permute-done((bf16[256,768]{1,0:T(8,128)(2,1)}, bf16[256,768]{1,0:T(8,128)(2,1)S(1)}, u32[]{:S(2)}, u32[]{:S(2)}) %collective-permute-start.9) | collective-permute-done | bytes 393248 | tf_op jit(solution)/shard_map/ppermute | solution.py:906
  443.8 10.6 attend.3
  463.4 23.4 %ff.3 = (bf16[256,1024]{1,0:T(8,128)(2,1)}, f32[256,1024]{1,0:T(8,128)}, bf16[256,1024]{1,0:T(8,128)(2,1)}, f32[16,256,256]{2,1,0:T(8,128)}, bf16[16,256,256]{2,1,0:T(8,128)(2,1)}, /*index=5*/f32[256,1024]{1,0:T(8,128)}) custom-call(s32[2]{0:T(128)} %pad_add_fusion.me, bf16[256,256]{1,0:T(8,128)(2,1)} %get-tuple-element.103.in0, ...), custom_call_target="tpu_custom_call" | custom-call | tf_op jit(solution)/shard_map/ff/pallas_call | solution.py:282
  486.8 24.7 %ff_back.2 = (bf16[256,1024]{1,0:T(8,128)(2,1)}, bf16[16,256,256]{2,1,0:T(8,128)(2,1)}, f32[256,1024]{1,0:T(8,128)}, bf16[256,1024]{1,0:T(8,128)(2,1)}, bf16[256...) custom-call(s32[2]{0:T(128)} %pad_add_fusion.me, ...), custom_call_target="tpu_custom_call" | custom-call | tf_op jit(solution)/shard_map/ff_back/pallas_call | solution.py:351
  520.4 16.4 %attend_back.2 = (bf16[256,768]{1,0:T(8,128)(2,1)}, bf16[256,768]{1,0:T(8,128)(2,1)}, bf16[256,768]{1,0:T(8,128)(2,1)}, bf16[256,768]{1,0:T(8,128)(2,1)}, f32[8,256]{1,0:T(8,128)}) custom-call(s32[2]{0:T(128)} %pad_add_fusion.me, bf16[256,768]{1,0:T(8,128)(2,1)} %get-tuple-element.99.in0, bf16[256,768]{1,0:T(8,128)(2,1)} %copy-done.3, ...), custom_call_target="tpu_custom_call" | custom-call | tf_op jit(solution)/shard_map/attend_back/pallas_call | solution.py:433
  540.6 9.0 collective-permute-done.19.in2
  557.2 10.6 qkv_back.2
  567.8 24.6 %ff_back.3 = (bf16[256,1024]{1,0:T(8,128)(2,1)}, bf16[16,256,256]{2,1,0:T(8,128)(2,1)}, f32[256,1024]{1,0:T(8,128)}, bf16[256,1024]{1,0:T(8,128)(2,1)}, bf16[256...) custom-call(s32[2]{0:T(128)} %pad_add_fusion.me, ...), custom_call_target="tpu_custom_call" | custom-call | tf_op jit(solution)/shard_map/ff_back/pallas_call | solution.py:351
  601.4 16.2 %attend_back.3 = (bf16[256,768]{1,0:T(8,128)(2,1)}, bf16[256,768]{1,0:T(8,128)(2,1)}, bf16[256,768]{1,0:T(8,128)(2,1)}, bf16[256,768]{1,0:T(8,128)(2,1)}, f32[8,256]{1,0:T(8,128)}) custom-call(s32[2]{0:T(128)} %pad_add_fusion.me, bf16[256,768]{1,0:T(8,128)(2,1)} %get-tuple-element.89.in0, bf16[256,768]{1,0:T(8,128)(2,1)} %copy-done, ...), custom_call_target="tpu_custom_call" | custom-call | tf_op jit(solution)/shard_map/attend_back/pallas_call | solution.py:433
  622.9 7.4 collective-permute-done.25.in2
  637.8 10.6 qkv_back.3
  665.3 16.9 %collective-permute-done.36 = f32[768]{0:T(1024)S(1)} collective-permute-done((f32[768]{0:T(1024)S(1)}, f32[768]{0:T(1024)S(1)}, u32[]{:S(2)}, u32[]{:S(2)}) %collective-permute-start.36) | collective-permute-done | bytes 3104 | tf_op jit(solution)/shard_map/ppermute | solution.py:619
  684.4 17.8 %ff_weight.3.before = bf16[4,8,3072,128]{3,2,1,0:T(8,128)(2,1)} custom-call(bf16[256,1024]{1,0:T(8,128)(2,1)} %get-tuple-element.144.attended, bf16[256,1024]{1,0:T(8,128)(2,1)} %get-tuple-element.145.normed, bf16[16,256,256]{2,1,0:T(8,128)(2,1)} %get-tuple-element.146.active, bf16[256,1024]{1,0:T(8,128)(2,1)} %get-tuple-element.147.dhb, ...), custom_call_target="tpu_custom_call" | custom-call | tf_op jit(solution)/shard_map/ff_weight/pallas_call | solution.py:514
  702.2 8.5 qkv_weight.3.grads
  710.8 170.5 %scatter.3.owned = f32[3072,128]{1,0:T(8,128)} custom-call(bf16[4,8,3072,128]{3,2,1,0:T(8,128)(2,1)} %qkv_weight.3.grads), custom_call_target="tpu_custom_call" | custom-call | tf_op jit(solution)/shard_map/scatter/pallas_call | solution.py:863
  887.0 18.0 %ff_weight.2.before = bf16[4,8,3072,128]{3,2,1,0:T(8,128)(2,1)} custom-call(bf16[256,1024]{1,0:T(8,128)(2,1)} %get-tuple-element.136.attended, bf16[256,1024]{1,0:T(8,128)(2,1)} %get-tuple-element.137.normed, bf16[16,256,256]{2,1,0:T(8,128)(2,1)} %get-tuple-element.138.active, bf16[256,1024]{1,0:T(8,128)(2,1)} %get-tuple-element.139.dhb, ...), custom_call_target="tpu_custom_call" | custom-call | tf_op jit(solution)/shard_map/ff_weight/pallas_call | solution.py:514
  905.1 8.5 qkv_weight.2.grads
  913.6 171.0 %scatter.2.owned = f32[3072,128]{1,0:T(8,128)} custom-call(bf16[4,8,3072,128]{3,2,1,0:T(8,128)(2,1)} %qkv_weight.2.grads), custom_call_target="tpu_custom_call" | custom-call | tf_op jit(solution)/shard_map/scatter/pallas_call | solution.py:863
  (197 shorter events, 134.2 us)
Async XLA Ops:
  0.6 333.8 %collective-permute-start = (bf16[256,1024]{1,0:T(8,128)(2,1)}, bf16[256,1024]{1,0:T(8,128)(2,1)S(1)}, u32[]{:S(2)}, u32[]{:S(2)}) collective-permute-start(bf16[256,1024]{1,0:T(8,128)(2,1)} %param.8), channel_id=1, source_target_pairs={{0,0},{1,4},{2,8},{3,12},{4,1},{5,5},{6,9},{7,13},{8,2},{9,6},{10,... | collective-permute-start | bytes 1572872 | tf_op jit(solution)/shard_map/ppermute | solution.py:899
  343.0 12.2 %collective-permute-start.2 = (bf16[256,768]{1,0:T(8,128)(2,1)}, bf16[256,768]{1,0:T(8,128)(2,1)S(1)}, u32[]{:S(2)}, u32[]{:S(2)}) collective-permute-start(bf16[256,768]{1,0:T(8,128)(2,1)} %get-tuple-element.91), channel_id=1, source_target_pairs={{0,8},{1,9},{2,10},{3,11},{4,12},{5,13},{6,14},{7,15},{8,0},{9,1},... | collective-permute-start | bytes 1179656 | tf_op jit(solution)/shard_map/ppermute | solution.py:906
  344.1 17.9 %collective-permute-start.3 = (bf16[256,768]{1,0:T(8,128)(2,1)}, bf16[256,768]{1,0:T(8,128)(2,1)S(1)}, u32[]{:S(2)}, u32[]{:S(2)}) collective-permute-start(bf16[256,768]{1,0:T(8,128)(2,1)} %get-tuple-element.92), channel_id=1, source_target_pairs={{0,12},{1,13},{2,14},{3,15},{4,8},{5,9},{6,10},{7,11},{8,4},{9,5},... | collective-permute-start | bytes 1179656 | tf_op jit(solution)/shard_map/ppermute | solution.py:906
  373.9 6.6 collective-permute-start.5
  375.0 6.4 collective-permute-start.6
  413.3 12.5 %collective-permute-start.8 = (bf16[256,768]{1,0:T(8,128)(2,1)}, bf16[256,768]{1,0:T(8,128)(2,1)S(1)}, u32[]{:S(2)}, u32[]{:S(2)}) collective-permute-start(bf16[256,768]{1,0:T(8,128)(2,1)} %get-tuple-element.101), channel_id=1, source_target_pairs={{0,8},{1,9},{2,10},{3,11},{4,12},{5,13},{6,14},{7,15},{8,0},{9,1},... | collective-permute-start | bytes 1179656 | tf_op jit(solution)/shard_map/ppermute | solution.py:906
  414.4 28.6 %collective-permute-start.9 = (bf16[256,768]{1,0:T(8,128)(2,1)}, bf16[256,768]{1,0:T(8,128)(2,1)S(1)}, u32[]{:S(2)}, u32[]{:S(2)}) collective-permute-start(bf16[256,768]{1,0:T(8,128)(2,1)} %get-tuple-element.102), channel_id=1, source_target_pairs={{0,12},{1,13},{2,14},{3,15},{4,8},{5,9},{6,10},{7,11},{8,4},{9,5},... | collective-permute-start | bytes 1179656 | tf_op jit(solution)/shard_map/ppermute | solution.py:906
  414.7 41.8 %collective-permute-start.14 = (bf16[256,1024]{1,0:T(8,128)(2,1)S(1)}, bf16[256,1024]{1,0:T(8,128)(2,1)S(1)}, u32[]{:S(2)}, u32[]{:S(2)}) collective-permute-start(bf16[256,1024]{1,0:T(8,128)(2,1)S(1)} %copy-done.28), channel_id=1, source_target_pairs={{0,0},{1,4},{2,8},{3,12},{4,1},{5,5},{6,9},{7,13},{8,2},{9,6},{10,... | collective-permute-start | bytes 1572872 | tf_op jit(solution)/shard_map/ppermute | solution.py:899
  454.4 6.7 collective-permute-start.11
  456.6 6.2 collective-permute-start.12
  511.9 6.5 collective-permute-start.16
  513.7 391.3 %collective-permute-start.13 = (bf16[256,1024]{1,0:T(8,128)(2,1)S(1)}, bf16[256,1024]{1,0:T(8,128)(2,1)S(1)}, u32[]{:S(2)}, u32[]{:S(2)}) collective-permute-start(bf16[256,1024]{1,0:T(8,128)(2,1)S(1)} %convert_element_type.24), channel_id=1, source_target_pairs={{0,0},{1,4},{2,8},{3,12},{4,1},{5,5},{6,9},{7,13},{8,2},{9,6},{10,... | collective-permute-start | bytes 1572872 | tf_op jit(solution)/shard_map/ppermute | solution.py:899
  537.4 12.2 %collective-permute-start.19 = (bf16[256,768]{1,0:T(8,128)(2,1)}, bf16[256,768]{1,0:T(8,128)(2,1)S(1)}, u32[]{:S(2)}, u32[]{:S(2)}) collective-permute-start(bf16[256,768]{1,0:T(8,128)(2,1)} %get-tuple-element.117), channel_id=1, source_target_pairs={{0,8},{1,9},{2,10},{3,11},{4,12},{5,13},{6,14},{7,15},{8,0},{9,1},... | collective-permute-start | bytes 1179656 | tf_op jit(solution)/shard_map/ppermute | solution.py:906
  539.0 17.4 %collective-permute-start.20 = (bf16[256,768]{1,0:T(8,128)(2,1)}, bf16[256,768]{1,0:T(8,128)(2,1)S(1)}, u32[]{:S(2)}, u32[]{:S(2)}) collective-permute-start(bf16[256,768]{1,0:T(8,128)(2,1)} %get-tuple-element.118), channel_id=1, source_target_pairs={{0,12},{1,13},{2,14},{3,15},{4,8},{5,9},{6,10},{7,11},{8,4},{9,5},... | collective-permute-start | bytes 1179656 | tf_op jit(solution)/shard_map/ppermute | solution.py:906
  592.9 6.5 collective-permute-start.22
  595.6 26.5 %collective-permute-start.33 = (f32[6144]{0:T(1024)S(1)}, f32[6144]{0:T(1024)S(1)}, u32[]{:S(2)}, u32[]{:S(2)}) collective-permute-start(f32[6144]{0:T(1024)S(1)} %bitcast.22), channel_id=1, source_target_pairs={{0,16},{1,17},{2,18},{3,19},{4,20},{5,21},{6,22},{7,23},{8,24},{9,... | collective-permute-start | bytes 73736 | tf_op jit(solution)/shard_map/ppermute | solution.py:619
  618.1 12.2 %collective-permute-start.25 = (bf16[256,768]{1,0:T(8,128)(2,1)}, bf16[256,768]{1,0:T(8,128)(2,1)S(1)}, u32[]{:S(2)}, u32[]{:S(2)}) collective-permute-start(bf16[256,768]{1,0:T(8,128)(2,1)} %get-tuple-element.130), channel_id=1, source_target_pairs={{0,8},{1,9},{2,10},{3,11},{4,12},{5,13},{6,14},{7,15},{8,0},{9,1},... | collective-permute-start | bytes 1179656 | tf_op jit(solution)/shard_map/ppermute | solution.py:906
  619.8 17.4 %collective-permute-start.26 = (bf16[256,768]{1,0:T(8,128)(2,1)}, bf16[256,768]{1,0:T(8,128)(2,1)S(1)}, u32[]{:S(2)}, u32[]{:S(2)}) collective-permute-start(bf16[256,768]{1,0:T(8,128)(2,1)} %get-tuple-element.131), channel_id=1, source_target_pairs={{0,12},{1,13},{2,14},{3,15},{4,8},{5,9},{6,10},{7,11},{8,4},{9,5},... | collective-permute-start | bytes 1179656 | tf_op jit(solution)/shard_map/ppermute | solution.py:906
  650.9 6.9 collective-permute-start.34
  653.7 437.4 %collective-permute-start.27 = (bf16[256,1024]{1,0:T(8,128)(2,1)S(1)}, bf16[256,1024]{1,0:T(8,128)(2,1)S(1)}, u32[]{:S(2)}, u32[]{:S(2)}) collective-permute-start(bf16[256,1024]{1,0:T(8,128)(2,1)S(1)} %convert_element_type.26), channel_id=1, source_target_pairs={{0,0},{1,4},{2,8},{3,12},{4,1},{5,5},{6,9},{7,13},{8,2},{9,6},{10,... | collective-permute-start | bytes 1572872 | tf_op jit(solution)/shard_map/ppermute | solution.py:899
  662.2 20.0 %collective-permute-start.36 = (f32[768]{0:T(1024)S(1)}, f32[768]{0:T(1024)S(1)}, u32[]{:S(2)}, u32[]{:S(2)}) collective-permute-start(f32[768]{0:T(1024)S(1)} %get-tuple-element.174), channel_id=1, source_target_pairs={{0,2},{1,3},{2,0},{3,1},{4,6},{5,7},{6,4},{7,5},{8,10},{9,11},{10,... | collective-permute-start | bytes 9224 | tf_op jit(solution)/shard_map/ppermute | solution.py:619
  664.2 18.1 %collective-permute-start.31 = (f32[768]{0:T(1024)S(1)}, f32[768]{0:T(1024)S(1)}, u32[]{:S(2)}, u32[]{:S(2)}) collective-permute-start(f32[768]{0:T(1024)S(1)} %get-tuple-element.172), channel_id=1, source_target_pairs={{0,2},{1,3},{2,0},{3,1},{4,6},{5,7},{6,4},{7,5},{8,10},{9,11},{10,... | collective-permute-start | bytes 9224 | tf_op jit(solution)/shard_map/ppermute | solution.py:619
  682.2 222.8 %collective-permute-start.37 = (f32[384]{0:T(512)S(1)}, f32[384]{0:T(512)S(1)}, u32[]{:S(2)}, u32[]{:S(2)}) collective-permute-start(f32[384]{0:T(512)S(1)} %get-tuple-element.178), channel_id=1, source_target_pairs={{0,1},{1,0},{2,3},{3,2},{4,5},{5,4},{6,7},{7,6},{8,9},{9,8},{10,11... | collective-permute-start | bytes 4616 | tf_op jit(solution)/shard_map/ppermute | solution.py:619
  682.4 408.1 %collective-permute-start.32 = (f32[384]{0:T(512)S(1)}, f32[384]{0:T(512)S(1)}, u32[]{:S(2)}, u32[]{:S(2)}) collective-permute-start(f32[384]{0:T(512)S(1)} %get-tuple-element.176), channel_id=1, source_target_pairs={{0,1},{1,0},{2,3},{3,2},{4,5},{5,4},{6,7},{7,6},{8,9},{9,8},{10,11... | collective-permute-start | bytes 4616 | tf_op jit(solution)/shard_map/ppermute | solution.py:619
  (43 other events, 255.1 us)

commit v2 on v1

v2 whole, which is shorter than its diff:
```python
import functools

import jax
import jax.numpy as jnp
from jax import lax
from jax.experimental import pallas as pl
from jax.experimental.pallas import tpu as pltpu
from jax.sharding import PartitionSpec as P

D = 1024
HEADS = 16
HEAD = 64
FF = 4096
LAYERS = 2
STEP = 10
BF = jnp.bfloat16
F32 = jnp.float32
LANES = 128
GROUP = 4
WIDE = D // GROUP
CHUNKS = FF // WIDE

norm_eps = 1e-05
beta_one = 0.9
beta_two = 0.999
rate = 0.01
decay = 0.1
adam_eps = 1e-08
gelu_c = 0.7978845608028654
gelu_a = 0.044715

VMEM_LIMIT = 60 * 1024 * 1024

ROWS = (D, D, D, FF)
PANELS = (3 * D // 4 // LANES, D // 4 // LANES, FF // 4 // LANES, D // 4 // LANES)


def pieces_of(count):
    size = sum(r * p for r, p in zip(ROWS, PANELS)) // count
    result = []
    for d in range(count):
        low, high = d * size, (d + 1) * size
        held, start = [], 0
        for mat in range(4):
            end = start + ROWS[mat] * PANELS[mat]
            a, b = max(low, start), min(high, end)
            if a < b:
                held.append((mat, (a - start) // PANELS[mat], (b - start) // PANELS[mat], a - low))
            start = end
        result.append(held)
    return size, result


TURN = (0, 2, 1, 3)


def place_of(d):
    return (d & 1) * 2 + (d >> 1) % 2


def params_of(**extra):
    return pltpu.CompilerParams(vmem_limit_bytes=VMEM_LIMIT, **extra)


MESH = pl.DeviceIdType.MESH
ANY = pl.BlockSpec(memory_space=pl.ANY)
VM = pl.BlockSpec(memory_space=pltpu.VMEM)
SM = pl.BlockSpec(memory_space=pltpu.SMEM)


def shape(dims, dtype):
    return jax.ShapeDtypeStruct(dims, dtype)


def nt(a, b):
    return lax.dot_general(a, b, (((1,), (1,)), ((), ())), preferred_element_type=F32)


def tn(a, b):
    return lax.dot_general(a, b, (((0,), (0,)), ((), ())), preferred_element_type=F32)


def nn(a, b):
    return jnp.dot(a, b, preferred_element_type=F32)


def norm_parts(values):
    center = values - jnp.mean(values, axis=-1, keepdims=True)
    spread = jnp.mean(center * center, axis=-1, keepdims=True)
    scale = lax.rsqrt(spread + norm_eps)
    return center * scale, scale


def norm_back(values, gain, grad):
    hat, scale = norm_parts(values)
    dhat = grad * gain
    back = scale * (
        dhat
        - jnp.mean(dhat, axis=-1, keepdims=True)
        - hat * jnp.mean(dhat * hat, axis=-1, keepdims=True)
    )
    return back, jnp.sum(grad * hat, axis=0, keepdims=True), jnp.sum(grad, axis=0, keepdims=True)


def load_matrix(whole, target, mat, pieces, sem, split=False):
    for c in range(4):
        for d, held in enumerate(pieces):
            for m, k0, k1, base in held:
                if m != mat:
                    continue
                for j in range(PANELS[mat]):
                    panel, k = c * PANELS[mat] + j, k0
                    while k < k1:
                        n = min(k1 - k, D - k % D) if split else k1 - k
                        at = (panel * 4 + k // D, pl.ds(k % D, n)) if split else (panel, pl.ds(k, n))
                        pltpu.make_async_copy(
                            whole.at[c, d, pl.ds(base + j * (k1 - k0) + k - k0, n)], target.at[at], sem
                        ).start()
                        k += n


def wait_all(ref, sem):
    pltpu.make_async_copy(ref, ref, sem).wait()


def prep_kernel(plan, me, slabs, lines, *outs):
    for layer, out in enumerate(outs):
        out[plan.size :, :] = jnp.zeros((plan.span - plan.size, LANES), BF)
        for r in range(lines.shape[1] // LANES):
            at = plan.size + r
            out[at : at + 1, :] = lines[layer : layer + 1, r * LANES : (r + 1) * LANES].astype(BF)
    for d, held in enumerate(plan.pieces):

        @pl.when(me[0] == d)
        def _(held=held):
            for layer, out in enumerate(outs):
                for mat, k0, k1, base in held:
                    count, step = k1 - k0, PANELS[mat]
                    for j in range(step):
                        rows = slabs[layer, 0, pl.ds(base + j, count, stride=step), :]
                        out[pl.ds(base + j * count, count), :] = rows.astype(BF)


def prepare(plan, me, slabs, lines):
    lines = jnp.pad(lines, ((0, 0), (0, -lines.shape[1] % LANES)))
    return pl.pallas_call(
        functools.partial(prep_kernel, plan),
        out_shape=[shape((plan.span, LANES), BF)] * LAYERS,
        in_specs=[SM, VM, VM],
        out_specs=[VM] * LAYERS,
        compiler_params=params_of(),
        name="prep",
    )(me, slabs, lines)


def qkv_kernel(pieces, me, x, vec, whole, normed, out0, out1, out2, out3, weight, qkv, sem):
    load_matrix(whole, weight, 0, pieces, sem)
    hat, _ = norm_parts(x[...].astype(F32))
    normed[...] = (hat * vec[0:1, :] + vec[1:2, :]).astype(BF)
    wait_all(weight, sem)
    for b in range(3 * GROUP):
        kind, at = b // GROUP, b % GROUP
        acc = nn(normed[...], jnp.concatenate([weight[2 * b], weight[2 * b + 1]], axis=1))
        if kind != 1:
            row = 2 if kind == 0 else 3
            acc = acc + vec[row : row + 1, at * WIDE : (at + 1) * WIDE]
        qkv[b] = acc.astype(BF)
    mine = place_of(me[0])
    for r, out in enumerate((out0, out1, out2, out3)):
        for kind in range(3):
            out[:, kind * WIDE : (kind + 1) * WIDE] = qkv[kind * GROUP + (mine ^ TURN[r])]


def qkv_call(plan, me, x, vec, whole):
    rows = x.shape[0]
    return pl.pallas_call(
        functools.partial(qkv_kernel, plan.pieces),
        out_shape=[shape((rows, D), BF)] + [shape((rows, 3 * WIDE), BF)] * GROUP,
        in_specs=[SM, VM, VM, ANY],
        out_specs=[VM] * 5,
        scratch_shapes=[
            pltpu.VMEM((3 * D // LANES, D, LANES), BF),
            pltpu.VMEM((3 * GROUP, rows, WIDE), BF),
            pltpu.SemaphoreType.DMA,
        ],
        compiler_params=params_of(),
        name="qkv",
    )(me, x, vec, whole)


def diagonal(rows):
    return lax.broadcasted_iota(jnp.int32, (rows, rows), 1) <= lax.broadcasted_iota(jnp.int32, (rows, rows), 0)


def attend_kernel(me, in0, in1, in2, in3, out0, out1, out2, out3, lse, q, k, v, o):
    mine = place_of(me[0])
    rows = in0.shape[0]
    for r, ref in enumerate((in0, in1, in2, in3)):
        at = pl.ds(pl.multiple_of((mine ^ TURN[r]) * rows, rows), rows)
        q[at, :] = ref[:, 0:WIDE]
        k[at, :] = ref[:, WIDE : 2 * WIDE]
        v[at, :] = ref[:, 2 * WIDE : 3 * WIDE]
    seen = diagonal(rows)
    for h in range(WIDE // HEAD):
        cols = slice(h * HEAD, (h + 1) * HEAD)
        for i in range(GROUP):
            here = slice(i * rows, (i + 1) * rows)
            qi = q[here, cols]
            near = jnp.where(seen, nt(qi, k[here, cols]) * 0.125, -1000000000.0)
            top = jnp.max(near, axis=1, keepdims=True)
            if i:
                far = nt(qi, k[0 : i * rows, cols]) * 0.125
                top = jnp.maximum(top, jnp.max(far, axis=1, keepdims=True))
                far = jnp.exp(far - top)
            near = jnp.exp(near - top)
            total = jnp.sum(near, axis=1, keepdims=True)
            if i:
                total = total + jnp.sum(far, axis=1, keepdims=True)
            inv = 1.0 / total
            res = nn((near * inv).astype(BF), v[here, cols])
            if i:
                res = res + nn((far * inv).astype(BF), v[0 : i * rows, cols])
            o[i, :, cols] = res.astype(BF)
            lse[here, h : h + 1] = top + jnp.log(total)
    for r, out in enumerate((out0, out1, out2, out3)):
        out[...] = o[mine ^ TURN[r]]


def attend_call(me, heads):
    rows = heads[0].shape[0]
    span = GROUP * rows
    return pl.pallas_call(
        attend_kernel,
        out_shape=[shape((rows, WIDE), BF)] * GROUP + [shape((span, LANES), F32)],
        in_specs=[SM] + [VM] * GROUP,
        out_specs=[VM] * 5,
        scratch_shapes=[pltpu.VMEM((span, WIDE), BF)] * 3 + [pltpu.VMEM((GROUP, rows, WIDE), BF)],
        compiler_params=params_of(),
        name="attend",
    )(me, *heads)


def side(ref, at, count=2):
    return jnp.concatenate([ref[at + i] for i in range(count)], axis=1)


def rows_of(ref, at):
    return jnp.concatenate([ref[p, at, :] for p in range(D // LANES)], axis=1)


def ff_kernel(
    pieces, me, in0, in1, in2, in3, x, vec, bias, whole,
    attended, hidden, normed, upper, active, out,
    wo, we, wr, parts, sems,
):
    load_matrix(whole, wo, 1, pieces, sems.at[0])
    load_matrix(whole, we, 2, pieces, sems.at[1])
    load_matrix(whole, wr, 3, pieces, sems.at[2])
    mine = place_of(me[0])
    for r, ref in enumerate((in0, in1, in2, in3)):
        parts[mine ^ TURN[r]] = ref[...]
    for g in range(GROUP):
        attended[:, g * WIDE : (g + 1) * WIDE] = parts[g]
    wait_all(wo, sems.at[0])
    for g in range(GROUP):
        cols = slice(g * WIDE, (g + 1) * WIDE)
        hidden[:, cols] = x[:, cols] + nn(attended[...], side(wo, 2 * g)) + vec[4:5, cols]
    hat, _ = norm_parts(hidden[...])
    normed[...] = (hat * vec[5:6, :] + vec[6:7, :]).astype(BF)
    out[...] = hidden[...] + vec[11:12, :]
    wait_all(we, sems.at[1])
    wait_all(wr, sems.at[2])

    def body(n, _):
        u = nn(normed[...], side(we, 2 * n)) + bias[n]
        upper[n] = u
        act = (0.5 * u * (1.0 + jnp.tanh(gelu_c * (u + gelu_a * u * u * u)))).astype(BF)
        active[n] = act
        out[...] += nn(act, rows_of(wr, pl.ds(pl.multiple_of(n * WIDE, WIDE), WIDE)))
        return 0

    lax.fori_loop(0, CHUNKS, body, 0)


def ff_call(plan, me, heads, x, vec, bias, whole):
    rows = x.shape[0]
    return pl.pallas_call(
        functools.partial(ff_kernel, plan.pieces),
        out_shape=[
            shape((rows, D), BF),
            shape((rows, D), F32),
            shape((rows, D), BF),
            shape((CHUNKS, rows, WIDE), F32),
            shape((CHUNKS, rows, WIDE), BF),
            shape((rows, D), F32),
        ],
        in_specs=[SM] + [VM] * 7 + [ANY],
        out_specs=[VM] * 6,
        scratch_shapes=[
            pltpu.VMEM((D // LANES, D, LANES), BF),
            pltpu.VMEM((FF // LANES, D, LANES), BF),
            pltpu.VMEM((D // LANES, FF, LANES), BF),
            pltpu.VMEM((GROUP, rows, WIDE), BF),
            pltpu.SemaphoreType.DMA((3,)),
        ],
        compiler_params=params_of(),
        name="ff",
    )(me, *heads, x, vec, bias, whole)


def ff_back_kernel(
    pieces, me, dy, upper, hidden, vec, whole,
    dyb, dub, dh, dhb, out0, out1, out2, out3, bias_grad, vec_grad,
    wo, we, wr, acc, parts, sems,
):
    load_matrix(whole, wr, 3, pieces, sems.at[2])
    load_matrix(whole, we, 2, pieces, sems.at[1])
    load_matrix(whole, wo, 1, pieces, sems.at[0])
    dyb[...] = dy[...].astype(BF)
    vec_grad[0:1, :] = jnp.sum(dy[...], axis=0, keepdims=True)
    acc[...] = jnp.zeros_like(acc)
    wait_all(wr, sems.at[2])
    wait_all(we, sems.at[1])

    def body(n, _):
        dg = nt(dyb[...], rows_of(wr, pl.ds(pl.multiple_of(n * WIDE, WIDE), WIDE)))
        u = upper[n]
        t = jnp.tanh(gelu_c * (u + gelu_a * u * u * u))
        slope = 0.5 * (1.0 + t) + 0.5 * u * (1.0 - t * t) * (gelu_c * (1.0 + 3.0 * gelu_a * u * u))
        du = dg * slope
        bias_grad[n] = jnp.sum(du, axis=0, keepdims=True)
        low = du.astype(BF)
        dub[n] = low
        acc[...] += nt(low, side(we, 2 * n))
        return 0

    lax.fori_loop(0, CHUNKS, body, 0)
    back, gain, shift = norm_back(hidden[...], vec[5:6, :], acc[...])
    total = dy[...] + back
    vec_grad[1:2, :] = gain
    vec_grad[2:3, :] = shift
    vec_grad[3:4, :] = jnp.sum(total, axis=0, keepdims=True)
    vec_grad[4:8, :] = jnp.zeros((4, D), F32)
    dh[...] = total
    dhb[...] = total.astype(BF)
    wait_all(wo, sems.at[0])
    for g in range(GROUP):
        parts[g] = nt(dhb[...], rows_of(wo, slice(g * WIDE, (g + 1) * WIDE))).astype(BF)
    mine = place_of(me[0])
    for r, out in enumerate((out0, out1, out2, out3)):
        out[...] = parts[mine ^ TURN[r]]


def ff_back_call(plan, me, dy, upper, hidden, vec, whole):
    rows = dy.shape[0]
    return pl.pallas_call(
        functools.partial(ff_back_kernel, plan.pieces),
        out_shape=[
            shape((rows, D), BF),
            shape((CHUNKS, rows, WIDE), BF),
            shape((rows, D), F32),
            shape((rows, D), BF),
        ]
        + [shape((rows, WIDE), BF)] * GROUP
        + [shape((CHUNKS, 1, WIDE), F32), shape((8, D), F32)],
        in_specs=[SM] + [VM] * 4 + [ANY],
        out_specs=[VM] * 10,
        scratch_shapes=[
            pltpu.VMEM((D // LANES, D, LANES), BF),
            pltpu.VMEM((FF // LANES, D, LANES), BF),
            pltpu.VMEM((D // LANES, FF, LANES), BF),
            pltpu.VMEM((rows, D), F32),
            pltpu.VMEM((GROUP, rows, WIDE), BF),
            pltpu.SemaphoreType.DMA((3,)),
        ],
        compiler_params=params_of(),
        name="ff_back",
    )(me, dy, upper, hidden, vec, whole)


def attend_back_kernel(
    me, in0, in1, in2, in3, do0, do1, do2, do3, lse,
    out0, out1, out2, out3, sums,
    q, k, v, do, dq, dk, dv,
):
    mine = place_of(me[0])
    rows = in0.shape[0]
    for r, (ref, grad) in enumerate(((in0, do0), (in1, do1), (in2, do2), (in3, do3))):
        at = pl.ds(pl.multiple_of((mine ^ TURN[r]) * rows, rows), rows)
        q[at, :] = ref[:, 0:WIDE]
        k[at, :] = ref[:, WIDE : 2 * WIDE]
        v[at, :] = ref[:, 2 * WIDE : 3 * WIDE]
        do[at, :] = grad[...]
    seen = diagonal(rows)
    for h in range(WIDE // HEAD):
        cols = slice(h * HEAD, (h + 1) * HEAD)
        total = jnp.zeros((1, HEAD), F32)
        for i in reversed(range(GROUP)):
            here = slice(i * rows, (i + 1) * rows)
            past = slice(0, i * rows)
            qi, doi, ls = q[here, cols], do[here, cols], lse[here, h : h + 1]
            near = jnp.exp(jnp.where(seen, nt(qi, k[here, cols]) * 0.125, -1000000000.0) - ls)
            dnear = nt(doi, v[here, cols])
            inner = jnp.sum(near * dnear, axis=1, keepdims=True)
            if i:
                far = jnp.exp(nt(qi, k[past, cols]) * 0.125 - ls)
                dfar = nt(doi, v[past, cols])
                inner = inner + jnp.sum(far * dfar, axis=1, keepdims=True)
            snear = (near * (dnear - inner) * 0.125).astype(BF)
            res = nn(snear, k[here, cols])
            dkn = tn(snear, qi)
            dvn = tn(near.astype(BF), doi)
            last = i == GROUP - 1
            dk[here, cols] = dkn if last else dk[here, cols] + dkn
            dv[here, cols] = dvn if last else dv[here, cols] + dvn
            if i:
                sfar = (far * (dfar - inner) * 0.125).astype(BF)
                res = res + nn(sfar, k[past, cols])
                dkf = tn(sfar, qi)
                dvf = tn(far.astype(BF), doi)
                dk[past, cols] = dkf if last else dk[past, cols] + dkf
                dv[past, cols] = dvf if last else dv[past, cols] + dvf
            total = total + jnp.sum(res, axis=0, keepdims=True)
            dq[i, :, cols] = res.astype(BF)
        sums[0:1, cols] = total
    sums[1:2, :] = jnp.sum(dv[...], axis=0, keepdims=True)
    sums[2:8, :] = jnp.zeros((6, WIDE), F32)
    for r, out in enumerate((out0, out1, out2, out3)):
        at = pl.ds(pl.multiple_of((mine ^ TURN[r]) * rows, rows), rows)
        out[:, 0:WIDE] = dq[mine ^ TURN[r]]
        out[:, WIDE : 2 * WIDE] = dk[at, :].astype(BF)
        out[:, 2 * WIDE : 3 * WIDE] = dv[at, :].astype(BF)


def attend_back_call(me, heads, grads, lse):
    rows = heads[0].shape[0]
    span = GROUP * rows
    return pl.pallas_call(
        attend_back_kernel,
        out_shape=[shape((rows, 3 * WIDE), BF)] * GROUP + [shape((8, WIDE), F32)],
        in_specs=[SM] + [VM] * 9,
        out_specs=[VM] * 5,
        scratch_shapes=[pltpu.VMEM((span, WIDE), BF)] * 4
        + [pltpu.VMEM((GROUP, rows, WIDE), BF)]
        + [pltpu.VMEM((span, WIDE), F32)] * 2,
        compiler_params=params_of(),
        name="attend_back",
    )(me, *heads, *grads, lse)


def qkv_back_kernel(pieces, me, in0, in1, in2, in3, dh, x, vec, whole, mixed, dx, vec_grad, weight, acc, sem):
    load_matrix(whole, weight, 0, pieces, sem)
    mine = place_of(me[0])
    for r, ref in enumerate((in0, in1, in2, in3)):
        mixed[mine ^ TURN[r]] = ref[...]
    acc[...] = jnp.zeros_like(acc)
    wait_all(weight, sem)

    for b in range(3 * GROUP):
        kind, at = b // GROUP, b % GROUP
        acc[...] += nt(mixed[at, :, kind * WIDE : (kind + 1) * WIDE], side(weight, 2 * b))
    back, gain, shift = norm_back(x[...].astype(F32), vec[0:1, :], acc[...])
    dx[...] = dh[...] + back
    vec_grad[0:1, :] = gain
    vec_grad[1:2, :] = shift
    vec_grad[2:8, :] = jnp.zeros((6, D), F32)


def qkv_back_call(plan, me, grads, dh, x, vec, whole):
    rows = x.shape[0]
    return pl.pallas_call(
        functools.partial(qkv_back_kernel, plan.pieces),
        out_shape=[shape((GROUP, rows, 3 * WIDE), BF), shape((rows, D), F32), shape((8, D), F32)],
        in_specs=[SM] + [VM] * 7 + [ANY],
        out_specs=[VM] * 3,
        scratch_shapes=[
            pltpu.VMEM((3 * D // LANES, D, LANES), BF),
            pltpu.VMEM((rows, D), F32),
            pltpu.SemaphoreType.DMA,
        ],
        compiler_params=params_of(),
        name="qkv_back",
    )(me, *grads, dh, x, vec, whole)


def weight_items(pieces, core):
    items = []
    for d in range(core, len(pieces), 2):
        for mat, k0, k1, base in pieces[d]:
            count, step = k1 - k0, PANELS[mat]
            k = k0
            while k < k1:
                n = min(WIDE - k % WIDE, k1 - k) if mat == 3 else k1 - k0
                if step == 2:
                    groups = [range(j, 4 * step, step) for j in range(step)]
                else:
                    groups = [range(2 * i, 2 * i + 2) for i in range(2 * step)]
                for group in groups:
                    low = base + group[0] % step * count + k - k0
                    items.append((low, d, mat, base - k0, count, k, n, group))
                k += n
    return items


def weight_part(items, own, other, out):
    normed1, attended, normed2, active, mixed, dhb, dub, dyb = zip(own, other)
    everything = slice(None)

    def both(pair, *at):
        return jnp.concatenate([ref[at] for ref in pair], axis=0)

    def panels(pair, group):
        return jnp.concatenate([both(pair, everything, slice(p * LANES, (p + 1) * LANES)) for p in group], axis=1)

    turned = {}
    for _, d, mat, base, count, k, n, group in items:
        if (d, mat, k) not in turned:
            if mat == 3:
                lhs = both(active, k // WIDE, everything, slice(k % WIDE, k % WIDE + n))
            else:
                lhs = both((normed1, attended, normed2)[mat], everything, slice(k, k + n))
            turned[d, mat, k] = lhs.T
        if mat == 0:
            at = group[0] // 2
            rhs = both(mixed, at % GROUP, everything, slice(at // GROUP * WIDE, (at // GROUP + 1) * WIDE))
        elif mat == 2:
            rhs = both(dub, group[0] // 2)
        else:
            rhs = panels(dhb if mat == 1 else dyb, group)
        res = nn(turned[d, mat, k], rhs).astype(BF)
        step = PANELS[mat]
        for i, p in enumerate(group):
            at = base + k + (p % step) * count
            out[p // step, d // 2, at : at + n, :] = res[:, i * LANES : (i + 1) * LANES]


def weight_kernel(pieces, me, *refs):
    for core in range(2):

        @pl.when(me[0] % 2 == core)
        def _(core=core):
            weight_part(weight_items(pieces, core), refs[:8], refs[8:16], refs[16])


def weight_call(plan, me, own, other):
    return pl.pallas_call(
        functools.partial(weight_kernel, plan.pieces),
        out_shape=shape((4, plan.n_dp // 2, plan.size, LANES), BF),
        in_specs=[SM] + [VM] * 16,
        out_specs=VM,
        compiler_params=params_of(),
        name="weight_grads",
    )(me, *own, *other)


def adam_parts(grad, moment, square, master, weight_decay):
    moment_next = beta_one * moment + (1.0 - beta_one) * grad
    square_next = beta_two * square + (1.0 - beta_two) * grad * grad
    corrected = moment_next / (1.0 - beta_one**STEP)
    scaled = square_next / (1.0 - beta_two**STEP)
    update = -rate * (corrected / (jnp.sqrt(scaled) + adam_eps) + weight_decay * master)
    return moment_next, square_next, update


def adam_kernel(plan, me, owned, master, moment, square, *refs):
    grad, moment_next, square_next, update = refs[-4:]
    for d, held in enumerate(plan.pieces):

        @pl.when(me[0] == d)
        def _(held=held):
            for mat, k0, k1, base in held:
                size, step = k1 - k0, PANELS[mat]
                for j in range(step):
                    grad[0, 0, pl.ds(base + j, size, stride=step), :] = owned[pl.ds(base + j * size, size), :]

    new = adam_parts(grad[0, 0], moment[0, 0], square[0, 0], master[0, 0], decay)
    moment_next[0, 0], square_next[0, 0], update[0, 0] = new


def adam_call(plan, me, layer, owned, master, moment, square, before):
    block = pl.BlockSpec((1, 1) + master.shape[2:], lambda i: (layer, 0, 0, 0))
    whole = pl.BlockSpec(owned.shape, lambda i: (0, 0))
    first = 5
    return pl.pallas_call(
        functools.partial(adam_kernel, plan),
        grid=(1,),
        out_shape=[shape(master.shape, F32)] * 4,
        in_specs=[SM, whole] + [block] * 3 + [ANY] * len(before),
        out_specs=[block] * 4,
        input_output_aliases={first + i: i for i in range(len(before))},
        compiler_params=params_of(),
        name="adam",
    )(me, owned, master, moment, square, *before)


class Wire:
    def __init__(self, send, recv):
        self.d, self.z = lax.axis_index("dp"), lax.axis_index("ctx")
        self.place = place_of(self.d)
        self.send, self.recv, self.next = send, recv, 0

    def copy(self, src, dst, d, z, at=None):
        slot = self.next
        self.next += 1
        return pltpu.make_async_remote_copy(
            src_ref=src, dst_ref=dst, send_sem=self.send.at[slot], recv_sem=self.recv.at[slot],
            device_id=(d, z), device_id_type=MESH,
        )

    def push(self, src, dst, flip_dp, flip_ctx):
        copy = self.copy(src, dst, self.d ^ flip_dp, self.z ^ flip_ctx)
        copy.start()
        return copy

    def greet(self, flips, swaps=False):
        barrier = pltpu.get_barrier_semaphore()
        for fd, fz in flips:
            pl.semaphore_signal(barrier, inc=1, device_id=(self.d ^ fd, self.z ^ fz), device_id_type=MESH)
        if not swaps:
            pl.semaphore_wait(barrier, len(flips))
            return

        @pl.when(self.place != self.z)
        def _():
            pl.semaphore_signal(barrier, inc=1, device_id=self.opposite(), device_id_type=MESH)
            pl.semaphore_wait(barrier, len(flips) + 1)

        @pl.when(self.place == self.z)
        def _():
            pl.semaphore_wait(barrier, len(flips))

    def opposite(self):
        return (self.d - self.d % GROUP + place_of(self.z), self.place)

    def swap(self, src, dst):
        copy = self.copy(src, dst, *self.opposite())

        @pl.when(self.place != self.z)
        def _():
            copy.start()

        @pl.when(self.place == self.z)
        def _():
            dst[...] = src[...]

        def finish():
            @pl.when(self.place != self.z)
            def _():
                copy.wait()

        return finish

    def post(self, blocks, into):
        base = self.next
        self.next += GROUP
        first = self.d - self.d % GROUP

        def copy(g, sender):
            return pltpu.make_async_remote_copy(
                src_ref=blocks.at[g], dst_ref=into.at[self.place],
                send_sem=self.send.at[base + g], recv_sem=self.recv.at[base + sender],
                device_id=(first + place_of(g), self.z), device_id_type=MESH,
            )

        def send(g):
            @pl.when(self.place != g)
            def _():
                copy(g, self.place).start()

            @pl.when(self.place == g)
            def _():
                into[g] = blocks[g]

        def finish():
            for r in range(1, GROUP):
                copy(0, self.place ^ r).wait_recv()
            for g in range(GROUP):

                @pl.when(self.place != g)
                def _(g=g):
                    copy(g, self.place).wait_send()

        return send, finish

    def trade(self, blocks, into):
        copies = []
        for r in (2, 3, 1):
            copies.append(self.push(blocks.at[self.place ^ TURN[r]], into.at[self.place], r, 0))
        into[self.place] = blocks[self.place]
        return copies


def drive(jobs, late):
    live = list(zip(jobs, late))
    step = 0
    while live:
        rest = []
        for job, wait in live:
            if step >= wait:
                try:
                    next(job)
                except StopIteration:
                    continue
                yield
            rest.append((job, wait))
        live = rest
        step += 1


def take(steps, count=1):
    for _ in range(count):
        next(steps, None)


def paced(steps, pace):
    owed = [0.0]

    def advance():
        owed[0] += pace
        while owed[0] >= 1.0:
            owed[0] -= 1.0
            next(steps, None)

    return advance


def unpack_vectors(raw, vec, n_dp, size):
    share = 12 * D // (4 * n_dp) // LANES
    per_row = D // LANES
    for d in range(n_dp):
        for z in range(4):
            lines = raw[z, d].astype(F32)
            for r in range(share):
                at = (d * 4 + z) * share + r
                col = at % per_row * LANES
                vec[at // per_row : at // per_row + 1, col : col + LANES] = lines[r : r + 1, :]


def qkv_part(wire, normed, weight, vec, blocks, heads, copies):
    for r in (2, 3, 1, 0):
        at = wire.place ^ TURN[r]
        cols = pl.ds(pl.multiple_of(at * WIDE, WIDE), WIDE)
        for kind in range(3):
            acc = nn(normed[...], side(weight, 2 * (kind * GROUP + at)))
            if kind != 1:
                row = 2 if kind == 0 else 3
                acc = acc + vec[row : row + 1, cols]
            blocks[at, :, kind * WIDE : (kind + 1) * WIDE] = acc.astype(BF)
            yield
        if r:
            copies.append(wire.push(blocks.at[at], heads.at[wire.place], r, 0))
        else:
            heads[at] = blocks[at]


def spread_heads(heads, q, k, v):
    rows = heads.shape[1]
    for g in range(GROUP):
        at = slice(g * rows, (g + 1) * rows)
        q[at, :] = heads[g, :, 0:WIDE]
        k[at, :] = heads[g, :, WIDE : 2 * WIDE]
        v[at, :] = heads[g, :, 2 * WIDE : 3 * WIDE]


def attend_part(q, k, v, o, lse, send):
    rows = o.shape[1]
    seen = diagonal(rows)
    for i in reversed(range(GROUP)):
        for h in range(WIDE // HEAD):
            cols = slice(h * HEAD, (h + 1) * HEAD)
            here = slice(i * rows, (i + 1) * rows)
            qi = q[here, cols]
            near = jnp.where(seen, nt(qi, k[here, cols]) * 0.125, -1000000000.0)
            top = jnp.max(near, axis=1, keepdims=True)
            if i:
                far = nt(qi, k[0 : i * rows, cols]) * 0.125
                top = jnp.maximum(top, jnp.max(far, axis=1, keepdims=True))
                far = jnp.exp(far - top)
            near = jnp.exp(near - top)
            total = jnp.sum(near, axis=1, keepdims=True)
            if i:
                total = total + jnp.sum(far, axis=1, keepdims=True)
            inv = 1.0 / total
            res = nn((near * inv).astype(BF), v[here, cols])
            if i:
                res = res + nn((far * inv).astype(BF), v[0 : i * rows, cols])
            o[i, :, cols] = res.astype(BF)
            lse[here, h : h + 1] = top + jnp.log(total)
            yield
        send(i)


def ff_part(x, parts, vec, weights, wr_rows, sems, attended, hidden, normed, upper, active, out):
    wo, we, wr = weights
    for g in range(GROUP):
        attended[:, g * WIDE : (g + 1) * WIDE] = parts[g]
    wait_all(wo, sems[0])
    for g in range(GROUP):
        cols = slice(g * WIDE, (g + 1) * WIDE)
        hidden[:, cols] = x[:, cols].astype(F32) + nn(attended[...], side(wo, 2 * g)) + vec[4:5, cols]
        yield
    hat, _ = norm_parts(hidden[...])
    normed[...] = (hat * vec[5:6, :] + vec[6:7, :]).astype(BF)
    out[...] = hidden[...] + vec[11:12, :]
    wait_all(we, sems[1])
    wait_all(wr, sems[2])
    yield
    for n in range(CHUNKS):
        row, col = 7 + n // GROUP, n % GROUP * WIDE
        u = nn(normed[...], side(we, 2 * n)) + vec[row : row + 1, col : col + WIDE]
        upper[n] = u
        act = (0.5 * u * (1.0 + jnp.tanh(gelu_c * (u + gelu_a * u * u * u)))).astype(BF)
        active[n] = act
        out[...] += nn(act, wr_rows(n))
        yield


def ring_reader(upper, ring, sems):
    def fetch(n):
        return pltpu.make_async_copy(upper.at[n], ring.at[n % 2], sems[n % 2])

    fetch(0).start()

    def read(n):
        if n + 1 < CHUNKS:
            fetch(n + 1).start()
        fetch(n).wait()
        return ring[n % 2]

    return read


def ff_back_part(dy, read_upper, hidden, vec, weights, sems, dyb, dub, dh, dhb, blocks, acc, bias_grad, vec_grad):
    wo, we, wr = weights
    dyb[...] = dy[...].astype(BF)
    vec_grad[0:1, :] = jnp.sum(dy[...].astype(F32), axis=0, keepdims=True)
    acc[...] = jnp.zeros_like(acc)
    if sems:
        wait_all(wr, sems[2])
        wait_all(we, sems[1])
    for n in range(CHUNKS):
        at = n * WIDE % D
        dg = nt(dyb[...], side_rows(wr, n * WIDE // D, slice(at, at + WIDE)))
        u = read_upper(n)
        t = jnp.tanh(gelu_c * (u + gelu_a * u * u * u))
        slope = 0.5 * (1.0 + t) + 0.5 * u * (1.0 - t * t) * (gelu_c * (1.0 + 3.0 * gelu_a * u * u))
        du = dg * slope
        row, col = n // GROUP, n % GROUP * WIDE
        bias_grad[row : row + 1, col : col + WIDE] = jnp.sum(du, axis=0, keepdims=True)
        low = du.astype(BF)
        dub[n] = low
        acc[...] += nt(low, side(we, 2 * n))
        yield
    back, gain, shift = norm_back(hidden[...], vec[5:6, :], acc[...])
    total = dy[...].astype(F32) + back
    vec_grad[1:2, :] = gain
    vec_grad[2:3, :] = shift
    vec_grad[3:4, :] = jnp.sum(total, axis=0, keepdims=True)
    dh[...] = total
    dhb[...] = total.astype(BF)
    if sems:
        wait_all(wo, sems[0])
    yield
    for g in range(GROUP):
        blocks[g] = nt(dhb[...], rows_of(wo, slice(g * WIDE, (g + 1) * WIDE))).astype(BF)
    yield


def side_rows(ref, at, rows):
    return jnp.concatenate([ref[p * 4 + at, rows, :] for p in range(D // LANES)], axis=1)


def attend_back_part(q, k, v, do, lse, dm, dk, dv, sums, send):
    rows = dm.shape[1]
    seen = diagonal(rows)
    sums[...] = jnp.zeros_like(sums)
    for i in reversed(range(GROUP)):
        here = slice(i * rows, (i + 1) * rows)
        past = slice(0, i * rows)
        last = i == GROUP - 1
        for h in range(WIDE // HEAD):
            cols = slice(h * HEAD, (h + 1) * HEAD)
            qi, doi, ls = q[here, cols], do[i, :, cols], lse[here, h : h + 1]
            near = jnp.exp(jnp.where(seen, nt(qi, k[here, cols]) * 0.125, -1000000000.0) - ls)
            dnear = nt(doi, v[here, cols])
            inner = jnp.sum(near * dnear, axis=1, keepdims=True)
            if i:
                far = jnp.exp(nt(qi, k[past, cols]) * 0.125 - ls)
                dfar = nt(doi, v[past, cols])
                inner = inner + jnp.sum(far * dfar, axis=1, keepdims=True)
            snear = (near * (dnear - inner) * 0.125).astype(BF)
            res = nn(snear, k[here, cols])
            dkn = tn(snear, qi)
            dvn = tn(near.astype(BF), doi)
            dk[here, cols] = dkn if last else dk[here, cols] + dkn
            dv[here, cols] = dvn if last else dv[here, cols] + dvn
            if i:
                sfar = (far * (dfar - inner) * 0.125).astype(BF)
                res = res + nn(sfar, k[past, cols])
                dkf = tn(sfar, qi)
                dvf = tn(far.astype(BF), doi)
                dk[past, cols] = dkf if last else dk[past, cols] + dkf
                dv[past, cols] = dvf if last else dv[past, cols] + dvf
            sums[0:1, cols] += jnp.sum(res, axis=0, keepdims=True)
            dm[i, :, cols] = res.astype(BF)
            yield
        dm[i, :, WIDE : 2 * WIDE] = dk[here, :].astype(BF)
        dm[i, :, 2 * WIDE : 3 * WIDE] = dv[here, :].astype(BF)
        sums[1:2, :] += jnp.sum(dv[here, :], axis=0, keepdims=True)
        send(i)


def qkv_back_part(mixed, weight, acc):
    for b in range(3 * GROUP):
        kind, at = b // GROUP, b % GROUP
        acc[...] += nt(mixed[at, :, kind * WIDE : (kind + 1) * WIDE], side(weight, 2 * b))
        yield


class Mover:
    def __init__(self, n_dp):
        self.n_dp = n_dp
        self.size, self.pieces = pieces_of(n_dp)
        self.line = 12 * D // (4 * n_dp)
        self.span = self.size + 16

    def gather_all(self, helds):
        wholes = [lax.all_gather(held, ("ctx", "dp"), axis=0, tiled=True) for held in helds]
        return [whole.reshape(4, self.n_dp, self.span, LANES) for whole in wholes]

    def vectors(self, whole):
        rows = -(-self.line // LANES)
        lines = whole[:, :, self.size : self.size + rows].reshape(4, self.n_dp, -1)[:, :, : self.line]
        return lines.transpose(1, 0, 2).reshape(12, D).astype(F32)

    def scatter(self, buffer):
        none = jnp.zeros_like(buffer)
        core = lax.axis_index("dp") % 2
        pair = jnp.stack([jnp.where(core == 0, buffer, none), jnp.where(core == 1, buffer, none)], axis=2)
        flat = pair.reshape(-1, LANES)
        return lax.psum_scatter(flat, ("ctx", "dp"), scatter_dimension=0, tiled=True).astype(F32)

    def scatter_vectors(self, grads):
        return lax.psum_scatter(grads.reshape(-1), ("dp", "ctx"), scatter_dimension=0, tiled=True)


CORE = 1
FLIPS = ((1, 0), (2, 0), (3, 0), (4, 0), (0, 1), (0, 2), (0, 3))


class BitMover(Mover):
    def __init__(self, n_dp):
        super().__init__(n_dp)
        self.gap, self.pace, self.pace_back = 5, (1.3, 4, 2), (1.5, 4, 2, 2)
        self.even = self.cut(((4, 4), (2, 2), (4, 4), (2, 2), (4, 4), (2, 2), (4, 4), (2, 2)))
        self.skew = self.cut(((5, 3), (3, 1), (5, 2), (3, 2), (5, 3), (3, 1), (5, 2), (3, 2)))

    def cut(self, plan):
        unit, row, chunks = self.size // 48, 0, []
        for i, pair in enumerate(plan):
            for units, (a, b) in zip(pair, ((2, 4), (4, 2))):
                chunks.append((row, units * unit, (i % 2 == 0, a, b), i // 2))
                row += units * unit
        return chunks

    def gather_jobs(self, wire, local, helds, wholes, plans, done):
        d, z = wire.d, wire.z

        def job(layer, part):
            low, size, (z_first, a, b), _ = plans[layer][part]
            if part == len(plans[layer]) - 1:
                size = self.span - low
            rows = pl.ds(low, size)
            held, whole = helds[layer].at[rows], wholes[layer]
            started = []

            def push(src, dst, fd, fz):
                started.append(wire.push(src, dst, fd, fz))
                return started[-1]

            def line(dd, fd):
                ref = whole.at[:, dd, rows]
                return push(ref, ref, fd, 0)

            own = pltpu.make_async_copy(held, whole.at[z, d, rows], local.at[layer * len(plans[0]) + part])
            own.start()
            mine = [push(held, whole.at[z, d, rows], 0, k) for k in (3, 2, 1)]
            if z_first:
                yield
                own.wait()
                for copy in mine:
                    copy.wait_recv()
                first = line(d, a)
                second = line(d, b)
                cores = [line(d, CORE)]
                yield
                first.wait_recv()
                third = line(d ^ a, b)
                cores.append(line(d ^ a, CORE))
                yield
                second.wait_recv()
                cores.append(line(d ^ b, CORE))
                yield
                third.wait_recv()
                cores.append(line(d ^ a ^ b, CORE))
            else:
                first = push(held, whole.at[z, d, rows], a, 0)
                yield
                first.wait_recv()
                other = whole.at[z, d ^ a, rows]
                theirs = [push(other, other, 0, k) for k in (3, 2, 1)]
                yield
                own.wait()
                for copy in mine:
                    copy.wait_recv()
                second = line(d, b)
                cores = [line(d, CORE)]
                yield
                for copy in theirs:
                    copy.wait_recv()
                third = line(d ^ a, b)
                cores.append(line(d ^ a, CORE))
                yield
                second.wait_recv()
                cores.append(line(d ^ b, CORE))
                yield
                third.wait_recv()
                cores.append(line(d ^ a ^ b, CORE))
            yield
            for copy in cores:
                copy.wait_recv()
            for copy in started:
                copy.wait_send()
            done[layer] += 1

        jobs = [job(layer, part) for layer, plan in enumerate(plans) for part in range(len(plan))]
        return drive(jobs, [chunk[3] + self.gap * layer for layer, plan in enumerate(plans) for chunk in plan])

    def forward_first(self, helds, tokens):
        rows = tokens.shape[0]
        span = GROUP * rows
        plans = (self.even, self.skew)
        pieces, count, pace = self.pieces, len(self.even), self.pace
        slots = 2 * count * 14 + 16

        def kernel(
            held0, held1, tokens,
            whole0, whole1, value, vec, normed1, heads_out, lse, attended, hidden, normed2, upper, active, out,
            swapped, heads, blocks, q, k, v, o, parts, raw, wa, wo, we, wr, local, sems, send, recv,
        ):
            wire = Wire(send, recv)
            wire.greet(FLIPS, swaps=True)
            done = [0, 0]
            comm = self.gather_jobs(wire, local, (held0, held1), (whole0, whole1), plans, done)
            take(comm, 6)
            swap_in = wire.swap(tokens, swapped)
            while done[0] < count:
                next(comm)
            load_vec = pltpu.make_async_copy(whole0.at[:, :, pl.ds(self.size, 16)], raw, sems.at[4])
            load_vec.start()
            load_matrix(whole0, wa, 0, pieces, sems.at[3])
            load_matrix(whole0, wo, 1, pieces, sems.at[0])
            swap_in()
            value[...] = swapped[...]
            load_vec.wait()
            unpack_vectors(raw, vec, self.n_dp, self.size)
            hat, _ = norm_parts(swapped[...].astype(F32))
            normed1[...] = (hat * vec[0:1, :] + vec[1:2, :]).astype(BF)
            wait_all(wa, sems.at[3])
            advance = paced(comm, pace[0])
            copies = []
            for _ in qkv_part(wire, normed1, wa, vec, blocks, heads, copies):
                advance()
            load_matrix(whole0, we, 2, pieces, sems.at[1])
            load_matrix(whole0, wr, 3, pieces, sems.at[2])
            take(comm, pace[1])
            for copy in copies:
                copy.wait()
            spread_heads(heads, q, k, v)
            heads_out[...] = heads[...]
            send_o, finish = wire.post(o, parts)
            for _ in attend_part(q, k, v, o, lse, send_o):
                advance()
            take(comm, pace[2])
            finish()
            for _ in ff_part(
                swapped, parts, vec, (wo, we, wr), lambda n: rows_of(wr, slice(n * WIDE, (n + 1) * WIDE)), [sems.at[i] for i in range(3)],
                attended, hidden, normed2, upper, active, out,
            ):
                advance()
            for _ in comm:
                pass

        return pl.pallas_call(
            kernel,
            out_shape=[shape((4, self.n_dp, self.span, LANES), BF)] * 2
            + [
                shape((rows, D), BF),
                shape((12, D), F32),
                shape((rows, D), BF),
                shape((GROUP, rows, 3 * WIDE), BF),
                shape((span, LANES), F32),
                shape((rows, D), BF),
                shape((rows, D), F32),
                shape((rows, D), BF),
                shape((CHUNKS, rows, WIDE), F32),
                shape((CHUNKS, rows, WIDE), BF),
                shape((rows, D), F32),
            ],
            in_specs=[VM] * 3,
            out_specs=[ANY] * 2 + [VM] * 11,
            scratch_shapes=[pltpu.VMEM((rows, D), BF)]
            + [pltpu.VMEM((GROUP, rows, 3 * WIDE), BF)] * 2
            + [pltpu.VMEM((span, WIDE), BF)] * 3
            + [pltpu.VMEM((GROUP, rows, WIDE), BF)] * 2
            + [
                pltpu.VMEM((4, self.n_dp, 16, LANES), BF),
                pltpu.VMEM((3 * D // LANES, D, LANES), BF),
                pltpu.VMEM((D // LANES, D, LANES), BF),
                pltpu.VMEM((FF // LANES, D, LANES), BF),
                pltpu.VMEM((D // LANES, FF, LANES), BF),
                pltpu.SemaphoreType.DMA((2 * count,)),
                pltpu.SemaphoreType.DMA((5,)),
                pltpu.SemaphoreType.DMA((slots,)),
                pltpu.SemaphoreType.DMA((slots,)),
            ],
            compiler_params=params_of(collective_id=1, has_side_effects=True),
            name="forward_first",
        )(*helds, tokens)

    def scatter_jobs(self, wire, parts):
        d, z = wire.d, wire.z

        def job(grads, acc, from_b, from_a, from_z, order, size, put, local):
            z_first, a, b = order
            started = []

            def push(src, dst, fd, fz):
                started.append(wire.push(src, dst, fd, fz))
                return started[-1]

            places = [(d ^ (ja * a)) // 2 for ja in (1, 0)]
            if acc is None:
                piece = [lambda k, p=p: grads.at[k, p] for p in places]
                pieces = [grads.at[:, p] for p in places]
            else:
                piece = [lambda k, i=i: acc.at[i, k] for i in range(2)]
                pieces = [acc.at[i] for i in range(2)]
            block = min(64, size)

            def add(into, more):
                def body(i, _):
                    at = pl.ds(pl.multiple_of(i * block, block), block)
                    for x, y in zip(into, more):
                        x[at, :] = x[at, :] + y[at, :]
                    return 0

                lax.fori_loop(0, size // block, body, 0)

            def every(i, more):
                add([piece[i](k) for k in range(4)], [more(k) for k in range(4)])

            to_b = [push(grads.at[:, p ^ (b // 2)], from_b.at[i], b, 0) for i, p in enumerate(places)]
            loads = []
            if acc is not None:
                for i in range(2):
                    loads.append(pltpu.make_async_copy(grads.at[:, places[i]], acc.at[i], local[i]))
                    loads[-1].start()
            yield
            for load in loads:
                load.wait()
            to_b[0].wait_recv()
            every(0, lambda k: from_b.at[0, k])
            if z_first:
                to_a = push(pieces[0], from_a, a, 0)
                yield
                to_b[1].wait_recv()
                every(1, lambda k: from_b.at[1, k])
                yield
                to_a.wait_recv()
                every(1, lambda k: from_a.at[k])
                to_z = [push(piece[1](z ^ k), from_z.at[k - 1, 0], 0, k) for k in (3, 2, 1)]
                yield
                more = [from_z.at[k, 0] for k in range(3)]
                last = to_z
            else:
                to_z = [push(piece[0](z ^ k), from_z.at[k - 1, 0], 0, k) for k in (3, 2, 1)]
                yield
                to_b[1].wait_recv()
                every(1, lambda k: from_b.at[1, k])
                to_z1 = [push(piece[1](z ^ k), from_z.at[k - 1, 1], 0, k) for k in (3, 2, 1)]
                yield
                for copy in to_z:
                    copy.wait_recv()
                for k in range(3):
                    add([piece[0](z)], [from_z.at[k, 0]])
                to_a = push(piece[0](z), from_a.at[0], a, 0)
                yield
                more = [from_z.at[k, 1] for k in range(3)] + [from_a.at[0]]
                last = to_z1 + [to_a]
            for copy in last:
                copy.wait_recv()

            def body(i, _):
                at = pl.multiple_of(i * block, block)
                here = pl.ds(at, block)
                value = piece[1](z)[here, :].astype(F32)
                for ref in more:
                    value = value + ref[here, :].astype(F32)
                put(at, block, value)
                return 0

            lax.fori_loop(0, size // block, body, 0)
            for copy in started:
                copy.wait_send()

        return [job(*part) for part in parts]

    def scatter_scratch(self, plan, with_acc):
        result = []
        for _, n, order, _ in plan:
            if with_acc:
                result.append(pltpu.VMEM((2, 4, n, LANES), BF))
            result.append(pltpu.VMEM((2, 4, n, LANES), BF))
            result.append(pltpu.VMEM((4 if order[0] else 1, n, LANES), BF))
            result.append(pltpu.VMEM((3, 1 if order[0] else 2, n, LANES), BF))
        return result

    def scatter_parts(self, plan, grads, scratch, owned, local):
        each = len(scratch) // len(plan)
        parts = []
        for i, (low, n, order, _) in enumerate(plan):
            refs = scratch[i * each : (i + 1) * each]
            acc, (from_b, from_a, from_z) = (refs[0] if each == 4 else None), refs[-3:]

            def put(at, block, value, low=low):
                owned[pl.ds(low + at, block), :] = value

            waits = [local.at[2 * i], local.at[2 * i + 1]] if each == 4 else None
            parts.append((grads.at[:, :, pl.ds(low, n)], acc, from_b, from_a, from_z, order, n, put, waits))
        return parts

    def backward_first(self, me, grads, saved, dy, vec, whole):
        x, normed1, heads, lse, attended, hidden, normed2, upper, active = saved
        rows = x.shape[0]
        span = GROUP * rows
        plan, pieces, pace = self.skew, self.pieces, self.pace_back
        count = len(plan)
        slots = count * 12 + 24
        scratch_count = 4 * count

        def kernel(
            grads, x, normed1, heads, lse, attended, hidden, normed2, upper, active, dy, vec, whole,
            owned, dx, dyb, dub, dhb, mixed, bias_grad, vec_grad, sums,
            o_normed1, o_attended, o_normed2, o_active, o_mixed, o_dhb, o_dub, o_dyb,
            *scratch,
        ):
            bufs = scratch[:scratch_count]
            q, k, v, do, blocks, dk, dv, dm, acc, dh, ring, wo, we, wr, local, sems, send, recv = scratch[scratch_count:]
            sems = [sems.at[i] for i in range(8)]
            load_matrix(whole, wr, 3, pieces, sems[2], split=True)
            load_matrix(whole, we, 2, pieces, sems[1])
            load_matrix(whole, wo, 1, pieces, sems[0])
            for g in range(GROUP):
                for i, ref in enumerate((q, k, v)):
                    pltpu.make_async_copy(
                        heads.at[g, :, pl.ds(i * WIDE, WIDE)], ref.at[pl.ds(g * rows, rows)], sems[5]
                    ).start()
            wire = Wire(send, recv)
            wire.greet(FLIPS)
            comm = drive(
                self.scatter_jobs(wire, self.scatter_parts(plan, grads, bufs, owned, local)), [chunk[3] for chunk in plan]
            )
            advance = paced(comm, pace[0])
            take(comm, pace[1])
            core = [wire.push(a, b, CORE, 0) for a, b in (
                (normed1, o_normed1), (attended, o_attended), (normed2, o_normed2), (active, o_active))]
            vec_grad[...] = jnp.zeros_like(vec_grad)
            read_upper = ring_reader(upper, ring, sems[3:5])
            for _ in ff_back_part(
                dy, read_upper, hidden, vec, (wo, we, wr), sems, dyb, dub, dh, dhb, blocks, acc, bias_grad, vec_grad
            ):
                advance()
            load_matrix(whole, wr, 0, pieces, sems[6])
            core += [wire.push(a, b, CORE, 0) for a, b in ((dyb, o_dyb), (dub, o_dub), (dhb, o_dhb))]
            copies = wire.trade(blocks, do)
            take(comm, pace[2])
            for ref in (q, k, v):
                wait_all(ref, sems[5])
            for copy in copies:
                copy.wait()
            send_m, finish = wire.post(dm, mixed)
            for _ in attend_back_part(q, k, v, do, lse, dm, dk, dv, sums, send_m):
                advance()
            acc[...] = jnp.zeros_like(acc)
            take(comm, pace[3])
            finish()
            core.append(wire.push(mixed, o_mixed, CORE, 0))
            wait_all(wr.at[pl.ds(0, 3 * D // LANES)], sems[6])
            for _ in qkv_back_part(mixed, wr, acc):
                advance()
            back, gain, shift = norm_back(x[...].astype(F32), vec[0:1, :], acc[...])
            dx[...] = dh[...] + back
            vec_grad[4:5, :] = gain
            vec_grad[5:6, :] = shift
            for _ in comm:
                pass
            for copy in core:
                copy.wait()

        token = shape((rows, D), BF)
        wide = shape((CHUNKS, rows, WIDE), BF)
        triple = shape((GROUP, rows, 3 * WIDE), BF)
        return pl.pallas_call(
            kernel,
            out_shape=[
                shape((self.size, LANES), F32),
                shape((rows, D), F32),
                token,
                wide,
                token,
                triple,
                shape((4, D), F32),
                shape((8, D), F32),
                shape((8, WIDE), F32),
            ]
            + [token, token, token, wide, triple, token, wide, token],
            in_specs=[ANY, VM, ANY, ANY, VM, ANY, VM, ANY, ANY, ANY, VM, VM, ANY],
            out_specs=[VM] * 9 + [ANY] * 8,
            scratch_shapes=self.scatter_scratch(plan, True)
            + [pltpu.VMEM((span, WIDE), BF)] * 3
            + [pltpu.VMEM((GROUP, rows, WIDE), BF)] * 2
            + [pltpu.VMEM((span, WIDE), F32)] * 2
            + [
                pltpu.VMEM((GROUP, rows, 3 * WIDE), BF),
                pltpu.VMEM((rows, D), F32),
                pltpu.VMEM((rows, D), F32),
                pltpu.VMEM((2, rows, WIDE), F32),
                pltpu.VMEM((D // LANES, D, LANES), BF),
                pltpu.VMEM((FF // LANES, D, LANES), BF),
                pltpu.VMEM((4 * D // LANES, D, LANES), BF),
                pltpu.SemaphoreType.DMA((2 * count,)),
                pltpu.SemaphoreType.DMA((8,)),
                pltpu.SemaphoreType.DMA((slots,)),
                pltpu.SemaphoreType.DMA((slots,)),
            ],
            compiler_params=params_of(collective_id=2, has_side_effects=True),
            name="backward_first",
        )(grads, x, normed1, heads, lse, attended, hidden, normed2, upper, active, dy, vec, whole)

    def middle(self, x, cotangent, vec, whole):
        rows = x.shape[0]
        span = GROUP * rows
        pieces = self.pieces
        slots = 40

        def kernel(
            x, cotangent, vec, whole,
            output, dx, normed1, attended, normed2, active, mixed, dhb, dub, dyb,
            o_normed1, o_attended, o_normed2, o_active, o_mixed, o_dhb, o_dub, o_dyb, bias_grad, vec_grad, sums,
            dy, result, returned, heads, blocks, q, k, v, o, parts, do, lse, hidden, upper, acc, dh, dk, dv, wa, wo, we, wr,
            sems, send, recv,
        ):
            sems = [sems.at[i] for i in range(4)]
            load_matrix(whole, wa, 0, pieces, sems[3])
            load_matrix(whole, wo, 1, pieces, sems[0])
            wire = Wire(send, recv)
            hat, _ = norm_parts(x[...])
            normed1[...] = (hat * vec[0:1, :] + vec[1:2, :]).astype(BF)
            wire.greet(FLIPS, swaps=True)
            wait_all(wa, sems[3])
            copies = []
            for _ in qkv_part(wire, normed1, wa, vec, blocks, heads, copies):
                pass
            load_matrix(whole, we, 2, pieces, sems[1])
            load_matrix(whole, wr, 3, pieces, sems[2], split=True)
            core = [wire.push(normed1, o_normed1, CORE, 0)]
            for copy in copies:
                copy.wait()
            swap_in = wire.swap(cotangent, dy)
            spread_heads(heads, q, k, v)
            send_o, finish = wire.post(o, parts)
            for _ in attend_part(q, k, v, o, lse, send_o):
                pass
            finish()
            for _ in ff_part(
                x, parts, vec, (wo, we, wr), lambda n: side_rows(wr, n // GROUP, slice(n % GROUP * WIDE, (n % GROUP + 1) * WIDE)),
                sems, attended, hidden, normed2, upper, active, dx,
            ):
                pass
            core += [wire.push(a, b, CORE, 0) for a, b in (
                (attended, o_attended), (normed2, o_normed2), (active, o_active))]
            result[...] = dx[...].astype(BF)
            swap_out = wire.swap(result, returned)
            swap_in()
            vec_grad[...] = jnp.zeros_like(vec_grad)
            for _ in ff_back_part(
                dy, lambda n: upper[n], hidden, vec, (wo, we, wr), None, dyb, dub, dh, dhb, o, acc, bias_grad, vec_grad
            ):
                pass
            copies = wire.trade(o, do)
            core += [wire.push(a, b, CORE, 0) for a, b in ((dyb, o_dyb), (dub, o_dub), (dhb, o_dhb))]
            for copy in copies:
                copy.wait()
            send_m, finish = wire.post(blocks, mixed)
            for _ in attend_back_part(q, k, v, do, lse, blocks, dk, dv, sums, send_m):
                pass
            acc[...] = jnp.zeros_like(acc)
            finish()
            core.append(wire.push(mixed, o_mixed, CORE, 0))
            for _ in qkv_back_part(mixed, wa, acc):
                pass
            back, gain, shift = norm_back(x[...], vec[0:1, :], acc[...])
            dx[...] = dh[...] + back
            vec_grad[4:5, :] = gain
            vec_grad[5:6, :] = shift
            swap_out()
            output[...] = returned[...]
            for copy in core:
                copy.wait()

        token = shape((rows, D), BF)
        wide = shape((CHUNKS, rows, WIDE), BF)
        triple = shape((GROUP, rows, 3 * WIDE), BF)
        kept = [token, token, token, wide, triple, token, wide, token]
        return pl.pallas_call(
            kernel,
            out_shape=[token, shape((rows, D), F32)] + kept * 2
            + [shape((4, D), F32), shape((8, D), F32), shape((8, WIDE), F32)],
            in_specs=[VM, VM, VM, ANY],
            out_specs=[VM] * 10 + [ANY] * 8 + [VM] * 3,
            scratch_shapes=[pltpu.VMEM((rows, D), BF)] * 3
            + [pltpu.VMEM((GROUP, rows, 3 * WIDE), BF)] * 2
            + [pltpu.VMEM((span, WIDE), BF)] * 3
            + [pltpu.VMEM((GROUP, rows, WIDE), BF)] * 3
            + [
                pltpu.VMEM((span, LANES), F32),
                pltpu.VMEM((rows, D), F32),
                pltpu.VMEM((CHUNKS, rows, WIDE), F32),
                pltpu.VMEM((rows, D), F32),
                pltpu.VMEM((rows, D), F32),
                pltpu.VMEM((span, WIDE), F32),
                pltpu.VMEM((span, WIDE), F32),
                pltpu.VMEM((3 * D // LANES, D, LANES), BF),
                pltpu.VMEM((D // LANES, D, LANES), BF),
                pltpu.VMEM((FF // LANES, D, LANES), BF),
                pltpu.VMEM((4 * D // LANES, D, LANES), BF),
                pltpu.SemaphoreType.DMA((4,)),
                pltpu.SemaphoreType.DMA((slots,)),
                pltpu.SemaphoreType.DMA((slots,)),
            ],
            compiler_params=params_of(collective_id=4, has_side_effects=True),
            name="middle",
        )(x, cotangent, vec, whole)

    def scatter_first(self, own, other, vectors0, vectors1):
        plan, pieces, thirds = self.even, self.pieces, self.size // 3
        count = len(plan)
        slots = count * 12 + 24
        scratch_count = 3 * count

        def kernel(*refs):
            own, other, vectors, (owned, vec_owned) = refs[:8], refs[8:16], (refs[16:19], refs[19:22]), refs[22:24]
            scratch = refs[24:]
            bufs = scratch[:scratch_count]
            grads, lines, got, small, from_b, from_a, from_z, send, recv = scratch[scratch_count:]
            wire = Wire(send, recv)
            wire.greet([flip for flip in FLIPS if flip[0] != 3])
            mine = pl.ds(pl.multiple_of(wire.place * WIDE, WIDE), WIDE)
            for i, (bias_grad, vec_grad, sums) in enumerate(vectors):
                lines[i, 0:2, :] = vec_grad[4:6, :]
                lines[i, 2:4, :] = jnp.zeros((2, D), F32)
                lines[i, 2:4, mine] = sums[0:2, :]
                lines[i, 4:5, :] = vec_grad[3:4, :]
                lines[i, 5:7, :] = vec_grad[1:3, :]
                lines[i, 7:11, :] = bias_grad[...]
                lines[i, 11:12, :] = vec_grad[0:1, :]
            trade = wire.push(lines, got, CORE, 0)

            def make(group):
                for core in range(2):
                    items = [item for item in weight_items(pieces, core) if item[0] // thirds == group]

                    @pl.when(wire.d % 2 == core)
                    def _(items=items):
                        weight_part(items, own, other, grads)

            def put(at, block, value):
                vec_owned[pl.ds(at, block), :] = value

            parts = self.scatter_parts(plan, grads, bufs, owned, None)
            jobs = self.scatter_jobs(wire, parts)
            made = [0]

            def after(job, rows):
                while made[0] * thirds < rows:
                    make(made[0])
                    made[0] += 1
                yield from job

            jobs = [after(job, low + n) for job, (low, n, _, _) in zip(jobs, plan)]

            def vector_job():
                trade.wait()
                lines[...] = lines[...] + got[...]
                share, per_row = self.line // LANES, D // LANES
                small[...] = jnp.zeros_like(small)
                for core in range(2):

                    @pl.when(wire.d % 2 == core)
                    def _(core=core):
                        for d in range(core, self.n_dp, 2):
                            for z in range(4):
                                for r in range(share):
                                    at = (d * 4 + z) * share + r
                                    row, col = at // per_row, at % per_row * LANES
                                    for i in range(2):
                                        here = slice(i * 4 + r, i * 4 + r + 1)
                                        small[z, d // 2, here, :] = lines[i, row : row + 1, col : col + LANES]

                yield from self.scatter_jobs(wire, [(small, None, from_b, from_a, from_z, (True, 2, 4), 8, put, None)])[0]

            jobs.append(vector_job())
            for _ in drive(jobs, [chunk[3] for chunk in plan] + [1]):
                pass

        return pl.pallas_call(
            kernel,
            out_shape=[shape((self.size, LANES), F32), shape((8, LANES), F32)],
            in_specs=[VM] * 22,
            out_specs=[VM] * 2,
            scratch_shapes=self.scatter_scratch(plan, False)
            + [
                pltpu.VMEM((4, self.n_dp // 2, self.size, LANES), BF),
                pltpu.VMEM((2, 12, D), F32),
                pltpu.VMEM((2, 12, D), F32),
                pltpu.VMEM((4, self.n_dp // 2, 8, LANES), F32),
                pltpu.VMEM((2, 4, 8, LANES), F32),
                pltpu.VMEM((4, 8, LANES), F32),
                pltpu.VMEM((3, 1, 8, LANES), F32),
                pltpu.SemaphoreType.DMA((slots,)),
                pltpu.SemaphoreType.DMA((slots,)),
            ],
            compiler_params=params_of(collective_id=3, has_side_effects=True),
            name="scatter_first",
        )(*own, *other, *vectors0, *vectors1)


def swap(values, n_dp):
    pairs = [
        (d * GROUP + z, ((d // GROUP) * GROUP + place_of(z)) * GROUP + place_of(d % GROUP))
        for d in range(n_dp)
        for z in range(GROUP)
    ]
    return lax.ppermute(values, ("dp", "ctx"), pairs)


def send_core(values, n_dp):
    pairs = [(d * GROUP + z, (d ^ 1) * GROUP + z) for d in range(n_dp) for z in range(GROUP)]
    return lax.ppermute(values, ("dp", "ctx"), pairs)


def trade(arrays, n_dp):
    result = [arrays[0]]
    for r in range(1, GROUP):
        pairs = [(d * GROUP + z, (d ^ r) * GROUP + z) for d in range(n_dp) for z in range(GROUP)]
        result.append(lax.ppermute(arrays[r], ("dp", "ctx"), pairs))
    return result


def per_device(
    n_dp,
    layer_input,
    out_cotangent,
    params,
    vectors,
    param_moment,
    vector_moment,
    param_square,
    vector_square,
):
    plan = BitMover(n_dp) if n_dp == 8 else Mover(n_dp)
    me = jnp.stack([lax.axis_index("dp"), lax.axis_index("ctx")]).astype(jnp.int32)
    place = place_of(me[0])

    helds = prepare(plan, me, params, vectors)
    fused = n_dp == 8
    if fused:
        whole0, whole1, value0, vec0, normed1, heads, *rest, value = plan.forward_first(helds, layer_input)
        wholes, vecs = [whole0, whole1], [vec0, plan.vectors(whole1)]
        first = (value0, normed1, heads, *rest)
    else:
        wholes = plan.gather_all(helds)
        vecs = [plan.vectors(whole) for whole in wholes]
        value = swap(layer_input, n_dp).astype(F32)
        grad = swap(out_cotangent, n_dp).astype(F32)

    saved = [None] * LAYERS
    for layer in range(LAYERS if fused else 0, LAYERS):
        vec, whole = vecs[layer], wholes[layer]
        bias = vec[7:11].reshape(CHUNKS, 1, WIDE)
        normed1, *sent = qkv_call(plan, me, value, vec, whole)
        heads = trade(sent, n_dp)
        *sent, lse = attend_call(me, heads)
        attended, hidden, normed2, upper, active, result = ff_call(
            plan, me, trade(sent, n_dp), value, vec, bias, whole
        )
        saved[layer] = (value, normed1, heads, lse, attended, hidden, normed2, upper, active)
        value = result
    if not fused:
        layer_output = swap(value.astype(BF), n_dp)

    def lines_of(gain_one, shift_one, sums, bias_output, gain_two, shift_two, bias_expand, bias_reduce):
        spread = lax.dynamic_update_slice(jnp.zeros((2, D), F32), sums[0:2], (0, place * WIDE))
        rows = [gain_one, shift_one, spread, bias_output, gain_two, shift_two, bias_expand, bias_reduce]
        return jnp.concatenate([row.reshape(-1, D) for row in rows])

    owned, lines = [None] * LAYERS, [None] * LAYERS
    for layer in reversed(range(LAYERS if fused else 0, LAYERS)):
        vec, whole = vecs[layer], wholes[layer]
        x, normed1, heads, lse, attended, hidden, normed2, upper, active = saved[layer]
        dyb, dub, dh, dhb, *rest = ff_back_call(plan, me, grad, upper, hidden, vec, whole)
        sent, bias_grad, vec2 = rest[:GROUP], rest[GROUP], rest[GROUP + 1]
        *sent, sums = attend_back_call(me, heads, trade(sent, n_dp), lse)
        mixed, grad, vec1 = qkv_back_call(plan, me, trade(sent, n_dp), dh, x, vec, whole)
        own = (normed1, attended, normed2, active, mixed, dhb, dub, dyb)
        buffer = weight_call(plan, me, own, [send_core(x, n_dp) for x in own])
        lines[layer] = lines_of(vec1[0], vec1[1], sums, vec2[3], vec2[1], vec2[2], bias_grad, vec2[0])
        owned[layer] = plan.scatter(buffer)
    if fused:
        layer_output, grad, *kept, bias_grad, vec2, sums = plan.middle(value, out_cotangent, vecs[1], whole1)
        buffer = weight_call(plan, me, kept[:8], kept[8:])
        vectors1 = (bias_grad, vec2, sums)
        owned[1], grad, dyb, dub, dhb, mixed, bias_grad, vec2, sums, *other = plan.backward_first(
            me, buffer, first, grad, vec0, whole0
        )
        _, normed1, _, _, attended, _, normed2, _, active = first
        own = (normed1, attended, normed2, active, mixed, dhb, dub, dyb)
        owned[0], vec_sums = plan.scatter_first(own, other, (bias_grad, vec2, sums), vectors1)
        share = plan.line // LANES
        vec_owned = [vec_sums[4 * layer : 4 * layer + share].reshape(-1) for layer in range(LAYERS)]
    else:
        vec_owned = [plan.scatter_vectors(line) for line in lines]
    input_grad = swap(grad.astype(BF), n_dp).astype(F32)

    done = []
    for layer in reversed(range(LAYERS)):
        done = adam_call(plan, me, layer, owned[layer], params, param_moment, param_square, done)
    vector_grad = jnp.stack(vec_owned)
    vector_step = adam_parts(vector_grad, vector_moment, vector_square, vectors, 0.0)
    return (
        layer_output,
        input_grad,
        done[0],
        vector_grad,
        done[1],
        vector_step[0],
        done[2],
        vector_step[1],
        done[3],
        vector_step[2],
    )


def solution(mesh):
    tokens = P(("dp", "ctx"), None)
    slabs = P(None, "ctx", "dp", None)
    lines = P(None, ("dp", "ctx"))
    return jax.shard_map(
        functools.partial(per_device, mesh.shape["dp"]),
        mesh=mesh,
        in_specs=(tokens, tokens, slabs, lines, slabs, lines, slabs, lines),
        out_specs=(tokens, tokens, slabs, lines, slabs, lines, slabs, lines, slabs, lines),
        check_vma=False,
    )
```

time: 1100 us -> 698 us (0.63)
  Pallas kernels: 831 us -> 687 us
  waiting for transfers between devices: 109 us -> 0.01 us
  blocking collectives: 86 us -> 0 us
  starting transfers between devices: 37.8 us -> 0.69 us
  local copies, waits for them, and re-layouts: 19.4 us -> 2.26 us
    pallas_call x21 -> x6, Pallas kernels: 820 us -> 675 us  [the longest x1 258 us: forward_first(): pl.pallas_call(kernel, out_shape=[shape((4, self.n_dp, self.span, LANES),...]
    ppermute x34 -> x0, waiting for transfers between devices: 109 us -> none  [the longest x24 92.4 us: trade(): result.append(lax.ppermute(arrays[r], ('dp', 'ctx'), pairs))]
    all_gather x1 -> x0, blocking collectives: 86 us -> none  [per_device(): lax.all_gather(vectors.astype(BF), ('dp', 'ctx'), axis=1, tiled=True)]
    ppermute x34 -> x0, starting transfers between devices: 34.1 us -> none  [the longest x24 17.2 us: trade(): result.append(lax.ppermute(arrays[r], ('dp', 'ctx'), pairs))]
  transfers between devices with their start and end apart: 38 -> 1, of which waited for: 18 -> 0; matrix products, arithmetic and copies ran while one was open for 2% -> 0% of each run, Pallas kernels for 67% -> 22%
where the time goes in v2:
time: 698 us; the launch traced here: 695 us
  Pallas kernels  687 us (98%)
    pallas_call x1, Pallas kernels, forward_first(): pl.pallas_call(kernel, out_shape=[shape((4, self.n_dp, self.span, LANES),...  258 us
    pallas_call x1, Pallas kernels, backward_first(): pl.pallas_call(kernel, out_shape=[shape((self.size, LANES), F32), shape((...  149 us
    pallas_call x1, Pallas kernels, scatter_first(): pl.pallas_call(kernel, out_shape=[shape((self.size, LANES), F32), shape((...  138 us
    pallas_call x1, Pallas kernels, middle(): pl.pallas_call(kernel, out_shape=[token, shape((rows, D), F32)] + kept *...  107 us
    pallas_call x1, Pallas kernels, weight_call(): pl.pallas_call(functools.partial(weight_kernel, plan.pieces), out_shape=s...  19 us
  transfers between devices with their start and end apart: 1, of which 0 were waited for; matrix products, arithmetic and copies ran while one was open for 0% of the time, Pallas kernels for 22%

profile of v2, /device:TPU:0, one launch (start us, length us, event | category | flops | bytes accessed | tf_op | source)
XLA Modules:
  0.0 695.0 jit_solution(2951069232277980889)
XLA Ops:
  0.6 0.6 pad_add_fusion.me
  1.2 3.3 prep.1
  4.5 257.6 %forward_first.1 = (bf16[4,8,3088,128]{3,2,1,0:T(8,128)(2,1)}, bf16[4,8,3088,128]{3,2,1,0:T(8,128)(2,1)}, bf16[256,1024]{1,0:T(8,128)(2,1)}, f32[12,1024]{1,0:T(...) custom-call(bf16[3088,128]{1,0:T(8,128)(2,1)} %get-tuple-element.73., ...), custom_call_target="tpu_custom_call" | custom-call | tf_op jit(solution)/shard_map/forward_first/pallas_call | solution.py:1094
  262.2 0.9 slice_convert_fusion
  263.1 0.7 reshape.26.vec
  263.8 107.3 %middle.1 = (bf16[256,1024]{1,0:T(8,128)(2,1)}, f32[256,1024]{1,0:T(8,128)}, bf16[256,1024]{1,0:T(8,128)(2,1)}, bf16[256,1024]{1,0:T(8,128)(2,1)}, bf16[256,1024...) custom-call(f32[256,1024]{1,0:T(8,128)} %get-tuple-element.75.x, ...), custom_call_target="tpu_custom_call" | custom-call | tf_op jit(solution)/shard_map/middle/pallas_call | solution.py:1426
  371.0 19.0 %weight_grads.1.grads = bf16[4,4,3072,128]{3,2,1,0:T(8,128)(2,1)} custom-call(s32[2]{0:T(128)} %pad_add_fusion.me, bf16[256,1024]{1,0:T(8,128)(2,1)} %get-tuple-element.78.refs_0_, bf16[256,1024]{1,0:T(8,128)(2,1)} %get-tuple-element.79.refs_1_, bf16[256,1024]{1,0:T(8,128)(2,1)} %get-tuple-element.80.refs_2_, ...), custom_call_target="tpu_custom_call" | custom-call | tf_op jit(solution)/shard_map/weight_grads/pallas_call | solution.py:546
  390.0 149.3 %backward_first.1 = (f32[3072,128]{1,0:T(8,128)}, f32[256,1024]{1,0:T(8,128)}, bf16[256,1024]{1,0:T(8,128)(2,1)}, bf16[16,256,256]{2,1,0:T(8,128)(2,1)}, bf16[25...) custom-call(bf16[4,4,3072,128]{3,2,1,0:T(8,128)(2,1)} %weight_grads., ...), custom_call_target="tpu_custom_call" | custom-call | tf_op jit(solution)/shard_map/backward_first/pallas_call | solution.py:1314
  539.4 1.3 convert_element_type.19
  540.7 0.7 collective-permute-start
  541.4 138.3 %scatter_first.1 = (f32[3072,128]{1,0:T(8,128)}, f32[8,128]{1,0:T(8,128)}) custom-call(bf16[256,1024]{1,0:T(8,128)(2,1)} %get-tuple-element.95.normed1.refs_0_, bf16[256,1024]{1,0:T(8,128)(2,1)} %get-tuple-element.98.attended.refs_1_, bf16[256,1024]{1,0:T(8,128)(2,1)} %get-tuple-element.100.normed2.refs_2_, ...), custom_call_target="tpu_custom_call" | custom-call | tf_op jit(solution)/shard_map/scatter_first/pallas_call | solution.py:1527
  679.7 0.8 slice_bitcast_fusion.1
  680.4 6.0 adam.2
  686.4 0.0 copy-start.1
  686.4 0.0 copy-start
  686.4 5.8 adam.3
  692.2 0.0 copy-done.1
  692.2 0.0 copy-done.2
  692.2 0.0 copy-done.3
  692.2 0.6 add_multiply_fusion
  692.9 0.0 collective-permute-done
  692.9 1.1 convert_element_type.20
  693.9 0.0 copy-done
  694.0 0.8 copy.33
  (5 shorter events, 0.0 us)
Async XLA Ops:
  540.7 152.2 %collective-permute-start = (bf16[256,1024]{1,0:T(8,128)(2,1)S(1)}, bf16[256,1024]{1,0:T(8,128)(2,1)S(1)}, u32[]{:S(2)}, u32[]{:S(2)}) collective-permute-start(bf16[256,1024]{1,0:T(8,128)(2,1)S(1)} %convert_element_type.19), channel_id=1, source_target_pairs={{0,0},{1,8},{2,4},{3,12},{4,2},{5,10},{6,6},{7,14},{8,1},{9,9},{10... | collective-permute-start | bytes 1572872 | tf_op jit(solution)/shard_map/ppermute | solution.py:1555
  686.4 5.8 copy-start.1
  686.4 5.8 copy-start.2
  686.4 5.8 copy-start.3
  686.4 7.5 %copy-start = (bf16[256,1024]{1,0:T(8,128)(2,1)S(1)}, bf16[256,1024]{1,0:T(8,128)(2,1)}, u32[]{:S(2)}) copy-start(bf16[256,1024]{1,0:T(8,128)(2,1)} %get-tuple-element.154) | copy-start | bytes 1572868

commit v3 on v2

--- a/solution.py
+++ b/solution.py
@@ -502,11 +502,12 @@
     return items
 
 
-def weight_part(items, own, other, out):
+def weight_part(items, own, other, out, arrive):
     normed1, attended, normed2, active, mixed, dhb, dub, dyb = zip(own, other)
     everything = slice(None)
 
     def both(pair, *at):
+        arrive(pair[0])
         return jnp.concatenate([ref[at] for ref in pair], axis=0)
 
     def panels(pair, group):
@@ -534,20 +535,65 @@
             out[p // step, d // 2, at : at + n, :] = res[:, i * LANES : (i + 1) * LANES]
 
 
-def weight_kernel(pieces, me, *refs):
-    for core in range(2):
-
-        @pl.when(me[0] % 2 == core)
-        def _(core=core):
-            weight_part(weight_items(pieces, core), refs[:8], refs[8:16], refs[16])
+LOAD_ORDER = (0, 4, 1, 5, 2, 6, 3, 7)
+
+
+class Loader:
+    def __init__(self, sources, targets, sems):
+        self.copies = [pltpu.make_async_copy(a, b, sems.at[i]) for i, (a, b) in enumerate(zip(sources, targets))]
+        self.targets, self.pending = targets, []
+        for i in LOAD_ORDER:
+            self.copies[i].start()
+            self.copies[i + 8].start()
+
+    def begin(self):
+        self.pending = list(range(8))
+
+    def arrive(self, ref):
+        for i in list(self.pending):
+            if self.targets[i] is ref:
+                self.finish((i,))
+
+    def finish(self, which=None):
+        for i in list(self.pending) if which is None else which:
+            self.copies[i].wait()
+            self.copies[i + 8].wait()
+            self.pending.remove(i)
+
+
+def weight_kernel(pieces, thirds, me, *refs):
+    held, (out, grads, sems, leave) = refs[17:33], (refs[16], *refs[33:])
+    loader = Loader(refs[:16], held, sems)
+    flushes = []
+    groups = grads.shape[2] // thirds
+    for group in range(groups):
+        for core in range(2):
+
+            @pl.when(me[0] % 2 == core)
+            def _(core=core):
+                if group == 0:
+                    loader.begin()
+                items = [item for item in weight_items(pieces, core) if item[0] // thirds == group]
+                weight_part(items, held[:8], held[8:], grads, loader.arrive)
+                loader.finish()
+
+        rows = pl.ds(group * thirds, thirds)
+        flushes.append(pltpu.make_async_copy(grads.at[:, :, rows], out.at[:, :, rows], leave.at[group]))
+        flushes[-1].start()
+    for copy in flushes:
+        copy.wait()
 
 
 def weight_call(plan, me, own, other):
+    dims = (4, plan.n_dp // 2, plan.size, LANES)
+    thirds = plan.size // 3
     return pl.pallas_call(
-        functools.partial(weight_kernel, plan.pieces),
-        out_shape=shape((4, plan.n_dp // 2, plan.size, LANES), BF),
-        in_specs=[SM] + [VM] * 16,
-        out_specs=VM,
+        functools.partial(weight_kernel, plan.pieces, thirds),
+        out_shape=shape(dims, BF),
+        in_specs=[SM] + [ANY] * 16,
+        out_specs=ANY,
+        scratch_shapes=[pltpu.VMEM(x.shape, BF) for x in (*own, *other)]
+        + [pltpu.VMEM(dims, BF), pltpu.SemaphoreType.DMA((16,)), pltpu.SemaphoreType.DMA((3,))],
         compiler_params=params_of(),
         name="weight_grads",
     )(me, *own, *other)
@@ -736,30 +782,39 @@
                 vec[at // per_row : at // per_row + 1, col : col + LANES] = lines[r : r + 1, :]
 
 
-def qkv_part(wire, normed, weight, vec, blocks, heads, copies):
-    for r in (2, 3, 1, 0):
-        at = wire.place ^ TURN[r]
-        cols = pl.ds(pl.multiple_of(at * WIDE, WIDE), WIDE)
-        for kind in range(3):
-            acc = nn(normed[...], side(weight, 2 * (kind * GROUP + at)))
+def share_normed(wire, normed, everyone):
+    mine = everyone.at[wire.place]
+    everyone[wire.place] = normed[...]
+    return wire.push(mine, mine, 2, 0), wire.push(mine, mine, 1, 0)
+
+
+def qkv_part(wire, shared, everyone, weight, vec, q, k, v):
+    far, near = shared
+    rows = everyone.shape[1]
+    cols = pl.ds(pl.multiple_of(wire.place * WIDE, WIDE), WIDE)
+
+    def block(g):
+        at = pl.ds(pl.multiple_of(g * rows, rows), rows)
+        for kind, target in enumerate((q, k, v)):
+            acc = nn(everyone[g], side(weight, 2 * (kind * GROUP + wire.place)))
             if kind != 1:
                 row = 2 if kind == 0 else 3
                 acc = acc + vec[row : row + 1, cols]
-            blocks[at, :, kind * WIDE : (kind + 1) * WIDE] = acc.astype(BF)
+            low = acc.astype(BF)
+            target[at, :] = (low.astype(F32) * 0.125).astype(BF) if kind == 0 else low
             yield
-        if r:
-            copies.append(wire.push(blocks.at[at], heads.at[wire.place], r, 0))
-        else:
-            heads[at] = blocks[at]
-
-
-def spread_heads(heads, q, k, v):
-    rows = heads.shape[1]
-    for g in range(GROUP):
-        at = slice(g * rows, (g + 1) * rows)
-        q[at, :] = heads[g, :, 0:WIDE]
-        k[at, :] = heads[g, :, WIDE : 2 * WIDE]
-        v[at, :] = heads[g, :, 2 * WIDE : 3 * WIDE]
+
+    yield from block(wire.place)
+    near.wait_recv()
+    yield from block(wire.place ^ TURN[1])
+    far.wait_recv()
+    other = everyone.at[wire.place ^ TURN[2]]
+    relay = wire.push(other, other, 1, 0)
+    yield from block(wire.place ^ TURN[2])
+    relay.wait_recv()
+    yield from block(wire.place ^ TURN[3])
+    for copy in (far, near, relay):
+        copy.wait_send()
 
 
 def attend_part(q, k, v, o, lse, send):
@@ -770,27 +825,26 @@
             cols = slice(h * HEAD, (h + 1) * HEAD)
             here = slice(i * rows, (i + 1) * rows)
             qi = q[here, cols]
-            near = jnp.where(seen, nt(qi, k[here, cols]) * 0.125, -1000000000.0)
+            near = jnp.where(seen, nt(qi, k[here, cols]), -1000000000.0)
             top = jnp.max(near, axis=1, keepdims=True)
             if i:
-                far = nt(qi, k[0 : i * rows, cols]) * 0.125
+                far = nt(qi, k[0 : i * rows, cols])
                 top = jnp.maximum(top, jnp.max(far, axis=1, keepdims=True))
                 far = jnp.exp(far - top)
             near = jnp.exp(near - top)
             total = jnp.sum(near, axis=1, keepdims=True)
             if i:
                 total = total + jnp.sum(far, axis=1, keepdims=True)
-            inv = 1.0 / total
-            res = nn((near * inv).astype(BF), v[here, cols])
+            res = nn(near.astype(BF), v[here, cols])
             if i:
-                res = res + nn((far * inv).astype(BF), v[0 : i * rows, cols])
-            o[i, :, cols] = res.astype(BF)
+                res = res + nn(far.astype(BF), v[0 : i * rows, cols])
+            o[i, :, cols] = (res * (1.0 / total)).astype(BF)
             lse[here, h : h + 1] = top + jnp.log(total)
             yield
         send(i)
 
 
-def ff_part(x, parts, vec, weights, wr_rows, sems, attended, hidden, normed, upper, active, out):
+def ff_part(x, parts, vec, weights, wr_rows, sems, attended, hidden, normed, upper, active, out, made):
     wo, we, wr = weights
     for g in range(GROUP):
         attended[:, g * WIDE : (g + 1) * WIDE] = parts[g]
@@ -811,8 +865,12 @@
         upper[n] = u
         act = (0.5 * u * (1.0 + jnp.tanh(gelu_c * (u + gelu_a * u * u * u)))).astype(BF)
         active[n] = act
-        out[...] += nn(act, wr_rows(n))
         yield
+        if n % GROUP == GROUP - 1:
+            quarter = jnp.concatenate([active[n - i] for i in reversed(range(GROUP))], axis=1)
+            out[...] += nn(quarter, wr_rows(n // GROUP))
+            made(n)
+            yield
 
 
 def ring_reader(upper, ring, sems):
@@ -834,7 +892,6 @@
     wo, we, wr = weights
     dyb[...] = dy[...].astype(BF)
     vec_grad[0:1, :] = jnp.sum(dy[...].astype(F32), axis=0, keepdims=True)
-    acc[...] = jnp.zeros_like(acc)
     if sems:
         wait_all(wr, sems[2])
         wait_all(we, sems[1])
@@ -849,8 +906,12 @@
         bias_grad[row : row + 1, col : col + WIDE] = jnp.sum(du, axis=0, keepdims=True)
         low = du.astype(BF)
         dub[n] = low
-        acc[...] += nt(low, side(we, 2 * n))
         yield
+        if n % GROUP == GROUP - 1:
+            quarter = jnp.concatenate([dub[n - i] for i in reversed(range(GROUP))], axis=1)
+            more = nt(quarter, side(we, 2 * (n - GROUP + 1), 2 * GROUP))
+            acc[...] = more if n < GROUP else acc[...] + more
+            yield
     back, gain, shift = norm_back(hidden[...], vec[5:6, :], acc[...])
     total = dy[...].astype(F32) + back
     vec_grad[1:2, :] = gain
@@ -881,26 +942,27 @@
         for h in range(WIDE // HEAD):
             cols = slice(h * HEAD, (h + 1) * HEAD)
             qi, doi, ls = q[here, cols], do[i, :, cols], lse[here, h : h + 1]
-            near = jnp.exp(jnp.where(seen, nt(qi, k[here, cols]) * 0.125, -1000000000.0) - ls)
+            near = jnp.exp(jnp.where(seen, nt(qi, k[here, cols]), -1000000000.0) - ls)
             dnear = nt(doi, v[here, cols])
             inner = jnp.sum(near * dnear, axis=1, keepdims=True)
             if i:
-                far = jnp.exp(nt(qi, k[past, cols]) * 0.125 - ls)
+                far = jnp.exp(nt(qi, k[past, cols]) - ls)
                 dfar = nt(doi, v[past, cols])
                 inner = inner + jnp.sum(far * dfar, axis=1, keepdims=True)
-            snear = (near * (dnear - inner) * 0.125).astype(BF)
+            snear = (near * (dnear - inner)).astype(BF)
             res = nn(snear, k[here, cols])
             dkn = tn(snear, qi)
             dvn = tn(near.astype(BF), doi)
             dk[here, cols] = dkn if last else dk[here, cols] + dkn
             dv[here, cols] = dvn if last else dv[here, cols] + dvn
             if i:
-                sfar = (far * (dfar - inner) * 0.125).astype(BF)
+                sfar = (far * (dfar - inner)).astype(BF)
                 res = res + nn(sfar, k[past, cols])
                 dkf = tn(sfar, qi)
                 dvf = tn(far.astype(BF), doi)
                 dk[past, cols] = dkf if last else dk[past, cols] + dkf
                 dv[past, cols] = dvf if last else dv[past, cols] + dvf
+            res = res * 0.125
             sums[0:1, cols] += jnp.sum(res, axis=0, keepdims=True)
             dm[i, :, cols] = res.astype(BF)
             yield
@@ -911,10 +973,12 @@
 
 
 def qkv_back_part(mixed, weight, acc):
-    for b in range(3 * GROUP):
-        kind, at = b // GROUP, b % GROUP
-        acc[...] += nt(mixed[at, :, kind * WIDE : (kind + 1) * WIDE], side(weight, 2 * b))
-        yield
+    for kind in range(3):
+        part = jnp.concatenate([mixed[g, :, kind * WIDE : (kind + 1) * WIDE] for g in range(GROUP)], axis=1)
+        more = nt(part, side(weight, 2 * GROUP * kind, 2 * GROUP))
+        acc[...] = acc[...] + more if kind else more
+        for _ in range(3):
+            yield
 
 
 class Mover:
@@ -951,15 +1015,15 @@
 class BitMover(Mover):
     def __init__(self, n_dp):
         super().__init__(n_dp)
-        self.gap, self.pace, self.pace_back = 5, (1.3, 4, 2), (1.5, 4, 2, 2)
+        self.gap, self.pace, self.pace_back = 8, (1.3, 4, 2), (1.5, 4, 2, 2)
         self.even = self.cut(((4, 4), (2, 2), (4, 4), (2, 2), (4, 4), (2, 2), (4, 4), (2, 2)))
-        self.skew = self.cut(((5, 3), (3, 1), (5, 2), (3, 2), (5, 3), (3, 1), (5, 2), (3, 2)))
+        self.skew = self.cut(((5, 3), (3, 2), (4, 3), (3, 1), (5, 3), (3, 2), (4, 3), (2, 2)))
 
     def cut(self, plan):
         unit, row, chunks = self.size // 48, 0, []
         for i, pair in enumerate(plan):
             for units, (a, b) in zip(pair, ((2, 4), (4, 2))):
-                chunks.append((row, units * unit, (i % 2 == 0, a, b), i // 2))
+                chunks.append((row, units * unit, (i % 2 == 0, a, b), i // 2 * 2))
                 row += units * unit
         return chunks
 
@@ -1045,10 +1109,21 @@
 
         def kernel(
             held0, held1, tokens,
-            whole0, whole1, value, vec, normed1, heads_out, lse, attended, hidden, normed2, upper, active, out,
-            swapped, heads, blocks, q, k, v, o, parts, raw, wa, wo, we, wr, local, sems, send, recv,
+            whole0, whole1, value, vec, normed1, heads_out, lse, attended, hidden, normed2, upper_out, active_out, out,
+            upper, active, swapped, everyone, q, k, v, o, parts, raw, wa, wo, we, wr, local, sems, send, recv,
         ):
             wire = Wire(send, recv)
+            leaving = []
+
+            def leave(src, dst):
+                leaving.append(pltpu.make_async_copy(src, dst, sems.at[5 + len(leaving)]))
+                leaving[-1].start()
+
+            def made(n):
+                if n % 4 == 3:
+                    for src, dst in ((upper, upper_out), (active, active_out)):
+                        leave(src.at[pl.ds(n - 3, 4)], dst.at[pl.ds(n - 3, 4)])
+
             wire.greet(FLIPS, swaps=True)
             done = [0, 0]
             comm = self.gather_jobs(wire, local, (held0, held1), (whole0, whole1), plans, done)
@@ -1066,30 +1141,30 @@
             unpack_vectors(raw, vec, self.n_dp, self.size)
             hat, _ = norm_parts(swapped[...].astype(F32))
             normed1[...] = (hat * vec[0:1, :] + vec[1:2, :]).astype(BF)
+            shared = share_normed(wire, normed1, everyone)
             wait_all(wa, sems.at[3])
             advance = paced(comm, pace[0])
-            copies = []
-            for _ in qkv_part(wire, normed1, wa, vec, blocks, heads, copies):
+            for _ in qkv_part(wire, shared, everyone, wa, vec, q, k, v):
                 advance()
             load_matrix(whole0, we, 2, pieces, sems.at[1])
             load_matrix(whole0, wr, 3, pieces, sems.at[2])
             take(comm, pace[1])
-            for copy in copies:
-                copy.wait()
-            spread_heads(heads, q, k, v)
-            heads_out[...] = heads[...]
+            for i, ref in enumerate((q, k, v)):
+                leave(ref, heads_out.at[i])
             send_o, finish = wire.post(o, parts)
             for _ in attend_part(q, k, v, o, lse, send_o):
                 advance()
             take(comm, pace[2])
             finish()
             for _ in ff_part(
-                swapped, parts, vec, (wo, we, wr), lambda n: rows_of(wr, slice(n * WIDE, (n + 1) * WIDE)), [sems.at[i] for i in range(3)],
-                attended, hidden, normed2, upper, active, out,
+                swapped, parts, vec, (wo, we, wr), lambda n: rows_of(wr, slice(n * D, (n + 1) * D)), [sems.at[i] for i in range(3)],
+                attended, hidden, normed2, upper, active, out, made,
             ):
                 advance()
             for _ in comm:
                 pass
+            for copy in leaving:
+                copy.wait()
 
         return pl.pallas_call(
             kernel,
@@ -1098,7 +1173,7 @@
                 shape((rows, D), BF),
                 shape((12, D), F32),
                 shape((rows, D), BF),
-                shape((GROUP, rows, 3 * WIDE), BF),
+                shape((3, span, WIDE), BF),
                 shape((span, LANES), F32),
                 shape((rows, D), BF),
                 shape((rows, D), F32),
@@ -1108,9 +1183,13 @@
                 shape((rows, D), F32),
             ],
             in_specs=[VM] * 3,
-            out_specs=[ANY] * 2 + [VM] * 11,
-            scratch_shapes=[pltpu.VMEM((rows, D), BF)]
-            + [pltpu.VMEM((GROUP, rows, 3 * WIDE), BF)] * 2
+            out_specs=[ANY] * 2 + [VM] * 3 + [ANY] + [VM] * 4 + [ANY] * 2 + [VM],
+            scratch_shapes=[
+                pltpu.VMEM((CHUNKS, rows, WIDE), F32),
+                pltpu.VMEM((CHUNKS, rows, WIDE), BF),
+                pltpu.VMEM((rows, D), BF),
+            ]
+            + [pltpu.VMEM((GROUP, rows, D), BF)]
             + [pltpu.VMEM((span, WIDE), BF)] * 3
             + [pltpu.VMEM((GROUP, rows, WIDE), BF)] * 2
             + [
@@ -1120,7 +1199,7 @@
                 pltpu.VMEM((FF // LANES, D, LANES), BF),
                 pltpu.VMEM((D // LANES, FF, LANES), BF),
                 pltpu.SemaphoreType.DMA((2 * count,)),
-                pltpu.SemaphoreType.DMA((5,)),
+                pltpu.SemaphoreType.DMA((16,)),
                 pltpu.SemaphoreType.DMA((slots,)),
                 pltpu.SemaphoreType.DMA((slots,)),
             ],
@@ -1251,21 +1330,18 @@
 
         def kernel(
             grads, x, normed1, heads, lse, attended, hidden, normed2, upper, active, dy, vec, whole,
-            owned, dx, dyb, dub, dhb, mixed, bias_grad, vec_grad, sums,
+            owned, dx, dyb, dub_out, dhb, mixed_out, bias_grad, vec_grad, sums,
             o_normed1, o_attended, o_normed2, o_active, o_mixed, o_dhb, o_dub, o_dyb,
             *scratch,
         ):
             bufs = scratch[:scratch_count]
-            q, k, v, do, blocks, dk, dv, dm, acc, dh, ring, wo, we, wr, local, sems, send, recv = scratch[scratch_count:]
-            sems = [sems.at[i] for i in range(8)]
+            dub, mixed, q, k, v, do, blocks, dk, dv, dm, acc, dh, ring, wo, we, wr, local, sems, send, recv = scratch[scratch_count:]
+            sems = [sems.at[i] for i in range(10)]
             load_matrix(whole, wr, 3, pieces, sems[2], split=True)
             load_matrix(whole, we, 2, pieces, sems[1])
             load_matrix(whole, wo, 1, pieces, sems[0])
-            for g in range(GROUP):
-                for i, ref in enumerate((q, k, v)):
-                    pltpu.make_async_copy(
-                        heads.at[g, :, pl.ds(i * WIDE, WIDE)], ref.at[pl.ds(g * rows, rows)], sems[5]
-                    ).start()
+            for i, ref in enumerate((q, k, v)):
+                pltpu.make_async_copy(heads.at[i], ref, sems[5]).start()
             wire = Wire(send, recv)
             wire.greet(FLIPS)
             comm = drive(
@@ -1282,6 +1358,8 @@
             ):
                 advance()
             load_matrix(whole, wr, 0, pieces, sems[6])
+            leaving = [pltpu.make_async_copy(dub, dub_out, sems[8]), pltpu.make_async_copy(mixed, mixed_out, sems[9])]
+            leaving[0].start()
             core += [wire.push(a, b, CORE, 0) for a, b in ((dyb, o_dyb), (dub, o_dub), (dhb, o_dhb))]
             copies = wire.trade(blocks, do)
             take(comm, pace[2])
@@ -1292,10 +1370,10 @@
             send_m, finish = wire.post(dm, mixed)
             for _ in attend_back_part(q, k, v, do, lse, dm, dk, dv, sums, send_m):
                 advance()
-            acc[...] = jnp.zeros_like(acc)
             take(comm, pace[3])
             finish()
             core.append(wire.push(mixed, o_mixed, CORE, 0))
+            leaving[1].start()
             wait_all(wr.at[pl.ds(0, 3 * D // LANES)], sems[6])
             for _ in qkv_back_part(mixed, wr, acc):
                 advance()
@@ -1305,7 +1383,7 @@
             vec_grad[5:6, :] = shift
             for _ in comm:
                 pass
-            for copy in core:
+            for copy in core + leaving:
                 copy.wait()
 
         token = shape((rows, D), BF)
@@ -1326,8 +1404,9 @@
             ]
             + [token, token, token, wide, triple, token, wide, token],
             in_specs=[ANY, VM, ANY, ANY, VM, ANY, VM, ANY, ANY, ANY, VM, VM, ANY],
-            out_specs=[VM] * 9 + [ANY] * 8,
+            out_specs=[VM] * 3 + [ANY, VM, ANY] + [VM] * 3 + [ANY] * 8,
             scratch_shapes=self.scatter_scratch(plan, True)
+            + [pltpu.VMEM((CHUNKS, rows, WIDE), BF), pltpu.VMEM((GROUP, rows, 3 * WIDE), BF)]
             + [pltpu.VMEM((span, WIDE), BF)] * 3
             + [pltpu.VMEM((GROUP, rows, WIDE), BF)] * 2
             + [pltpu.VMEM((span, WIDE), F32)] * 2
@@ -1340,7 +1419,7 @@
                 pltpu.VMEM((FF // LANES, D, LANES), BF),
                 pltpu.VMEM((4 * D // LANES, D, LANES), BF),
                 pltpu.SemaphoreType.DMA((2 * count,)),
-                pltpu.SemaphoreType.DMA((8,)),
+                pltpu.SemaphoreType.DMA((10,)),
                 pltpu.SemaphoreType.DMA((slots,)),
                 pltpu.SemaphoreType.DMA((slots,)),
             ],
@@ -1356,40 +1435,44 @@
 
         def kernel(
             x, cotangent, vec, whole,
-            output, dx, normed1, attended, normed2, active, mixed, dhb, dub, dyb,
+            output, dx, normed1, attended, normed2, active_out, mixed_out, dhb, dub_out, dyb,
             o_normed1, o_attended, o_normed2, o_active, o_mixed, o_dhb, o_dub, o_dyb, bias_grad, vec_grad, sums,
-            dy, result, returned, heads, blocks, q, k, v, o, parts, do, lse, hidden, upper, acc, dh, dk, dv, wa, wo, we, wr,
+            active, mixed, dub, dy, result, returned, everyone, blocks, q, k, v, o, parts, do, lse, hidden, upper, acc, dh, dk, dv, wa, wo, we, wr,
             sems, send, recv,
         ):
-            sems = [sems.at[i] for i in range(4)]
+            sems = [sems.at[i] for i in range(7)]
+            leaving = []
+
+            def leave(src, dst):
+                leaving.append(pltpu.make_async_copy(src, dst, sems[4 + len(leaving)]))
+                leaving[-1].start()
+
             load_matrix(whole, wa, 0, pieces, sems[3])
-            load_matrix(whole, wo, 1, pieces, sems[0])
             wire = Wire(send, recv)
             hat, _ = norm_parts(x[...])
             normed1[...] = (hat * vec[0:1, :] + vec[1:2, :]).astype(BF)
             wire.greet(FLIPS, swaps=True)
+            shared = share_normed(wire, normed1, everyone)
+            core = [wire.push(normed1, o_normed1, CORE, 0)]
+            load_matrix(whole, wo, 1, pieces, sems[0])
             wait_all(wa, sems[3])
-            copies = []
-            for _ in qkv_part(wire, normed1, wa, vec, blocks, heads, copies):
+            for _ in qkv_part(wire, shared, everyone, wa, vec, q, k, v):
                 pass
             load_matrix(whole, we, 2, pieces, sems[1])
             load_matrix(whole, wr, 3, pieces, sems[2], split=True)
-            core = [wire.push(normed1, o_normed1, CORE, 0)]
-            for copy in copies:
-                copy.wait()
             swap_in = wire.swap(cotangent, dy)
-            spread_heads(heads, q, k, v)
             send_o, finish = wire.post(o, parts)
             for _ in attend_part(q, k, v, o, lse, send_o):
                 pass
             finish()
             for _ in ff_part(
-                x, parts, vec, (wo, we, wr), lambda n: side_rows(wr, n // GROUP, slice(n % GROUP * WIDE, (n % GROUP + 1) * WIDE)),
-                sems, attended, hidden, normed2, upper, active, dx,
+                x, parts, vec, (wo, we, wr), lambda n: side_rows(wr, n, slice(0, D)),
+                sems, attended, hidden, normed2, upper, active, dx, lambda n: None,
             ):
                 pass
             core += [wire.push(a, b, CORE, 0) for a, b in (
                 (attended, o_attended), (normed2, o_normed2), (active, o_active))]
+            leave(active, active_out)
             result[...] = dx[...].astype(BF)
             swap_out = wire.swap(result, returned)
             swap_in()
@@ -1398,6 +1481,7 @@
                 dy, lambda n: upper[n], hidden, vec, (wo, we, wr), None, dyb, dub, dh, dhb, o, acc, bias_grad, vec_grad
             ):
                 pass
+            leave(dub, dub_out)
             copies = wire.trade(o, do)
             core += [wire.push(a, b, CORE, 0) for a, b in ((dyb, o_dyb), (dub, o_dub), (dhb, o_dhb))]
             for copy in copies:
@@ -1405,9 +1489,9 @@
             send_m, finish = wire.post(blocks, mixed)
             for _ in attend_back_part(q, k, v, do, lse, blocks, dk, dv, sums, send_m):
                 pass
-            acc[...] = jnp.zeros_like(acc)
             finish()
             core.append(wire.push(mixed, o_mixed, CORE, 0))
+            leave(mixed, mixed_out)
             for _ in qkv_back_part(mixed, wa, acc):
                 pass
             back, gain, shift = norm_back(x[...], vec[0:1, :], acc[...])
@@ -1416,7 +1500,7 @@
             vec_grad[5:6, :] = shift
             swap_out()
             output[...] = returned[...]
-            for copy in core:
+            for copy in core + leaving:
                 copy.wait()
 
         token = shape((rows, D), BF)
@@ -1428,9 +1512,14 @@
             out_shape=[token, shape((rows, D), F32)] + kept * 2
             + [shape((4, D), F32), shape((8, D), F32), shape((8, WIDE), F32)],
             in_specs=[VM, VM, VM, ANY],
-            out_specs=[VM] * 10 + [ANY] * 8 + [VM] * 3,
-            scratch_shapes=[pltpu.VMEM((rows, D), BF)] * 3
-            + [pltpu.VMEM((GROUP, rows, 3 * WIDE), BF)] * 2
+            out_specs=[VM] * 5 + [ANY, ANY, VM, ANY, VM] + [ANY] * 8 + [VM] * 3,
+            scratch_shapes=[
+                pltpu.VMEM((CHUNKS, rows, WIDE), BF),
+                pltpu.VMEM((GROUP, rows, 3 * WIDE), BF),
+                pltpu.VMEM((CHUNKS, rows, WIDE), BF),
+            ]
+            + [pltpu.VMEM((rows, D), BF)] * 3
+            + [pltpu.VMEM((GROUP, rows, D), BF), pltpu.VMEM((GROUP, rows, 3 * WIDE), BF)]
             + [pltpu.VMEM((span, WIDE), BF)] * 3
             + [pltpu.VMEM((GROUP, rows, WIDE), BF)] * 3
             + [
@@ -1445,7 +1534,7 @@
                 pltpu.VMEM((D // LANES, D, LANES), BF),
                 pltpu.VMEM((FF // LANES, D, LANES), BF),
                 pltpu.VMEM((4 * D // LANES, D, LANES), BF),
-                pltpu.SemaphoreType.DMA((4,)),
+                pltpu.SemaphoreType.DMA((7,)),
                 pltpu.SemaphoreType.DMA((slots,)),
                 pltpu.SemaphoreType.DMA((slots,)),
             ],
@@ -1460,10 +1549,12 @@
         scratch_count = 3 * count
 
         def kernel(*refs):
-            own, other, vectors, (owned, vec_owned) = refs[:8], refs[8:16], (refs[16:19], refs[19:22]), refs[22:24]
+            vectors, (owned, vec_owned) = (refs[16:19], refs[19:22]), refs[22:24]
             scratch = refs[24:]
-            bufs = scratch[:scratch_count]
-            grads, lines, got, small, from_b, from_a, from_z, send, recv = scratch[scratch_count:]
+            bufs, scratch = scratch[:scratch_count], scratch[scratch_count:]
+            held, scratch = scratch[:16], scratch[16:]
+            loader = Loader(refs[:16], held, scratch[0])
+            grads, lines, got, small, from_b, from_a, from_z, send, recv = scratch[1:]
             wire = Wire(send, recv)
             wire.greet([flip for flip in FLIPS if flip[0] != 3])
             mine = pl.ds(pl.multiple_of(wire.place * WIDE, WIDE), WIDE)
@@ -1483,7 +1574,10 @@
 
                     @pl.when(wire.d % 2 == core)
                     def _(items=items):
-                        weight_part(items, own, other, grads)
+                        if group == 0:
+                            loader.begin()
+                        weight_part(items, held[:8], held[8:], grads, loader.arrive)
+                        loader.finish()
 
             def put(at, block, value):
                 vec_owned[pl.ds(at, block), :] = value
@@ -1527,10 +1621,12 @@
         return pl.pallas_call(
             kernel,
             out_shape=[shape((self.size, LANES), F32), shape((8, LANES), F32)],
-            in_specs=[VM] * 22,
+            in_specs=[ANY] * 16 + [VM] * 6,
             out_specs=[VM] * 2,
             scratch_shapes=self.scatter_scratch(plan, False)
+            + [pltpu.VMEM(x.shape, BF) for x in (*own, *other)]
             + [
+                pltpu.SemaphoreType.DMA((16,)),
                 pltpu.VMEM((4, self.n_dp // 2, self.size, LANES), BF),
                 pltpu.VMEM((2, 12, D), F32),
                 pltpu.VMEM((2, 12, D), F32),

time: 698 us -> 670 us (0.960)
  Pallas kernels: 687 us -> 653 us
    pallas_call x1, Pallas kernels: 258 us -> 246 us  [forward_first(): pl.pallas_call(kernel, out_shape=[shape((4, self.n_dp, self.span, LANES),...]
    pallas_call x1, Pallas kernels: 138 us -> 128 us  [scatter_first(): pl.pallas_call(kernel, out_shape=[shape((self.size, LANES), F32), shape((...]
  transfers between devices with their start and end apart: 1 -> 1, of which waited for: 0 -> 0; matrix products, arithmetic and copies ran while one was open for 0% -> 0% of each run, Pallas kernels for 22% -> 21%
where the time goes in v3:
time: 670 us; the launch traced here: 661 us
  Pallas kernels  653 us (97%)
    pallas_call x1, Pallas kernels, forward_first(): pl.pallas_call(kernel, out_shape=[shape((4, self.n_dp, self.span, LANES),...  246 us
    pallas_call x1, Pallas kernels, backward_first(): pl.pallas_call(kernel, out_shape=[shape((self.size, LANES), F32), shape((...  145 us
    pallas_call x1, Pallas kernels, scatter_first(): pl.pallas_call(kernel, out_shape=[shape((self.size, LANES), F32), shape((...  128 us
    pallas_call x1, Pallas kernels, middle(): pl.pallas_call(kernel, out_shape=[token, shape((rows, D), F32)] + kept *...  104 us
    pallas_call x1, Pallas kernels, weight_call(): pl.pallas_call(functools.partial(weight_kernel, plan.pieces, thirds), out...  14.1 us
  transfers between devices with their start and end apart: 1, of which 0 were waited for; matrix products, arithmetic and copies ran while one was open for 0% of the time, Pallas kernels for 21%

profile of v3, /device:TPU:0, one launch (start us, length us, event | category | flops | bytes accessed | tf_op | source)
XLA Modules:
  0.0 661.3 jit_solution(7536018617389740215)
XLA Ops:
  0.6 0.6 pad_add_fusion.me
  1.2 3.3 prep.1
  4.5 246.3 %forward_first.1 = (bf16[4,8,3088,128]{3,2,1,0:T(8,128)(2,1)}, bf16[4,8,3088,128]{3,2,1,0:T(8,128)(2,1)}, bf16[256,1024]{1,0:T(8,128)(2,1)}, f32[12,1024]{1,0:T(...) custom-call(bf16[3088,128]{1,0:T(8,128)(2,1)} %get-tuple-element.73., ...), custom_call_target="tpu_custom_call" | custom-call | tf_op jit(solution)/shard_map/forward_first/pallas_call | solution.py:1169
  250.9 0.9 slice_convert_fusion
  251.8 0.7 reshape.26.vec
  252.4 103.9 %middle.1 = (bf16[256,1024]{1,0:T(8,128)(2,1)}, f32[256,1024]{1,0:T(8,128)}, bf16[256,1024]{1,0:T(8,128)(2,1)}, bf16[256,1024]{1,0:T(8,128)(2,1)}, bf16[256,1024...) custom-call(f32[256,1024]{1,0:T(8,128)} %get-tuple-element.75.x, ...), custom_call_target="tpu_custom_call" | custom-call | tf_op jit(solution)/shard_map/middle/pallas_call | solution.py:1510
  356.4 14.1 %weight_grads.1.grads = bf16[4,4,3072,128]{3,2,1,0:T(8,128)(2,1)} custom-call(s32[2]{0:T(128)} %pad_add_fusion.me, bf16[256,1024]{1,0:T(8,128)(2,1)} %get-tuple-element.78.refs_0_, bf16[256,1024]{1,0:T(8,128)(2,1)} %get-tuple-element.79.refs_1_, bf16[256,1024]{1,0:T(8,128)(2,1)} %get-tuple-element.80.refs_2_, ...), custom_call_target="tpu_custom_call" | custom-call | tf_op jit(solution)/shard_map/weight_grads/pallas_call | solution.py:590
  370.5 145.0 %backward_first.1 = (f32[3072,128]{1,0:T(8,128)}, f32[256,1024]{1,0:T(8,128)}, bf16[256,1024]{1,0:T(8,128)(2,1)}, bf16[16,256,256]{2,1,0:T(8,128)(2,1)}, bf16[25...) custom-call(bf16[4,4,3072,128]{3,2,1,0:T(8,128)(2,1)} %weight_grads., ...), custom_call_target="tpu_custom_call" | custom-call | tf_op jit(solution)/shard_map/backward_first/pallas_call | solution.py:1392
  515.4 1.3 convert_element_type.19
  516.7 0.7 collective-permute-start
  517.4 128.4 %scatter_first.1 = (f32[3072,128]{1,0:T(8,128)}, f32[8,128]{1,0:T(8,128)}) custom-call(bf16[256,1024]{1,0:T(8,128)(2,1)} %get-tuple-element.95.normed1.refs_0_, bf16[256,1024]{1,0:T(8,128)(2,1)} %get-tuple-element.98.attended.refs_1_, bf16[256,1024]{1,0:T(8,128)(2,1)} %get-tuple-element.100.normed2.refs_2_, ...), custom_call_target="tpu_custom_call" | custom-call | tf_op jit(solution)/shard_map/scatter_first/pallas_call | solution.py:1621
  645.8 0.8 slice_bitcast_fusion.1
  646.6 6.0 adam.2
  652.5 0.0 copy-start.1
  652.6 0.0 copy-start
  652.6 5.8 adam.3
  658.4 0.0 copy-done.1
  658.4 0.0 copy-done.2
  658.4 0.0 copy-done.3
  658.4 0.6 add_multiply_fusion
  659.0 0.0 collective-permute-done
  659.0 1.1 convert_element_type.20
  660.1 0.0 copy-done
  660.1 0.8 copy.33
  (5 shorter events, 0.0 us)
Async XLA Ops:
  516.7 142.3 %collective-permute-start = (bf16[256,1024]{1,0:T(8,128)(2,1)S(1)}, bf16[256,1024]{1,0:T(8,128)(2,1)S(1)}, u32[]{:S(2)}, u32[]{:S(2)}) collective-permute-start(bf16[256,1024]{1,0:T(8,128)(2,1)S(1)} %convert_element_type.19), channel_id=1, source_target_pairs={{0,0},{1,8},{2,4},{3,12},{4,2},{5,10},{6,6},{7,14},{8,1},{9,9},{10... | collective-permute-start | bytes 1572872 | tf_op jit(solution)/shard_map/ppermute | solution.py:1651
  652.5 5.8 copy-start.1
  652.5 5.8 copy-start.2
  652.6 5.8 copy-start.3
  652.6 7.5 %copy-start = (bf16[256,1024]{1,0:T(8,128)(2,1)S(1)}, bf16[256,1024]{1,0:T(8,128)(2,1)}, u32[]{:S(2)}) copy-start(bf16[256,1024]{1,0:T(8,128)(2,1)} %get-tuple-element.154) | copy-start | bytes 1572868

commit v4 on v3

--- a/solution.py
+++ b/solution.py
@@ -608,35 +608,35 @@
     return moment_next, square_next, update
 
 
-def adam_kernel(plan, me, owned, master, moment, square, *refs):
-    grad, moment_next, square_next, update = refs[-4:]
-    for d, held in enumerate(plan.pieces):
-
-        @pl.when(me[0] == d)
-        def _(held=held):
-            for mat, k0, k1, base in held:
-                size, step = k1 - k0, PANELS[mat]
-                for j in range(step):
-                    grad[0, 0, pl.ds(base + j, size, stride=step), :] = owned[pl.ds(base + j * size, size), :]
+def adam_kernel(plan, me, *refs):
+    owned, (master, moment, square, grad, moment_next, square_next, update) = refs[:LAYERS], refs[LAYERS:]
+    for layer in range(LAYERS):
+        for d, held in enumerate(plan.pieces):
+
+            @pl.when((pl.program_id(0) == layer) & (me[0] == d))
+            def _(layer=layer, held=held):
+                for mat, k0, k1, base in held:
+                    size, step = k1 - k0, PANELS[mat]
+                    for j in range(step):
+                        rows = owned[layer][pl.ds(base + j * size, size), :]
+                        grad[0, 0, pl.ds(base + j, size, stride=step), :] = rows
 
     new = adam_parts(grad[0, 0], moment[0, 0], square[0, 0], master[0, 0], decay)
     moment_next[0, 0], square_next[0, 0], update[0, 0] = new
 
 
-def adam_call(plan, me, layer, owned, master, moment, square, before):
-    block = pl.BlockSpec((1, 1) + master.shape[2:], lambda i: (layer, 0, 0, 0))
-    whole = pl.BlockSpec(owned.shape, lambda i: (0, 0))
-    first = 5
+def adam_call(plan, me, owned, master, moment, square):
+    block = pl.BlockSpec((1, 1) + master.shape[2:], lambda layer: (layer, 0, 0, 0))
+    whole = pl.BlockSpec(owned[0].shape, lambda layer: (0, 0))
     return pl.pallas_call(
         functools.partial(adam_kernel, plan),
-        grid=(1,),
+        grid=(LAYERS,),
         out_shape=[shape(master.shape, F32)] * 4,
-        in_specs=[SM, whole] + [block] * 3 + [ANY] * len(before),
+        in_specs=[SM] + [whole] * LAYERS + [block] * 3,
         out_specs=[block] * 4,
-        input_output_aliases={first + i: i for i in range(len(before))},
         compiler_params=params_of(),
         name="adam",
-    )(me, owned, master, moment, square, *before)
+    )(me, *owned, master, moment, square)
 
 
 class Wire:
@@ -1015,7 +1015,7 @@
 class BitMover(Mover):
     def __init__(self, n_dp):
         super().__init__(n_dp)
-        self.gap, self.pace, self.pace_back = 8, (1.3, 4, 2), (1.5, 4, 2, 2)
+        self.gap, self.pace, self.pace_back = 8, (1.3, 4, 2), (1.0, 4, 2, 2, 2.0)
         self.even = self.cut(((4, 4), (2, 2), (4, 4), (2, 2), (4, 4), (2, 2), (4, 4), (2, 2)))
         self.skew = self.cut(((5, 3), (3, 2), (4, 3), (3, 1), (5, 3), (3, 2), (4, 3), (2, 2)))
 
@@ -1367,6 +1367,7 @@
                 wait_all(ref, sems[5])
             for copy in copies:
                 copy.wait()
+            advance = paced(comm, pace[4])
             send_m, finish = wire.post(dm, mixed)
             for _ in attend_back_part(q, k, v, do, lse, dm, dk, dv, sums, send_m):
                 advance()
@@ -1739,9 +1740,7 @@
         vec_owned = [plan.scatter_vectors(line) for line in lines]
     input_grad = swap(grad.astype(BF), n_dp).astype(F32)
 
-    done = []
-    for layer in reversed(range(LAYERS)):
-        done = adam_call(plan, me, layer, owned[layer], params, param_moment, param_square, done)
+    done = adam_call(plan, me, owned, params, param_moment, param_square)
     vector_grad = jnp.stack(vec_owned)
     vector_step = adam_parts(vector_grad, vector_moment, vector_square, vectors, 0.0)
     return (

time: 670 us -> 660 us (0.985)
  Pallas kernels: 653 us -> 643 us
where the time goes in v4:
time: 660 us; the launch traced here: 651 us
  Pallas kernels  643 us (97%)
    pallas_call x1, Pallas kernels, forward_first(): pl.pallas_call(kernel, out_shape=[shape((4, self.n_dp, self.span, LANES),...  246 us
    pallas_call x1, Pallas kernels, backward_first(): pl.pallas_call(kernel, out_shape=[shape((self.size, LANES), F32), shape((...  141 us
    pallas_call x1, Pallas kernels, scatter_first(): pl.pallas_call(kernel, out_shape=[shape((self.size, LANES), F32), shape((...  128 us
    pallas_call x1, Pallas kernels, middle(): pl.pallas_call(kernel, out_shape=[token, shape((rows, D), F32)] + kept *...  101 us
    pallas_call x1, Pallas kernels, weight_call(): pl.pallas_call(functools.partial(weight_kernel, plan.pieces, thirds), out...  14.3 us
  transfers between devices with their start and end apart: 1, of which 0 were waited for; matrix products, arithmetic and copies ran while one was open for 0% of the time, Pallas kernels for 21%

profile of v4, /device:TPU:0, one launch (start us, length us, event | category | flops | bytes accessed | tf_op | source)
XLA Modules:
  0.0 651.2 jit_solution(7134774376325999400)
XLA Ops:
  0.6 0.6 pad_add_fusion.me
  1.2 3.3 prep.1
  4.5 246.3 %forward_first.1 = (bf16[4,8,3088,128]{3,2,1,0:T(8,128)(2,1)}, bf16[4,8,3088,128]{3,2,1,0:T(8,128)(2,1)}, bf16[256,1024]{1,0:T(8,128)(2,1)}, f32[12,1024]{1,0:T(...) custom-call(bf16[3088,128]{1,0:T(8,128)(2,1)} %get-tuple-element.69., ...), custom_call_target="tpu_custom_call" | custom-call | tf_op jit(solution)/shard_map/forward_first/pallas_call | solution.py:1169
  250.9 0.9 slice_convert_fusion
  251.8 0.7 reshape.26.vec
  252.5 101.3 %middle.1 = (bf16[256,1024]{1,0:T(8,128)(2,1)}, f32[256,1024]{1,0:T(8,128)}, bf16[256,1024]{1,0:T(8,128)(2,1)}, bf16[256,1024]{1,0:T(8,128)(2,1)}, bf16[256,1024...) custom-call(f32[256,1024]{1,0:T(8,128)} %get-tuple-element.71.x, ...), custom_call_target="tpu_custom_call" | custom-call | tf_op jit(solution)/shard_map/middle/pallas_call | solution.py:1511
  353.8 14.3 %weight_grads.1.grads = bf16[4,4,3072,128]{3,2,1,0:T(8,128)(2,1)} custom-call(s32[2]{0:T(128)} %pad_add_fusion.me, bf16[256,1024]{1,0:T(8,128)(2,1)} %get-tuple-element.74.refs_0_, bf16[256,1024]{1,0:T(8,128)(2,1)} %get-tuple-element.75.refs_1_, bf16[256,1024]{1,0:T(8,128)(2,1)} %get-tuple-element.76.refs_2_, ...), custom_call_target="tpu_custom_call" | custom-call | tf_op jit(solution)/shard_map/weight_grads/pallas_call | solution.py:590
  368.1 140.6 %backward_first.1 = (f32[3072,128]{1,0:T(8,128)}, f32[256,1024]{1,0:T(8,128)}, bf16[256,1024]{1,0:T(8,128)(2,1)}, bf16[16,256,256]{2,1,0:T(8,128)(2,1)}, bf16[25...) custom-call(bf16[4,4,3072,128]{3,2,1,0:T(8,128)(2,1)} %weight_grads., ...), custom_call_target="tpu_custom_call" | custom-call | tf_op jit(solution)/shard_map/backward_first/pallas_call | solution.py:1393
  508.7 1.3 convert_element_type.19
  510.0 0.7 collective-permute-start
  510.7 127.7 %scatter_first.1 = (f32[3072,128]{1,0:T(8,128)}, f32[8,128]{1,0:T(8,128)}) custom-call(bf16[256,1024]{1,0:T(8,128)(2,1)} %get-tuple-element.91.normed1.refs_0_, bf16[256,1024]{1,0:T(8,128)(2,1)} %get-tuple-element.94.attended.refs_1_, bf16[256,1024]{1,0:T(8,128)(2,1)} %get-tuple-element.96.normed2.refs_2_, ...), custom_call_target="tpu_custom_call" | custom-call | tf_op jit(solution)/shard_map/scatter_first/pallas_call | solution.py:1622
  638.4 0.8 slice_bitcast_fusion.1
  639.2 0.0 copy-start.1
  639.2 0.0 copy-start.2
  639.2 0.0 copy-start
  639.2 9.3 %adam.1 = (f32[2,1,3072,128]{3,2,1,0:T(8,128)}, f32[2,1,3072,128]{3,2,1,0:T(8,128)}, f32[2,1,3072,128]{3,2,1,0:T(8,128)}, f32[2,1,3072,128]{3,2,1,0:T(8,128)}) custom-call(s32[2]{0:T(128)} %pad_add_fusion.me, f32[3072,128]{1,0:T(8,128)} %get-tuple-element.121.refs_0_, f32[3072,128]{1,0:T(8,128)} %get-tuple-element.122.refs_1_, f32[2,1,3072,128]{3,2,1,0:T(8,128)} %refs_2_.1, ...), custom_call_target="tpu_custom_call" | custom-call | tf_op jit(solution)/shard_map/adam/pallas_call | solution.py:631
  648.5 0.0 copy-done.1
  648.5 0.0 copy-done.2
  648.5 0.0 copy-done.3
  648.5 0.6 add_multiply_fusion
  649.1 0.0 collective-permute-done
  649.1 1.1 convert_element_type.20
  650.2 0.0 copy-done
  650.2 0.8 copy.25
  (4 shorter events, 0.0 us)
Async XLA Ops:
  510.0 139.1 %collective-permute-start = (bf16[256,1024]{1,0:T(8,128)(2,1)S(1)}, bf16[256,1024]{1,0:T(8,128)(2,1)S(1)}, u32[]{:S(2)}, u32[]{:S(2)}) collective-permute-start(bf16[256,1024]{1,0:T(8,128)(2,1)S(1)} %convert_element_type.19), channel_id=1, source_target_pairs={{0,0},{1,8},{2,4},{3,12},{4,2},{5,10},{6,6},{7,14},{8,1},{9,9},{10... | collective-permute-start | bytes 1572872 | tf_op jit(solution)/shard_map/ppermute | solution.py:1652
  639.2 9.3 %copy-start.1 = (f32[2,384]{1,0:T(2,128)S(1)}, f32[2,384]{1,0:T(2,128)}, u32[]{:S(2)}) copy-start(f32[2,384]{1,0:T(2,128)} %lines.1) | copy-start | bytes 9220
  639.2 9.3 %copy-start.2 = (f32[2,384]{1,0:T(2,128)S(1)}, f32[2,384]{1,0:T(2,128)}, u32[]{:S(2)}) copy-start(f32[2,384]{1,0:T(2,128)} %param.15) | copy-start | bytes 9220
  639.2 9.4 %copy-start.3 = (f32[2,384]{1,0:T(2,128)S(1)}, f32[2,384]{1,0:T(2,128)}, u32[]{:S(2)}) copy-start(f32[2,384]{1,0:T(2,128)} %param.13) | copy-start | bytes 9220
  639.2 11.1 %copy-start = (bf16[256,1024]{1,0:T(8,128)(2,1)S(1)}, bf16[256,1024]{1,0:T(8,128)(2,1)}, u32[]{:S(2)}) copy-start(bf16[256,1024]{1,0:T(8,128)(2,1)} %get-tuple-element.146) | copy-start | bytes 1572868
